TPU v7x, 256 devices: a whole 4x4x8 slice. The times are simulated.
256 devices in a mesh: dp: 32 (over x_lo, z, core), fsdp: 8 (over y, x_hi).
Axes of the slice: x: 4 (x_hi: 2, x_lo: 2; x = x_hi * 2 + x_lo), y: 4, z: 8, core: 2. Of those that a mesh axis runs over, the one named last changes fastest.
Arguments:
- patches: bfloat16 [256, 8, 48, 1152], P(('dp', 'fsdp')), may hold values from -6 to 6
- counts: int32 [256, 8], P(('dp', 'fsdp')), may hold values from 1 to 48, as said below
- owners: int32 [256, 8], P(('dp', 'fsdp')), may hold values from 0 to 7, as said below
- captions: bfloat16 [256, 8, 1152], P(('dp', 'fsdp')), may hold values from -6 to 6
- norm_gain: float32 [1152], replicated, may hold values from 0.25 to 1.75
- key_probe: bfloat16 [1152, 16], replicated, may hold values from -12 to 12
- value_weight: bfloat16 [1152, 1152], P('fsdp'), may hold values from -0.1875 to 0.1875
- logit_scale: float32 [1], replicated, may hold values from 5 to 20
- logit_bias: float32 [1], replicated, may hold values from -4 to -1
Outputs:
- loss_part: float32 [32, 8], P('dp', 'fsdp')
- row_grad: bfloat16 [256, 8, 48, 1152], P(('dp', 'fsdp'))
- text_grad: bfloat16 [256, 8, 1152], P(('dp', 'fsdp'))
- value_grad: bfloat16 [32, 1152, 1152], P('dp', 'fsdp')
- probe_grad: bfloat16 [32, 1152, 16], P('dp', 'fsdp')
- gain_grad: bfloat16 [32, 1152], P('dp', 'fsdp')
Inputs may be any that keep to these rules, and one draw needn't show every extreme that they name: `counts`: each loader holds at least one image of exactly 48 rows. `owners`: each loader sends exactly 1 of its images to every device of its data rank.
All inputs are finite; a program needn't handle non-finite values.
Results may differ from a plain program's by a relative error of at most 0.02.
Values may be sent and summed in bfloat16 or wider, within the bound.
No kernel may reach another device: no remote copies, remote signals or barrier semaphores. Data moves between devices by JAX's collectives and lax.ppermute only.
A program may use at most 64 MiB of HBM per device.

v0:
```python
import math

import jax
import jax.numpy as jnp
from jax import lax
from jax.sharding import PartitionSpec as P

PAIR_IMAGES = 1


epsilon = 1e-06


def shifted(block, axis, distance):
    devices = range(lax.axis_size(axis))
    route = [((i - distance) % len(devices), i) for i in devices]
    return lax.ppermute(block, axis, route)


def pack_loader(loaded, sizes_in, targets):
    slot_count = targets.shape[0]
    position = jnp.arange(slot_count, dtype=jnp.int32)
    before = (targets[:, None] == targets[None, :]) & (position[None, :] < position[:, None])
    earlier = jnp.sum(before.astype(jnp.int32), axis=1)
    placed = targets * PAIR_IMAGES + earlier
    source = jnp.sum(jnp.where(placed[None, :] == position[:, None], position[None, :], 0), axis=1)
    return (jnp.take(loaded, source, axis=0), jnp.take(sizes_in, source, axis=0))


def encode(received, sizes_now, norm_gain, key_probe, value_weight):
    slot_count, patch_count, model_width = received.shape
    head_count = key_probe.shape[1]
    head_width = model_width // head_count
    flat_rows = received.reshape(slot_count * patch_count, model_width).astype(jnp.float32)
    row_mean = jnp.mean(flat_rows, axis=-1, keepdims=True)
    centered = flat_rows - row_mean
    inv_std = lax.rsqrt(jnp.mean(centered * centered, axis=-1, keepdims=True) + epsilon)
    normed = centered * inv_std
    scaled_in = (normed * norm_gain).astype(jnp.bfloat16)
    scores = jnp.dot(scaled_in, key_probe, preferred_element_type=jnp.float32).reshape(
        slot_count, patch_count, head_count
    ) / math.sqrt(head_width)
    valid_rows = jnp.arange(patch_count, dtype=jnp.int32)[None, :, None] < sizes_now[:, None, None]
    highest = jnp.max(jnp.where(valid_rows, scores, -jnp.inf), axis=1, keepdims=True)
    raised = jnp.where(valid_rows, jnp.exp(scores - highest), 0.0)
    weights_f = raised / jnp.sum(raised, axis=1, keepdims=True)
    weights_b = weights_f.astype(jnp.bfloat16)
    values = jnp.dot(scaled_in, value_weight, preferred_element_type=jnp.float32).astype(
        jnp.bfloat16
    )
    values = values.reshape(slot_count, patch_count, head_count, head_width)
    context = jnp.einsum(
        "sph,sphe->she", weights_b, values, preferred_element_type=jnp.float32
    ).reshape(slot_count, model_width)
    inv_norm = lax.rsqrt(jnp.sum(context * context, axis=-1, keepdims=True) + epsilon)
    unit_image = context * inv_norm
    return (normed, inv_std, scaled_in, weights_f, weights_b, values, unit_image, inv_norm)


def pair_terms(left_side, right_side, logit_scale, logit_bias, matched):
    logits = (
        logit_scale[0]
        * jnp.einsum("ad,bd->ab", left_side, right_side, preferred_element_type=jnp.float32)
        + logit_bias[0]
    )
    losses = jax.nn.softplus((1.0 - 2.0 * matched) * logits)
    coefficient = (logit_scale[0] * (jax.nn.sigmoid(logits) - matched)).astype(jnp.bfloat16)
    return (jnp.sum(losses), coefficient)


def pass_text(text_block):
    return shifted(text_block, "dp", 1)


def local(
    patches, counts, owners, captions, norm_gain, key_probe, value_weight, logit_scale, logit_bias
):
    sent, sent_sizes = pack_loader(patches[0], counts[0], owners[0])
    received, arrived = (
        lax.all_to_all(sent, "fsdp", split_axis=0, concat_axis=0, tiled=True),
        lax.all_to_all(
            sent_sizes.astype(jnp.bfloat16), "fsdp", split_axis=0, concat_axis=0, tiled=True
        ),
    )
    sizes_now = arrived.astype(jnp.int32)
    gathered = lax.all_gather(value_weight, "fsdp", axis=0, tiled=True)
    normed, inv_std, scaled_in, weights_f, weights_b, values, unit_image, inv_norm = encode(
        received, sizes_now, norm_gain, key_probe, gathered
    )
    slot_count, patch_count, head_count, head_width = values.shape
    model_width = head_count * head_width
    image_b = unit_image.astype(jnp.bfloat16)
    caption_f = captions[0].astype(jnp.float32)
    caption_inv = lax.rsqrt(jnp.sum(caption_f * caption_f, axis=-1, keepdims=True) + epsilon)
    caption_unit = caption_f * caption_inv
    caption_b = caption_unit.astype(jnp.bfloat16)
    cycle_size = lax.axis_size("dp")
    group_width = lax.axis_size("fsdp")
    group_rows = group_width * slot_count
    fsdp_index = lax.axis_index("fsdp")
    own_match = (
        jnp.arange(slot_count, dtype=jnp.int32)[:, None] + fsdp_index * slot_count
        == jnp.arange(group_rows, dtype=jnp.int32)[None, :]
    ).astype(jnp.float32)
    zero_rows = jnp.zeros((slot_count, model_width), jnp.float32)
    caption_group = lax.all_gather(caption_b, "fsdp", axis=0, tiled=True)

    def block_terms(turn_index, left_side, right_side, own):
        matched = jnp.where(turn_index == 0, own, 0.0)
        return pair_terms(left_side, right_side, logit_scale, logit_bias, matched)

    def transposed(coefficient, others):
        return lax.dot_general(
            coefficient, others, (((0,), (0,)), ((), ())), preferred_element_type=jnp.float32
        )

    def pass_grads(grad_carry):
        return shifted(grad_carry, "dp", 1)

    def carry_turn(turn_index, carried):
        text_block, grad_carry, d_image, total_loss = carried
        partial_value, coefficient = block_terms(turn_index, image_b, text_block, own_match)
        d_image = d_image + jnp.dot(coefficient, text_block, preferred_element_type=jnp.float32)
        grad_carry = grad_carry + transposed(coefficient, image_b)
        return (pass_text(text_block), pass_grads(grad_carry), d_image, total_loss + partial_value)

    zero_group = jnp.zeros((group_rows, model_width), jnp.float32)
    text_block, grad_carry, d_image, total_loss = lax.fori_loop(
        0,
        cycle_size - 1,
        carry_turn,
        (caption_group, zero_group, zero_rows, jnp.zeros((), jnp.float32)),
    )
    partial_value, coefficient = block_terms(cycle_size - 1, image_b, text_block, own_match)
    d_image = d_image + jnp.dot(coefficient, text_block, preferred_element_type=jnp.float32)
    group_grad = pass_grads(grad_carry + transposed(coefficient, image_b))
    d_caption = lax.psum_scatter(group_grad, "fsdp", scatter_dimension=0, tiled=True)
    total_loss = total_loss + partial_value
    loss_part = (total_loss / (cycle_size * group_rows)).reshape(1, 1)
    text_grad = (
        (d_caption - caption_unit * jnp.sum(d_caption * caption_unit, axis=-1, keepdims=True))
        * caption_inv
    ).astype(jnp.bfloat16)
    d_embed = (
        d_image - unit_image * jnp.sum(d_image * unit_image, axis=-1, keepdims=True)
    ) * inv_norm
    d_context = d_embed.astype(jnp.bfloat16).reshape(slot_count, head_count, head_width)
    d_weights = jnp.einsum("she,sphe->sph", d_context, values, preferred_element_type=jnp.float32)
    d_values = (
        weights_b.astype(jnp.float32)[..., None] * d_context.astype(jnp.float32)[:, None]
    ).astype(jnp.bfloat16)
    d_values = d_values.reshape(slot_count * patch_count, model_width)
    d_scores = (
        weights_f
        * (d_weights - jnp.sum(weights_f * d_weights, axis=1, keepdims=True))
        / math.sqrt(head_width)
    ).astype(jnp.bfloat16)
    d_scores = d_scores.reshape(slot_count * patch_count, head_count)
    probe_term = lax.dot_general(
        scaled_in, d_scores, (((0,), (0,)), ((), ())), preferred_element_type=jnp.float32
    )
    value_term = lax.dot_general(
        scaled_in, d_values, (((0,), (0,)), ((), ())), preferred_element_type=jnp.float32
    )
    d_scaled = jnp.einsum(
        "re,de->rd", d_values, gathered, preferred_element_type=jnp.float32
    ) + jnp.einsum("rh,dh->rd", d_scores, key_probe, preferred_element_type=jnp.float32)
    gain_term = jnp.sum(d_scaled * normed, axis=0)
    value_sum, probe_sum, gain_sum = (
        lax.psum_scatter(
            value_term.astype(jnp.bfloat16).astype(jnp.float32).astype(jnp.bfloat16),
            "fsdp",
            scatter_dimension=0,
            tiled=True,
        ).astype(jnp.float32),
        lax.psum_scatter(
            probe_term.astype(jnp.bfloat16).astype(jnp.float32).astype(jnp.bfloat16),
            "fsdp",
            scatter_dimension=0,
            tiled=True,
        ).astype(jnp.float32),
        lax.psum_scatter(
            gain_term.astype(jnp.bfloat16).astype(jnp.float32).astype(jnp.bfloat16),
            "fsdp",
            scatter_dimension=0,
            tiled=True,
        ).astype(jnp.float32),
    )
    grad_in = d_scaled * norm_gain
    row_grad = inv_std * (
        grad_in
        - jnp.mean(grad_in, axis=-1, keepdims=True)
        - normed * jnp.mean(grad_in * normed, axis=-1, keepdims=True)
    )
    row_grad = row_grad.astype(jnp.bfloat16).reshape(1, slot_count, patch_count, model_width)
    return (
        loss_part,
        row_grad,
        text_grad[None],
        value_sum.astype(jnp.bfloat16)[None],
        probe_sum.astype(jnp.bfloat16)[None],
        gain_sum.astype(jnp.bfloat16)[None],
    )


def solution(mesh):
    placed = (
        P(("dp", "fsdp"), None, None, None),
        P(("dp", "fsdp"), None),
        P(("dp", "fsdp"), None),
        P(("dp", "fsdp"), None, None),
        P(),
        P(),
        P("fsdp", None),
        P(),
        P(),
    )
    return jax.shard_map(
        local,
        mesh=mesh,
        in_specs=placed,
        out_specs=(
            P("dp", "fsdp"),
            P(("dp", "fsdp"), None, None, None),
            P(("dp", "fsdp"), None, None),
            P("dp", "fsdp", None),
            P("dp", "fsdp", None),
            P("dp", "fsdp"),
        ),
        check_vma=False,
    )
```

profile of v0, /device:TPU:2, one launch (start us, length us, event | category | flops | bytes accessed | tf_op | source)
XLA Modules:
  0.0 807.4 jit_solution(4536909643105671343)
XLA Ops:
  29.0 43.0 %all_gather.6 = bf16[64,1152]{1,0:T(8,128)(2,1)S(1)} all-gather(bf16[8,1152]{1,0:T(8,128)(2,1)S(1)} %fusion.35), channel_id=1, replica_groups=mesh['dp'=32,'fsdp'=8] {'fsdp'}, dimensions={0}, use_global_device_ids=true | all-gather | bytes 165888 | tf_op jit(solution)/shard_map/all_gather | solution.py:106
  95.8 449.9 %while.20 = (s32[]{:T(128)}, bf16[64,1152]{1,0:T(8,128)(2,1)S(1)}, f32[64,1152]{1,0:T(8,128)S(1)}, f32[8,1152]{1,0:T(8,128)}, f32[]{:T(128)}, /*index=5*/f32[1]{...) while((s32[]{:T(128)}, bf16[64,1152]{1,0:T(8,128)(2,1)S(1)}, ...), condition=%wide.region_10.11_spmd.clone, body=%wide.region_8.10_spmd.clone.sunk | while | flops 3648003 | bytes 3066185 | solution.py:128
  118.1 6.8 collective-permute-done
  132.6 6.8 collective-permute-done
  147.1 6.8 collective-permute-done
  161.6 6.8 collective-permute-done
  176.1 6.8 collective-permute-done
  190.6 6.8 collective-permute-done
  205.1 6.8 collective-permute-done
  219.6 6.8 collective-permute-done
  234.2 6.8 collective-permute-done
  248.7 6.8 collective-permute-done
  263.2 6.8 collective-permute-done
  277.7 6.8 collective-permute-done
  292.2 6.8 collective-permute-done
  306.7 6.8 collective-permute-done
  321.2 6.8 collective-permute-done
  335.8 6.8 collective-permute-done
  350.3 6.8 collective-permute-done
  379.3 6.8 collective-permute-done
  573.7 21.4 %all-reduce.1 = bf16[1152]{0:T(1024)(128)(2,1)} all-reduce(bf16[1152]{0:T(1024)(128)(2,1)} %get-tuple-element.200), channel_id=5, replica_groups=mesh['dp'=32,'fsdp'=8] {'fsdp'}, use_global_device_ids=true, to_apply=%region_21.22.clone | all-reduce | flops 1152 | bytes 4608
  599.3 24.3 %reduce-scatter.7.cloned.1.call-done = bf16[144,16]{1,0:T(8,128)(2,1)} async-done(((bf16[1152,16]{1,0:T(8,128)(2,1)}), bf16[144,16]{1,0:T(8,128)(2,1)}) %reduce-scatter.7.cloned.1.call-update) | async-done | bytes 4624
  625.0 90.1 %all-reduce.4.cloned.1.call-done = f32[64,1152]{1,0:T(8,128)} async-done(((f32[64,1152]{1,0:T(8,128)}), f32[64,1152]{1,0:T(8,128)}) %all-reduce.4.cloned.1.call-update) | async-done | bytes 294928
  717.5 82.2 %reduce-scatter.5.cloned.1.call-done = bf16[144,1152]{1,0:T(8,128)(2,1)} async-done(((bf16[1152,1152]{1,0:T(8,128)(2,1)}), bf16[144,1152]{1,0:T(8,128)(2,1)}) %reduce-scatter.5.cloned.1.call-update) | async-done | bytes 331792 | tf_op jit(solution)/shard_map/reduce_scatter | solution.py:170
  (347 shorter events, 382.6 us)
Async XLA Ops:
  7.2 75.6 %all-gather.2.cloned.1.call-start = ((), (), s32[]{:S(2)}) async-start(), calls=%async_computation.4 | async-start | bytes 2985984 | tf_op jit(solution)/shard_map/all_gather | solution.py:86
  11.6 13.6 %all-to-all-start = ((bf16[8,1,1]{2,1,0:T(2,128)(2,1)}), bf16[8,1,1]{2,1,0:T(2,128)(2,1)S(1)}, u32[]{:S(2)}, u32[]{:S(2)}) async-start(bf16[8,1,1]{2,1,0:T(2,128)(2,1)} %copy.24), calls=%async_computation | async-start | bytes 8192 | tf_op jit(solution)/shard_map/all_to_all | solution.py:81
  25.3 47.0 %all-to-all-start.1 = ((bf16[8,48,1152]{2,1,0:T(8,128)(2,1)}), bf16[8,48,1152]{2,1,0:T(8,128)(2,1)S(1)}, u32[]{:S(2)}, u32[]{:S(2)}) async-start(bf16[8,48,1152]{2,1,0:T(8,128)(2,1)} %broadcast_select_fusion), calls=%async_computation.1 | async-start | bytes 1769472 | tf_op jit(solution)/shard_map/all_to_all | solution.py:80
  28.8 594.7 %reduce-scatter.7.cloned.1.call-start = ((), (), s32[]{:S(2)}) async-start(), calls=%async_computation.6 | async-start | bytes 331776
  100.4 9.9 %collective-permute-start.1 = (f32[64,1152]{1,0:T(8,128)S(1)}, f32[64,1152]{1,0:T(8,128)S(1)}, u32[]{:S(2)}, u32[]{:S(2)}) collective-permute-start(f32[64,1152]{1,0:T(8,128)S(1)} %convolution_add_fusion.7), channel_id=1, source_target_pairs={{248,0},{0,8},{8,16},{16,24},{24,32},{32,40},{40,48},{48,56},{56,6... | collective-permute-start | bytes 884744 | tf_op jit(solution)/shard_map/while/body/eval_jaxpr/ppermute | solution.py:17
  115.0 9.9 %collective-permute-start.1 = (f32[64,1152]{1,0:T(8,128)S(1)}, f32[64,1152]{1,0:T(8,128)S(1)}, u32[]{:S(2)}, u32[]{:S(2)}) collective-permute-start(f32[64,1152]{1,0:T(8,128)S(1)} %convolution_add_fusion.7), channel_id=1, source_target_pairs={{248,0},{0,8},{8,16},{16,24},{24,32},{32,40},{40,48},{48,56},{56,6... | collective-permute-start | bytes 884744 | tf_op jit(solution)/shard_map/while/body/eval_jaxpr/ppermute | solution.py:17
  129.5 9.9 %collective-permute-start.1 = (f32[64,1152]{1,0:T(8,128)S(1)}, f32[64,1152]{1,0:T(8,128)S(1)}, u32[]{:S(2)}, u32[]{:S(2)}) collective-permute-start(f32[64,1152]{1,0:T(8,128)S(1)} %convolution_add_fusion.7), channel_id=1, source_target_pairs={{248,0},{0,8},{8,16},{16,24},{24,32},{32,40},{40,48},{48,56},{56,6... | collective-permute-start | bytes 884744 | tf_op jit(solution)/shard_map/while/body/eval_jaxpr/ppermute | solution.py:17
  144.0 9.9 %collective-permute-start.1 = (f32[64,1152]{1,0:T(8,128)S(1)}, f32[64,1152]{1,0:T(8,128)S(1)}, u32[]{:S(2)}, u32[]{:S(2)}) collective-permute-start(f32[64,1152]{1,0:T(8,128)S(1)} %convolution_add_fusion.7), channel_id=1, source_target_pairs={{248,0},{0,8},{8,16},{16,24},{24,32},{32,40},{40,48},{48,56},{56,6... | collective-permute-start | bytes 884744 | tf_op jit(solution)/shard_map/while/body/eval_jaxpr/ppermute | solution.py:17
  158.5 9.9 %collective-permute-start.1 = (f32[64,1152]{1,0:T(8,128)S(1)}, f32[64,1152]{1,0:T(8,128)S(1)}, u32[]{:S(2)}, u32[]{:S(2)}) collective-permute-start(f32[64,1152]{1,0:T(8,128)S(1)} %convolution_add_fusion.7), channel_id=1, source_target_pairs={{248,0},{0,8},{8,16},{16,24},{24,32},{32,40},{40,48},{48,56},{56,6... | collective-permute-start | bytes 884744 | tf_op jit(solution)/shard_map/while/body/eval_jaxpr/ppermute | solution.py:17
  173.0 9.9 %collective-permute-start.1 = (f32[64,1152]{1,0:T(8,128)S(1)}, f32[64,1152]{1,0:T(8,128)S(1)}, u32[]{:S(2)}, u32[]{:S(2)}) collective-permute-start(f32[64,1152]{1,0:T(8,128)S(1)} %convolution_add_fusion.7), channel_id=1, source_target_pairs={{248,0},{0,8},{8,16},{16,24},{24,32},{32,40},{40,48},{48,56},{56,6... | collective-permute-start | bytes 884744 | tf_op jit(solution)/shard_map/while/body/eval_jaxpr/ppermute | solution.py:17
  187.5 9.9 %collective-permute-start.1 = (f32[64,1152]{1,0:T(8,128)S(1)}, f32[64,1152]{1,0:T(8,128)S(1)}, u32[]{:S(2)}, u32[]{:S(2)}) collective-permute-start(f32[64,1152]{1,0:T(8,128)S(1)} %convolution_add_fusion.7), channel_id=1, source_target_pairs={{248,0},{0,8},{8,16},{16,24},{24,32},{32,40},{40,48},{48,56},{56,6... | collective-permute-start | bytes 884744 | tf_op jit(solution)/shard_map/while/body/eval_jaxpr/ppermute | solution.py:17
  202.0 9.9 %collective-permute-start.1 = (f32[64,1152]{1,0:T(8,128)S(1)}, f32[64,1152]{1,0:T(8,128)S(1)}, u32[]{:S(2)}, u32[]{:S(2)}) collective-permute-start(f32[64,1152]{1,0:T(8,128)S(1)} %convolution_add_fusion.7), channel_id=1, source_target_pairs={{248,0},{0,8},{8,16},{16,24},{24,32},{32,40},{40,48},{48,56},{56,6... | collective-permute-start | bytes 884744 | tf_op jit(solution)/shard_map/while/body/eval_jaxpr/ppermute | solution.py:17
  216.6 9.9 %collective-permute-start.1 = (f32[64,1152]{1,0:T(8,128)S(1)}, f32[64,1152]{1,0:T(8,128)S(1)}, u32[]{:S(2)}, u32[]{:S(2)}) collective-permute-start(f32[64,1152]{1,0:T(8,128)S(1)} %convolution_add_fusion.7), channel_id=1, source_target_pairs={{248,0},{0,8},{8,16},{16,24},{24,32},{32,40},{40,48},{48,56},{56,6... | collective-permute-start | bytes 884744 | tf_op jit(solution)/shard_map/while/body/eval_jaxpr/ppermute | solution.py:17
  231.1 9.9 %collective-permute-start.1 = (f32[64,1152]{1,0:T(8,128)S(1)}, f32[64,1152]{1,0:T(8,128)S(1)}, u32[]{:S(2)}, u32[]{:S(2)}) collective-permute-start(f32[64,1152]{1,0:T(8,128)S(1)} %convolution_add_fusion.7), channel_id=1, source_target_pairs={{248,0},{0,8},{8,16},{16,24},{24,32},{32,40},{40,48},{48,56},{56,6... | collective-permute-start | bytes 884744 | tf_op jit(solution)/shard_map/while/body/eval_jaxpr/ppermute | solution.py:17
  245.6 9.9 %collective-permute-start.1 = (f32[64,1152]{1,0:T(8,128)S(1)}, f32[64,1152]{1,0:T(8,128)S(1)}, u32[]{:S(2)}, u32[]{:S(2)}) collective-permute-start(f32[64,1152]{1,0:T(8,128)S(1)} %convolution_add_fusion.7), channel_id=1, source_target_pairs={{248,0},{0,8},{8,16},{16,24},{24,32},{32,40},{40,48},{48,56},{56,6... | collective-permute-start | bytes 884744 | tf_op jit(solution)/shard_map/while/body/eval_jaxpr/ppermute | solution.py:17
  260.1 9.9 %collective-permute-start.1 = (f32[64,1152]{1,0:T(8,128)S(1)}, f32[64,1152]{1,0:T(8,128)S(1)}, u32[]{:S(2)}, u32[]{:S(2)}) collective-permute-start(f32[64,1152]{1,0:T(8,128)S(1)} %convolution_add_fusion.7), channel_id=1, source_target_pairs={{248,0},{0,8},{8,16},{16,24},{24,32},{32,40},{40,48},{48,56},{56,6... | collective-permute-start | bytes 884744 | tf_op jit(solution)/shard_map/while/body/eval_jaxpr/ppermute | solution.py:17
  274.6 9.9 %collective-permute-start.1 = (f32[64,1152]{1,0:T(8,128)S(1)}, f32[64,1152]{1,0:T(8,128)S(1)}, u32[]{:S(2)}, u32[]{:S(2)}) collective-permute-start(f32[64,1152]{1,0:T(8,128)S(1)} %convolution_add_fusion.7), channel_id=1, source_target_pairs={{248,0},{0,8},{8,16},{16,24},{24,32},{32,40},{40,48},{48,56},{56,6... | collective-permute-start | bytes 884744 | tf_op jit(solution)/shard_map/while/body/eval_jaxpr/ppermute | solution.py:17
  289.1 9.9 %collective-permute-start.1 = (f32[64,1152]{1,0:T(8,128)S(1)}, f32[64,1152]{1,0:T(8,128)S(1)}, u32[]{:S(2)}, u32[]{:S(2)}) collective-permute-start(f32[64,1152]{1,0:T(8,128)S(1)} %convolution_add_fusion.7), channel_id=1, source_target_pairs={{248,0},{0,8},{8,16},{16,24},{24,32},{32,40},{40,48},{48,56},{56,6... | collective-permute-start | bytes 884744 | tf_op jit(solution)/shard_map/while/body/eval_jaxpr/ppermute | solution.py:17
  303.6 9.9 %collective-permute-start.1 = (f32[64,1152]{1,0:T(8,128)S(1)}, f32[64,1152]{1,0:T(8,128)S(1)}, u32[]{:S(2)}, u32[]{:S(2)}) collective-permute-start(f32[64,1152]{1,0:T(8,128)S(1)} %convolution_add_fusion.7), channel_id=1, source_target_pairs={{248,0},{0,8},{8,16},{16,24},{24,32},{32,40},{40,48},{48,56},{56,6... | collective-permute-start | bytes 884744 | tf_op jit(solution)/shard_map/while/body/eval_jaxpr/ppermute | solution.py:17
  318.1 9.9 %collective-permute-start.1 = (f32[64,1152]{1,0:T(8,128)S(1)}, f32[64,1152]{1,0:T(8,128)S(1)}, u32[]{:S(2)}, u32[]{:S(2)}) collective-permute-start(f32[64,1152]{1,0:T(8,128)S(1)} %convolution_add_fusion.7), channel_id=1, source_target_pairs={{248,0},{0,8},{8,16},{16,24},{24,32},{32,40},{40,48},{48,56},{56,6... | collective-permute-start | bytes 884744 | tf_op jit(solution)/shard_map/while/body/eval_jaxpr/ppermute | solution.py:17
  332.7 9.9 %collective-permute-start.1 = (f32[64,1152]{1,0:T(8,128)S(1)}, f32[64,1152]{1,0:T(8,128)S(1)}, u32[]{:S(2)}, u32[]{:S(2)}) collective-permute-start(f32[64,1152]{1,0:T(8,128)S(1)} %convolution_add_fusion.7), channel_id=1, source_target_pairs={{248,0},{0,8},{8,16},{16,24},{24,32},{32,40},{40,48},{48,56},{56,6... | collective-permute-start | bytes 884744 | tf_op jit(solution)/shard_map/while/body/eval_jaxpr/ppermute | solution.py:17
  521.3 9.9 %collective-permute-start.1 = (f32[64,1152]{1,0:T(8,128)S(1)}, f32[64,1152]{1,0:T(8,128)S(1)}, u32[]{:S(2)}, u32[]{:S(2)}) collective-permute-start(f32[64,1152]{1,0:T(8,128)S(1)} %convolution_add_fusion.7), channel_id=1, source_target_pairs={{248,0},{0,8},{8,16},{16,24},{24,32},{32,40},{40,48},{48,56},{56,6... | collective-permute-start | bytes 884744 | tf_op jit(solution)/shard_map/while/body/eval_jaxpr/ppermute | solution.py:17
  554.9 160.2 %all-reduce.4.cloned.1.call-start = ((), (), s32[]{:S(2)}) async-start(), calls=%async_computation.7 | async-start | bytes 589824
  562.1 237.6 %reduce-scatter.5.cloned.1.call-start = ((), (), s32[]{:S(2)}) async-start(), calls=%async_computation.5 | async-start | bytes 2985984 | tf_op jit(solution)/shard_map/reduce_scatter | solution.py:170
  (64 other events, 577.1 us)
Sparse Core Ops, SparseCore 0:
  10.6 72.1 all-gather.1
  555.0 68.5 reduce-scatter.6
  626.2 88.8 all-reduce.3
  720.3 79.3 reduce-scatter.4
where the time goes:
time: 816 us; the launch traced here: 807 us
  waiting for transfers between devices  421 us (52%)
  matrix products  231 us (28%)
  blocking collectives  64.4 us (8%)
  loops' own time  22.6 us (3%)
  local copies, waits for them, and re-layouts  18.8 us (2%)
  between operations  18.5 us (2%)
  starting transfers between devices  16.7 us (2%)
  other arithmetic  14 us (2%)
    ppermute x63, waiting for transfers between devices, shifted(): return lax.ppermute(block, axis, route)  213 us
    unnamed x6, waiting for transfers between devices  115 us
    dot_general x32, matrix products, pair_terms(): jnp.einsum('ad,bd->ab', left_side, right_side, preferred_element_type=jnp...  91.1 us
    reduce_scatter x1, waiting for transfers between devices, local(): lax.psum_scatter(value_term.astype(jnp.bfloat16).astype(jnp.float32).asty...  82.2 us
    dot_general x31, matrix products, carry_turn(): jnp.dot(coefficient, text_block, preferred_element_type=jnp.float32)  68.1 us
    dot_general x32, matrix products, transposed(): lax.dot_general(coefficient, others, (((0,), (0,)), ((), ())), preferred_...  53.6 us
    all_gather x1, blocking collectives, local(): caption_group = lax.all_gather(caption_b, 'fsdp', axis=0, tiled=True)  43 us
    another operation x1, loops' own time, local(): lax.fori_loop(0, cycle_size - 1, carry_turn, (caption_group, zero_group,...  22.6 us
  transfers between devices with their start and end apart: 69, of which 37 were waited for; matrix products, arithmetic and copies ran while one was open for 12% of the time, Pallas kernels for 0%

commit v1 on v0

v1 whole, which is shorter than its diff:
```python
import math

import jax
import jax.numpy as jnp
from jax import lax
from jax.experimental import pallas as pl
from jax.experimental.pallas import tpu as pltpu
from jax.sharding import PartitionSpec as P

epsilon = 1e-06
F32 = jnp.float32
BF16 = jnp.bfloat16

VMEM_LIMIT = 40 * 1024 * 1024
SEND_ROWS = 80


def vspec():
    return pl.BlockSpec(memory_space=pltpu.VMEM)


def sspec():
    return pl.BlockSpec(memory_space=pltpu.SMEM)


def call(body, out_shapes, in_specs, flops, nbytes, scratch=(), name=None):
    return pl.pallas_call(
        body,
        out_shape=out_shapes,
        in_specs=in_specs,
        out_specs=[vspec() for _ in out_shapes],
        scratch_shapes=list(scratch),
        compiler_params=pltpu.CompilerParams(vmem_limit_bytes=VMEM_LIMIT),
        cost_estimate=pl.CostEstimate(flops=flops, bytes_accessed=nbytes, transcendentals=0),
        name=name,
    )


def nt_dot(a, b):
    return lax.dot_general(a, b, (((1,), (1,)), ((), ())), preferred_element_type=F32)


def tn_dot(a, b):
    return lax.dot_general(a, b, (((0,), (0,)), ((), ())), preferred_element_type=F32)


def head_mask(heads, width):
    head_width = width // heads
    low = lax.broadcasted_iota(jnp.int32, (heads, width), 0) * head_width
    column = lax.broadcasted_iota(jnp.int32, (heads, width), 1)
    return ((column >= low) & (column < low + head_width)).astype(F32)


def pool_body(owners, counts, x_ref, gain_ref, probe_ref, normed_ref, scaled_ref, inv_ref, w_ref, a_ref):
    slots, rows, width = x_ref.shape
    heads = probe_ref.shape[0]
    scale = 1.0 / math.sqrt(width // heads)
    gain = gain_ref[...]
    probe = probe_ref[...]
    for r in range(slots):
        source = jnp.int32(0)
        for k in range(slots):
            source = source + jnp.where(owners[k] == r, k, 0)
        x = x_ref[source].astype(F32)
        mean = jnp.sum(x, axis=-1, keepdims=True) * (1.0 / width)
        centered = x - mean
        var = jnp.sum(centered * centered, axis=-1, keepdims=True) * (1.0 / width)
        inv = lax.rsqrt(var + epsilon)
        normed = centered * inv
        scaled = (normed * gain).astype(BF16)
        scores = nt_dot(probe, scaled) * scale
        valid = lax.broadcasted_iota(jnp.int32, (heads, rows), 1) < counts[source]
        highest = jnp.max(jnp.where(valid, scores, -jnp.inf), axis=-1, keepdims=True)
        raised = jnp.where(valid, jnp.exp(scores - highest), 0.0)
        weights = raised / jnp.sum(raised, axis=-1, keepdims=True)
        normed_ref[r] = normed
        scaled_ref[r] = scaled
        inv_ref[r] = jnp.broadcast_to(inv, inv_ref.shape[1:])
        w_ref[r] = weights
        a_ref[r] = jnp.dot(weights.astype(BF16), scaled, preferred_element_type=F32).astype(BF16)


def image_body(place, mine_ref, other_ref, a_ref, sent_a_ref, full_ref, unit_ref, inv_ref, out_ref):
    shards, part_rows, width = mine_ref.shape
    slots, heads, _ = a_ref.shape
    shard_rows = width // shards

    def put(low_ref, high_ref):
        skip = 2 * part_rows - shard_rows
        for j in range(shards):
            full_ref[pl.ds(j * shard_rows, part_rows), :] = low_ref[j]
            full_ref[pl.ds(j * shard_rows + part_rows, shard_rows - part_rows), :] = high_ref[
                j, pl.ds(skip, part_rows - skip), :
            ]

    @pl.when(place[2] == 0)
    def _():
        put(mine_ref, other_ref)

    @pl.when(place[2] != 0)
    def _():
        put(other_ref, mine_ref)

    wide = jnp.dot(
        a_ref[...].reshape(slots * heads, width), full_ref[...], preferred_element_type=F32
    ).reshape(slots, heads, width)
    context = jnp.sum(wide * head_mask(heads, width)[None], axis=1)
    inv = lax.rsqrt(jnp.sum(context * context, axis=-1, keepdims=True) + epsilon)
    unit = context * inv
    unit_ref[...] = unit
    inv_ref[...] = jnp.broadcast_to(inv, inv_ref.shape)
    for p in range(shards):
        out_ref[p] = jnp.concatenate([sent_a_ref[p].astype(F32), unit], axis=0).astype(BF16)


def pair_body(place, scalars, got_ref, text_ref, d_image_ref, d_text_ref, loss_ref):
    loaders, got_rows, width = got_ref.shape
    slots = d_image_ref.shape[1]
    images = jnp.concatenate(
        [got_ref[s].astype(F32)[got_rows - slots :] for s in range(loaders)], axis=0
    ).astype(BF16)
    texts = text_ref[...]
    count = images.shape[0]
    text_count = texts.shape[0]
    scale = scalars[0]
    logits = scale * nt_dot(images, texts) + scalars[1]
    row = lax.broadcasted_iota(jnp.int32, (count, text_count), 0)
    column = lax.broadcasted_iota(jnp.int32, (count, text_count), 1)
    loader, owner = row // slots, row % slots
    matched = (owner == place[1]) & (column == place[0] * slots + loader)
    matched = matched.astype(F32)
    decay = jnp.exp(-jnp.abs(logits))
    signed = (1.0 - 2.0 * matched) * logits
    losses = jnp.maximum(signed, 0.0) + jnp.log1p(decay)
    sigmoid = jnp.where(logits >= 0.0, 1.0, decay) / (1.0 + decay)
    coefficient = (scale * (sigmoid - matched)).astype(BF16)
    d_image = jnp.dot(coefficient, texts, preferred_element_type=F32)
    d_image_ref[...] = d_image.reshape(d_image_ref.shape).astype(BF16)
    d_text = tn_dot(coefficient, images)
    d_text_ref[...] = d_text.reshape(d_text_ref.shape).astype(BF16)
    per_image = jnp.sum(losses, axis=-1, keepdims=True)
    per_owner = jnp.sum(per_image.reshape(loaders, slots, 1), axis=0)
    loss_ref[...] = jnp.broadcast_to(per_owner, loss_ref.shape)


def back_body(
    got_ref, unit_ref, invn_ref, full_ref, normed_ref, scaled_ref, inv_ref, w_ref, probe_ref,
    gain_ref, loss_ref, out_ref,
):
    slots, rows, width = normed_ref.shape
    heads = probe_ref.shape[0]
    cut = width // slots
    scale = 1.0 / math.sqrt(width // heads)
    d_image = jnp.sum(got_ref[...].astype(F32), axis=0)
    unit = unit_ref[...]
    along = jnp.sum(d_image * unit, axis=-1, keepdims=True)
    d_context = (d_image - unit * along) * invn_ref[:, 0:1]
    d_context = d_context.astype(BF16).astype(F32)
    spread = (d_context[:, None, :] * head_mask(heads, width)[None]).reshape(slots * heads, width)
    back = nt_dot(spread.astype(BF16), full_ref[...]).astype(BF16).reshape(slots, heads, width)
    gain = gain_ref[...]
    probe = probe_ref[...]
    probe_total = jnp.zeros((heads, width), F32)
    gain_total = jnp.zeros((8, width), F32)
    for r in range(slots):
        scaled = scaled_ref[r]
        weights = w_ref[r]
        d_weights = nt_dot(back[r], scaled)
        centre = jnp.sum(weights * d_weights, axis=-1, keepdims=True)
        d_scores = (weights * (d_weights - centre) * scale).astype(BF16)
        probe_total = probe_total + jnp.dot(d_scores, scaled, preferred_element_type=F32)
        d_scaled = tn_dot(
            jnp.concatenate([weights.astype(BF16), d_scores], axis=0),
            jnp.concatenate([back[r], probe], axis=0),
        )
        normed = normed_ref[r]
        gain_total = gain_total + jnp.sum((d_scaled * normed).reshape(rows // 8, 8, width), axis=0)
        grad_in = d_scaled * gain
        mean_a = jnp.sum(grad_in, axis=-1, keepdims=True) * (1.0 / width)
        mean_b = jnp.sum(grad_in * normed, axis=-1, keepdims=True) * (1.0 / width)
        row_grad = inv_ref[r][:, 0:1] * (grad_in - mean_a - normed * mean_b)
        out_ref[r, 0:rows, :] = row_grad.astype(BF16)
    gain_sum = jnp.sum(gain_total, axis=0, keepdims=True)
    loss = loss_ref[...]
    high = loss.astype(BF16).astype(F32)
    middle = (loss - high).astype(BF16).astype(F32)
    low = loss - high - middle
    for p in range(slots):
        lanes = slice(p * cut, (p + 1) * cut)
        pad = jnp.zeros((8, 256 - cut), F32)
        losses = jnp.concatenate(
            [high[p : p + 1], middle[p : p + 1], low[p : p + 1], jnp.zeros((5, 128), F32)], axis=0
        )
        misc = jnp.concatenate(
            [
                probe_total[0:8, lanes],
                pad,
                probe_total[8:16, lanes],
                pad,
                jnp.broadcast_to(gain_sum[:, lanes], (8, cut)),
                pad,
                losses,
                jnp.zeros((8, width - 896), F32),
            ],
            axis=1,
        )
        out_ref[p, rows : rows + 16, :] = jnp.concatenate([d_context, misc], axis=0).astype(BF16)


def last_body(got_ref, a_ref, row_ref, value_ref, probe_ref, gain_ref, loss_ref, *, texts):
    loaders, got_rows, width = got_ref.shape
    rows = row_ref.shape[2]
    heads, images, cut = a_ref.shape
    tails = []
    for s in range(loaders):
        row_ref[0, s] = got_ref[s, 0:rows, :]
        tails.append(got_ref[s, rows : rows + 16, :].astype(F32))
    d_context = jnp.concatenate([t[0:8] for t in tails], axis=0)
    mask = head_mask(heads, width)
    total = jnp.zeros((cut, width), F32)
    for h in range(heads):
        total = total + tn_dot(a_ref[h], (d_context * mask[h : h + 1]).astype(BF16))
    value_ref[0] = total.astype(BF16)
    misc = tails[0][8:16]
    for s in range(1, loaders):
        misc = misc + tails[s][8:16]
    probe_ref[...] = jnp.concatenate([misc[:, 0:cut], misc[:, 256 : 256 + cut]], axis=0).astype(BF16)
    gain_ref[...] = misc[0:1, 512 : 512 + cut].astype(BF16)
    loss_ref[...] = (misc[0:1, 768:769] + misc[1:2, 768:769] + misc[2:3, 768:769]) / texts


def local(
    patches, counts, owners, captions, norm_gain, key_probe, value_weight, logit_scale, logit_bias
):
    _, slots, rows, width = patches.shape
    heads = key_probe.shape[1]
    peers = lax.axis_size("fsdp")
    ranks = lax.axis_size("dp")
    cut = width // peers
    dp_index = lax.axis_index("dp")
    core = dp_index % 2
    place = jnp.stack([dp_index, lax.axis_index("fsdp"), core]).astype(jnp.int32)
    scalars = jnp.concatenate([logit_scale, logit_bias])
    gain = norm_gain.reshape(1, width)
    probe = key_probe.T

    start = core * (cut - SEND_ROWS)
    part = lax.dynamic_slice_in_dim(value_weight, start, SEND_ROWS, axis=0)
    mine = lax.all_to_all(
        jnp.broadcast_to(part[None], (peers, SEND_ROWS, width)), "fsdp", 0, 0, tiled=True
    )
    other = lax.ppermute(mine, "dp", [(i, i ^ 1) for i in range(ranks)])

    caption_f = captions[0].astype(F32)
    caption_inv = lax.rsqrt(jnp.sum(caption_f * caption_f, axis=-1, keepdims=True) + epsilon)
    caption_unit = caption_f * caption_inv
    texts = lax.all_gather(caption_unit.astype(BF16), "dp", axis=0, tiled=True)

    shape = jax.ShapeDtypeStruct
    normed, scaled, inv_std, weights, pooled = call(
        pool_body,
        [
            shape((slots, rows, width), F32),
            shape((slots, rows, width), BF16),
            shape((slots, rows, 128), F32),
            shape((slots, heads, rows), F32),
            shape((slots, heads, width), BF16),
        ],
        [sspec(), sspec(), vspec(), vspec(), vspec()],
        40_000_000,
        4_000_000,
        name="pool",
    )(owners[0], counts[0], patches[0], gain, probe)
    sent_pooled = (
        pooled.reshape(slots, heads, peers, cut)
        .transpose(2, 1, 0, 3)
        .reshape(peers, heads, slots * cut)
    )
    full, unit, inv_norm, sent = call(
        image_body,
        [
            shape((width, width), BF16),
            shape((slots, width), F32),
            shape((slots, 128), F32),
            shape((peers, heads + slots, width), BF16),
        ],
        [sspec(), vspec(), vspec(), vspec(), vspec()],
        400_000_000,
        6_000_000,
        name="image",
    )(place, mine, other, pooled, sent_pooled)
    got = lax.all_to_all(sent, "fsdp", 0, 0, tiled=True)
    d_image_part, d_text_part, loss_sums = call(
        pair_body,
        [
            shape((peers, slots, width), BF16),
            shape((ranks, slots, width), BF16),
            shape((slots, 128), F32),
        ],
        [sspec(), sspec(), vspec(), vspec()],
        120_000_000,
        2_000_000,
        name="pair",
    )(place, scalars, got, texts)
    d_image_got = lax.all_to_all(d_image_part, "fsdp", 0, 0, tiled=True)
    d_text_got = lax.all_to_all(d_text_part, "dp", 0, 0, tiled=True)

    outgoing = call(
        back_body,
        [shape((peers, rows + 16, width), BF16)],
        [vspec()] * 11,
        500_000_000,
        8_000_000,
        name="back",
    )(
        d_image_got, unit, inv_norm, full, normed, scaled, inv_std, weights, probe, gain, loss_sums
    )[0]
    arrived = lax.all_to_all(outgoing, "fsdp", 0, 0, tiled=True)

    pooled_got = (
        got[:, :heads]
        .reshape(peers, heads, slots, cut)
        .transpose(1, 0, 2, 3)
        .reshape(heads, peers * slots, cut)
    )
    batch = ranks * peers * slots

    def last(*refs):
        last_body(*refs, texts=batch)

    row_grad, value_grad, probe_t, gain_grad, loss_part = call(
        last,
        [
            shape((1, slots, rows, width), BF16),
            shape((1, cut, width), BF16),
            shape((heads, cut), BF16),
            shape((1, cut), BF16),
            shape((1, 1), F32),
        ],
        [vspec(), vspec()],
        400_000_000,
        3_000_000,
        name="last",
    )(arrived, pooled_got)

    d_caption = jnp.sum(d_text_got.astype(F32), axis=0)
    text_grad = (
        (d_caption - caption_unit * jnp.sum(d_caption * caption_unit, axis=-1, keepdims=True))
        * caption_inv
    ).astype(BF16)
    return (loss_part, row_grad, text_grad[None], value_grad, probe_t.T[None], gain_grad)


def solution(mesh):
    placed = (
        P(("dp", "fsdp"), None, None, None),
        P(("dp", "fsdp"), None),
        P(("dp", "fsdp"), None),
        P(("dp", "fsdp"), None, None),
        P(),
        P(),
        P("fsdp", None),
        P(),
        P(),
    )
    return jax.shard_map(
        local,
        mesh=mesh,
        in_specs=placed,
        out_specs=(
            P("dp", "fsdp"),
            P(("dp", "fsdp"), None, None, None),
            P(("dp", "fsdp"), None, None),
            P("dp", "fsdp", None),
            P("dp", "fsdp", None),
            P("dp", "fsdp"),
        ),
        check_vma=False,
    )
```

time: 816 us -> 162 us (0.20)
  waiting for transfers between devices: 421 us -> 24 us
  matrix products: 231 us -> 0 us
  loops' own time: 22.6 us -> 0 us
  blocking collectives: 64.4 us -> 81.5 us
  between operations: 18.5 us -> 2.17 us
  Pallas kernels: 0 us -> 15.5 us
  other arithmetic: 14 us -> 1.95 us
    dot_general x104 -> x0, matrix products: 231 us -> none  [the longest x32 91.1 us: pair_terms(): jnp.einsum('ad,bd->ab', left_side, right_side, preferred_element_type=jnp...]
    ppermute x63 -> x1, waiting for transfers between devices: 213 us -> 0.01 us  [local(): other = lax.ppermute(mine, 'dp', [(i, i ^ 1) for i in range(ranks)])]
    unnamed x6 -> x0, waiting for transfers between devices: 115 us -> none
    reduce_scatter x1 -> x0, waiting for transfers between devices: 82.2 us -> none  [local(): lax.psum_scatter(value_term.astype(jnp.bfloat16).astype(jnp.float32).asty...]
    all_to_all x0 -> x2, blocking collectives: none -> 42.5 us  [the longest x1 27.9 us: local(): lax.all_to_all(jnp.broadcast_to(part[None], (peers, SEND_ROWS, width)), '...]
    another operation x1 -> x0, loops' own time: 22.6 us -> none  [local(): lax.fori_loop(0, cycle_size - 1, carry_turn, (caption_group, zero_group,...]
    unnamed x1 -> x0, blocking collectives: 21.4 us -> none
    all_to_all x2 -> x3, waiting for transfers between devices: 4.34 us -> 23.9 us  [the longest x1 13.8 us: local(): arrived = lax.all_to_all(outgoing, 'fsdp', 0, 0, tiled=True)]
  transfers between devices with their start and end apart: 69 -> 4, of which waited for: 37 -> 2; matrix products, arithmetic and copies ran while one was open for 12% -> 7% of each run, Pallas kernels for 0% -> 6%
where the time goes in v1:
time: 162 us; the launch traced here: 161 us
  blocking collectives  81.5 us (50%)
  waiting for transfers between devices  24 us (15%)
  local copies, waits for them, and re-layouts  23.2 us (14%)
  Pallas kernels  15.5 us (10%)
  starting transfers between devices  12.5 us (8%)
  between operations  2.17 us (1%)
  other arithmetic  1.95 us (1%)
    all_gather x1, blocking collectives, local(): texts = lax.all_gather(caption_unit.astype(BF16), 'dp', axis=0, tiled=True)  39 us
    all_to_all x1, blocking collectives, local(): lax.all_to_all(jnp.broadcast_to(part[None], (peers, SEND_ROWS, width)), '...  27.9 us
    all_to_all x1, blocking collectives, local(): d_image_got = lax.all_to_all(d_image_part, 'fsdp', 0, 0, tiled=True)  14.7 us
    all_to_all x1, waiting for transfers between devices, local(): arrived = lax.all_to_all(outgoing, 'fsdp', 0, 0, tiled=True)  13.8 us
    unnamed x42, local copies, waits for them, and re-layouts  13.7 us
    all_to_all x1, waiting for transfers between devices, local(): d_text_got = lax.all_to_all(d_text_part, 'dp', 0, 0, tiled=True)  10.1 us
    all_to_all x1, starting transfers between devices, local(): d_text_got = lax.all_to_all(d_text_part, 'dp', 0, 0, tiled=True)  5.51 us
    pallas_call x1, Pallas kernels, local(): call(back_body, [shape((peers, rows + 16, width), BF16)], [vspec()] * 11,...  5.05 us
  transfers between devices with their start and end apart: 4, of which 2 were waited for; matrix products, arithmetic and copies ran while one was open for 7% of the time, Pallas kernels for 6%

profile of v1, /device:TPU:2, one launch (start us, length us, event | category | flops | bytes accessed | tf_op | source)
XLA Modules:
  0.0 160.8 jit_solution(12120375978981832932)
XLA Ops:
  1.8 27.9 %all_to_all.25.mine_ref = bf16[8,80,1152]{2,1,0:T(8,128)(2,1)S(1)} all-to-all(bf16[8,80,1152]{2,1,0:T(8,128)(2,1)S(1)} %broadcast_in_dim.4), channel_id=1, replica_groups=mesh['dp'=32,'fsdp'=8] {'fsdp'}, dimensions={0} | all-to-all | bytes 2949120 | tf_op jit(solution)/shard_map/all_to_all | solution.py:249
  29.7 1.2 copy-done.10
  30.9 3.9 %pool.1 = (f32[8,48,1152]{2,1,0:T(8,128)S(1)}, bf16[8,48,1152]{2,1,0:T(8,128)(2,1)S(1)}, f32[8,48,128]{2,1,0:T(8,128)S(1)}, f32[8,16,48]{2,1,0:T(8,128)S(1)}, bf16[8,16,1152]{2,1,0:T(8,128)(2,1)S(1)}) custom-call(s32[8]{0:T(128)S(1)} %bitcast.40, s32[8]{0:T(128)S(1)} %bitcast.41, bf16[8,48,1152]{2,1,0:T(8,128)(2,1)S(1)} %bitcast.37, ...), custom_call_target="tpu_custom_call" | custom-call | flops 40000000 | bytes 4000000 | tf_op jit(solution)/shard_map/pool/pallas_call | solution.py:260
  34.8 1.2 copy-done.3
  38.3 2.5 %reshape.58 = bf16[8,16,8,144]{3,2,1,0:T(8,128)(2,1)} reshape(bf16[8,16,1152]{2,1,0:T(8,128)(2,1)} %copy-done.5) | data formatting | bytes 589824 | tf_op jit(solution)/shard_map/reshape | solution.py:275
  40.7 2.1 %copy.20 = bf16[8,16,8,144]{3,0,1,2:T(8,128)(2,1)} copy(bf16[8,16,8,144]{3,2,1,0:T(8,128)(2,1)} %reshape.58) | data formatting | bytes 589824 | tf_op jit(solution)/shard_map/reshape | solution.py:275
  42.9 2.2 %reshape.59.sent_a_ref = bf16[8,16,1152]{2,1,0:T(8,128)(2,1)} reshape(bf16[8,16,8,144]{3,2,1,0:T(8,128)(2,1)} %bitcast.42) | data formatting | bytes 589824 | tf_op jit(solution)/shard_map/reshape | solution.py:277
  47.3 1.0 copy-done.6
  49.2 1.4 image.1
  50.7 1.5 copy-done.1
  53.6 3.5 %all-to-all-start.1 = ((bf16[8,24,1152]{2,1,0:T(8,128)(2,1)}), bf16[8,24,1152]{2,1,0:T(8,128)(2,1)S(1)}, u32[]{:S(2)}, u32[]{:S(2)}) async-start(bf16[8,24,1152]{2,1,0:T(8,128)(2,1)} %copy-done.11), calls=%async_computation.1 | async-start | bytes 884736 | tf_op jit(solution)/shard_map/all_to_all | solution.py:292
  57.2 39.0 %all_gather.3.text_ref = bf16[256,1152]{1,0:T(8,128)(2,1)S(1)} all-gather(bf16[8,1152]{1,0:T(8,128)(2,1)} %fusion.3), channel_id=1, replica_groups=mesh['dp'=32,'fsdp'=8] {'dp'}, dimensions={0}, use_global_device_ids=true | all-gather | bytes 608256 | tf_op jit(solution)/shard_map/all_gather | solution.py:257
  96.1 2.3 %pair.1 = (bf16[8,8,1152]{2,1,0:T(8,128)(2,1)S(1)}, bf16[32,8,1152]{2,1,0:T(8,128)(2,1)}, f32[8,128]{1,0:T(8,128)S(1)}) custom-call(s32[3]{0:T(128)S(1)} %pad_add_fusion.place, f32[2]{0:T(128)S(1)} %pad_maximum_fusion.scalars, bf16[8,24,1152]{2,1,0:T(8,128)(2,1)S(1)} %all-to-all-done.1.got_ref, bf16[256,1152]{1,0:T(8,128)(2,1)S(1)} %all_gather.3.text_ref), custom_call_target="tpu_custom_call" | custom-call | flops 120000000 | bytes 2000000 | tf_op jit(solution)/shard_map/pair/pallas_call | solution.py:293
  98.5 14.7 %all_to_all.26.got_ref = bf16[8,8,1152]{2,1,0:T(8,128)(2,1)S(1)} all-to-all(bf16[8,8,1152]{2,1,0:T(8,128)(2,1)S(1)} %get-tuple-element.25), channel_id=1, replica_groups=mesh['dp'=32,'fsdp'=8] {'fsdp'}, dimensions={0} | all-to-all | bytes 294912 | tf_op jit(solution)/shard_map/all_to_all | solution.py:305
  113.1 5.5 %all-to-all-start.4 = ((bf16[32,8,1152]{2,1,0:T(8,128)(2,1)}), bf16[32,8,1152]{2,1,0:T(8,128)(2,1)S(1)}, u32[]{:S(2)}, u32[]{:S(2)}) async-start(bf16[32,8,1152]{2,1,0:T(8,128)(2,1)} %get-tuple-element.36), calls=%async_computation.4 | async-start | bytes 1179648 | tf_op jit(solution)/shard_map/all_to_all | solution.py:306
  118.7 1.7 %copy-done.2 = bf16[1152,1152]{1,0:T(8,128)(2,1)S(1)} copy-done((bf16[1152,1152]{1,0:T(8,128)(2,1)S(1)}, bf16[1152,1152]{1,0:T(8,128)(2,1)}, u32[]{:S(2)}) %copy-start.2) | copy-done | bytes 2654232
  120.4 1.5 copy-done.4
  121.9 5.1 %back.1 = bf16[8,64,1152]{2,1,0:T(8,128)(2,1)} custom-call(bf16[8,8,1152]{2,1,0:T(8,128)(2,1)S(1)} %all_to_all.26.got_ref, f32[8,1152]{1,0:T(8,128)S(1)} %copy-done.16, f32[8,128]{1,0:T(8,128)S(1)} %get-tuple-element.27.invn_ref, bf16[1152,1152]{1,0:T(8,128)(2,1)S(1)} %copy-done.2, f32[8,48,1152]{2,1,0:T(8,128)S(1)} %copy-done.4, ...), custom_call_target="tpu_custom_call" | custom-call | flops 500000000 | bytes 8000000 | tf_op jit(solution)/shard_map/back/pallas_call | solution.py:308
  127.0 10.1 %all-to-all-done.4 = bf16[32,8,1152]{2,1,0:T(8,128)(2,1)S(1)} async-done(((bf16[32,8,1152]{2,1,0:T(8,128)(2,1)}), bf16[32,8,1152]{2,1,0:T(8,128)(2,1)S(1)}, u32[]{:S(2)}, u32[]{:S(2)}) %all-to-all-start.4) | async-done | bytes 589856 | tf_op jit(solution)/shard_map/all_to_all | solution.py:306
  137.1 3.6 %all-to-all-start.3 = ((bf16[8,64,1152]{2,1,0:T(8,128)(2,1)}), bf16[8,64,1152]{2,1,0:T(8,128)(2,1)S(1)}, u32[]{:S(2)}, u32[]{:S(2)}) async-start(bf16[8,64,1152]{2,1,0:T(8,128)(2,1)} %back.1), calls=%async_computation.3 | async-start | bytes 2359296 | tf_op jit(solution)/shard_map/all_to_all | solution.py:318
  140.7 1.5 reshape.60
  142.2 1.1 copy.19
  144.2 13.8 %all-to-all-done.3.refs_0_ = bf16[8,64,1152]{2,1,0:T(8,128)(2,1)S(1)} async-done(((bf16[8,64,1152]{2,1,0:T(8,128)(2,1)}), bf16[8,64,1152]{2,1,0:T(8,128)(2,1)S(1)}, u32[]{:S(2)}, u32[]{:S(2)}) %all-to-all-start.3) | async-done | bytes 1179680 | tf_op jit(solution)/shard_map/all_to_all | solution.py:318
  158.0 2.7 %last.1 = (bf16[1,8,48,1152]{3,2,1,0:T(8,128)(2,1)}, bf16[1,144,1152]{2,1,0:T(8,128)(2,1)}, bf16[16,144]{1,0:T(8,128)(2,1)}, bf16[1,144]{1,0:T(2,128)(2,1)}, f32[1,1]{1,0:T(1,128)}) custom-call(bf16[8,64,1152]{2,1,0:T(8,128)(2,1)S(1)} %all-to-all-done.3.refs_0_, bf16[16,64,144]{2,1,0:T(8,128)(2,1)S(1)} %bitcast.36), custom_call_target="tpu_custom_call" | custom-call | flops 400000000 | bytes 3000000 | tf_op jit(solution)/shard_map/last/pallas_call | solution.py:331
  (51 shorter events, 7.7 us)
Async XLA Ops:
  0.6 1.0 copy-start
  1.7 27.9 %copy-start.20 = (f32[1152]{0:T(1024)S(1)}, f32[1152]{0:T(1024)}, u32[]{:S(2)}) copy-start(f32[1152]{0:T(1024)} %param.13) | copy-start | bytes 13828
  1.8 27.9 %copy-start.12 = (bf16[1152,16]{0,1:T(8,128)(2,1)S(1)}, bf16[1152,16]{0,1:T(8,128)(2,1)}, u32[]{:S(2)}) copy-start(bf16[1152,16]{0,1:T(8,128)(2,1)} %param.14) | copy-start | bytes 110596
  1.8 27.9 %copy-start.17 = (s32[1,8]{1,0:T(1,128)S(1)}, s32[1,8]{1,0:T(1,128)}, u32[]{:S(2)}) copy-start(s32[1,8]{1,0:T(1,128)} %param.11) | copy-start | bytes 100
  1.8 27.9 %copy-start.18 = (s32[1,8]{1,0:T(1,128)S(1)}, s32[1,8]{1,0:T(1,128)}, u32[]{:S(2)}) copy-start(s32[1,8]{1,0:T(1,128)} %param.10) | copy-start | bytes 100
  29.7 17.7 %collective-permute-start = (bf16[8,80,1152]{2,1,0:T(8,128)(2,1)S(1)}, bf16[8,80,1152]{2,1,0:T(8,128)(2,1)S(1)}, u32[]{:S(2)}, u32[]{:S(2)}) collective-permute-start(bf16[8,80,1152]{2,1,0:T(8,128)(2,1)S(1)} %all_to_all.25.mine_ref), channel_id=1, source_target_pairs={{0,8},{8,0},{16,24},{24,16},{32,40},{40,32},{48,56},{56,48},{64,72... | collective-permute-start | bytes 4423688 | tf_op jit(solution)/shard_map/ppermute | solution.py:252
  29.7 1.2 copy-start.10
  34.8 1.2 copy-start.3
  36.0 0.7 copy-start.5
  36.7 0.9 copy-start.8
  38.3 8.2 %copy-start.19 = (bf16[1,8,1152]{2,1,0:T(8,128)(2,1)S(1)}, bf16[1,8,1152]{2,1,0:T(8,128)(2,1)}, u32[]{:S(2)}) copy-start(bf16[1,8,1152]{2,1,0:T(8,128)(2,1)} %param.12) | copy-start | bytes 55300
  47.3 1.0 copy-start.6
  48.3 1.0 copy-start.7
  50.7 1.5 copy-start.1
  52.2 0.8 copy-start.11
  53.0 0.6 copy-start.15
  53.6 42.5 %all-to-all-start.1 = ((bf16[8,24,1152]{2,1,0:T(8,128)(2,1)}), bf16[8,24,1152]{2,1,0:T(8,128)(2,1)S(1)}, u32[]{:S(2)}, u32[]{:S(2)}) async-start(bf16[8,24,1152]{2,1,0:T(8,128)(2,1)} %copy-done.11), calls=%async_computation.1 | async-start | bytes 884736 | tf_op jit(solution)/shard_map/all_to_all | solution.py:292
  57.2 61.5 %copy-start.9 = (bf16[8,48,1152]{2,1,0:T(8,128)(2,1)S(1)}, bf16[8,48,1152]{2,1,0:T(8,128)(2,1)}, u32[]{:S(2)}) copy-start(bf16[8,48,1152]{2,1,0:T(8,128)(2,1)} %copy-done.8) | copy-start | bytes 2654212
  57.2 61.5 %copy-start.14 = (f32[8,16,48]{2,1,0:T(8,128)S(1)}, f32[8,16,48]{2,1,0:T(8,128)}, u32[]{:S(2)}) copy-start(f32[8,16,48]{2,1,0:T(8,128)} %copy-done.13) | copy-start | bytes 73732
  57.2 61.5 %copy-start.16 = (f32[8,1152]{1,0:T(8,128)S(1)}, f32[8,1152]{1,0:T(8,128)}, u32[]{:S(2)}) copy-start(f32[8,1152]{1,0:T(8,128)} %copy-done.15) | copy-start | bytes 110596
  113.1 24.0 %all-to-all-start.4 = ((bf16[32,8,1152]{2,1,0:T(8,128)(2,1)}), bf16[32,8,1152]{2,1,0:T(8,128)(2,1)S(1)}, u32[]{:S(2)}, u32[]{:S(2)}) async-start(bf16[32,8,1152]{2,1,0:T(8,128)(2,1)} %get-tuple-element.36), calls=%async_computation.4 | async-start | bytes 1179648 | tf_op jit(solution)/shard_map/all_to_all | solution.py:306
  118.7 1.8 %copy-start.2 = (bf16[1152,1152]{1,0:T(8,128)(2,1)S(1)}, bf16[1152,1152]{1,0:T(8,128)(2,1)}, u32[]{:S(2)}) copy-start(bf16[1152,1152]{1,0:T(8,128)(2,1)} %copy-done.1) | copy-start | bytes 7962628
  120.4 1.5 copy-start.4
  137.1 21.0 %all-to-all-start.3 = ((bf16[8,64,1152]{2,1,0:T(8,128)(2,1)}), bf16[8,64,1152]{2,1,0:T(8,128)(2,1)S(1)}, u32[]{:S(2)}, u32[]{:S(2)}) async-start(bf16[8,64,1152]{2,1,0:T(8,128)(2,1)} %back.1), calls=%async_computation.3 | async-start | bytes 2359296 | tf_op jit(solution)/shard_map/all_to_all | solution.py:318
  (1 other events, 0.6 us)

commit v2 on v1

v2 whole, which is shorter than its diff:
```python
import math

import jax
import jax.numpy as jnp
from jax import lax
from jax.experimental import pallas as pl
from jax.experimental.pallas import tpu as pltpu
from jax.sharding import PartitionSpec as P

epsilon = 1e-06
F32 = jnp.float32
BF16 = jnp.bfloat16

VMEM_LIMIT = 16 * 1024 * 1024
VMEM_LARGE = 60_180_000
SEND_ROWS = 80


TEXT_BITS = (8, 4, 2, 16, 1)


def swapped(block, bit):
    return lax.ppermute(block, "dp", [(i, i ^ bit) for i in range(lax.axis_size("dp"))])


def vspec():
    return pl.BlockSpec(memory_space=pltpu.VMEM)


def sspec():
    return pl.BlockSpec(memory_space=pltpu.SMEM)


def hspec():
    return pl.BlockSpec(memory_space=pltpu.HBM)


def call(body, outs, in_specs, flops, nbytes, scratch=(), name=None, limit=VMEM_LIMIT):
    return pl.pallas_call(
        body,
        out_shape=[shape for shape, _ in outs],
        in_specs=in_specs,
        out_specs=[spec for _, spec in outs],
        scratch_shapes=list(scratch),
        compiler_params=pltpu.CompilerParams(vmem_limit_bytes=limit),
        cost_estimate=pl.CostEstimate(flops=flops, bytes_accessed=nbytes, transcendentals=0),
        name=name,
    )


def source_of(owners, owner, slots):
    source = jnp.int32(0)
    for k in range(slots):
        source = source + jnp.where(owners[k] == owner, k, 0)
    return source


def nt_dot(a, b):
    return lax.dot_general(a, b, (((1,), (1,)), ((), ())), preferred_element_type=F32)


def tn_dot(a, b):
    return lax.dot_general(a, b, (((0,), (0,)), ((), ())), preferred_element_type=F32)


def head_mask(heads, width):
    head_width = width // heads
    low = lax.broadcasted_iota(jnp.int32, (heads, width), 0) * head_width
    column = lax.broadcasted_iota(jnp.int32, (heads, width), 1)
    return ((column >= low) & (column < low + head_width)).astype(F32)


def pool_body(owners, counts, x_ref, gain_ref, probe_ref, stats_ref, w_ref, a_ref, scaled_ref):
    slots, rows, width = x_ref.shape
    heads = probe_ref.shape[0]
    scale = 1.0 / math.sqrt(width // heads)
    gain = gain_ref[...]
    lanes = slots * heads
    column = lax.broadcasted_iota(jnp.int32, (rows, lanes), 1)
    patch = lax.broadcasted_iota(jnp.int32, (rows, lanes), 0)
    masks = []
    for r in range(slots):
        source = source_of(owners, r, slots)
        x = x_ref[source].astype(F32)
        mean = jnp.sum(x, axis=-1, keepdims=True) * (1.0 / width)
        centered = x - mean
        var = jnp.sum(centered * centered, axis=-1, keepdims=True) * (1.0 / width)
        inv = lax.rsqrt(var + epsilon)
        scaled_ref[r * rows : (r + 1) * rows, :] = ((centered * inv) * gain).astype(BF16)
        stats_ref[r * rows : (r + 1) * rows, :] = jnp.where(column < lanes // 2, mean, inv)
        own = (column >= r * heads) & (column < (r + 1) * heads)
        masks.append(jnp.where(own & (patch < counts[source]), 1.0, 0.0))
    valid = jnp.concatenate(masks, axis=0) > 0.5
    scaled = scaled_ref[...]
    tiled = jnp.concatenate([probe_ref[...].astype(F32)] * slots, axis=0).astype(BF16)
    scores = nt_dot(scaled, tiled) * scale
    highest = jnp.max(jnp.where(valid, scores, -jnp.inf), axis=0, keepdims=True)
    raised = jnp.where(valid, jnp.exp(jnp.where(valid, scores - highest, 0.0)), 0.0)
    weights = raised / jnp.sum(raised, axis=0, keepdims=True)
    w_ref[...] = weights
    a_ref[...] = tn_dot(weights.astype(BF16), scaled).astype(BF16)


def image_body(
    mine_ref, other_ref, a_ref, full_out, unit_ref, inv_ref, out_ref, full, sem
):
    shards, part_rows, width = mine_ref.shape
    slots = unit_ref.shape[0]
    heads = a_ref.shape[0] // slots
    cut = width // shards
    rest = cut - part_rows
    core = lax.rem(lax.axis_index("dp"), 2)

    def put(low_ref, high_ref):
        for j in range(shards):
            full[j * cut : j * cut + part_rows, :] = low_ref[j]
            full[j * cut + part_rows : (j + 1) * cut, :] = high_ref[j, part_rows - rest :, :]

    @pl.when(core == 0)
    def _():
        put(mine_ref, other_ref)

    @pl.when(core != 0)
    def _():
        put(other_ref, mine_ref)

    copy = pltpu.make_async_copy(full, full_out, sem)
    copy.start()
    pooled = a_ref[...]
    wide = jnp.dot(pooled, full[...], preferred_element_type=F32).reshape(slots, heads, width)
    context = jnp.sum(wide * head_mask(heads, width)[None], axis=1)
    inv = lax.rsqrt(jnp.sum(context * context, axis=-1, keepdims=True) + epsilon)
    unit = context * inv
    unit_ref[...] = unit
    inv_ref[...] = jnp.broadcast_to(inv, inv_ref.shape)
    wide_pooled = pooled.astype(F32)
    for p in range(shards):
        moved = jnp.concatenate(
            [
                wide_pooled[b * heads : (b + 1) * heads, p * cut : (p + 1) * cut]
                for b in range(slots)
            ],
            axis=1,
        )
        out_ref[p] = jnp.concatenate([moved, unit], axis=0).astype(BF16)
    copy.wait()


def pair_body(place, scalars, got_ref, text_ref, d_image_ref, keep_ref, send_ref, loss_ref):
    loaders, got_rows, width = got_ref.shape
    slots = d_image_ref.shape[1]
    images = jnp.concatenate(
        [got_ref[s].astype(F32)[got_rows - slots :] for s in range(loaders)], axis=0
    ).astype(BF16)
    texts = text_ref[...]
    count = images.shape[0]
    text_count = texts.shape[0]
    scale = scalars[0]
    logits = scale * nt_dot(images, texts) + scalars[1]
    row = lax.broadcasted_iota(jnp.int32, (count, text_count), 0)
    column = lax.broadcasted_iota(jnp.int32, (count, text_count), 1)
    loader, owner = row // slots, row % slots
    matched = (owner == place[0]) & (column == loader)
    matched = matched.astype(F32)
    decay = jnp.exp(-jnp.abs(logits))
    signed = (1.0 - 2.0 * matched) * logits
    losses = jnp.maximum(signed, 0.0) + jnp.log1p(decay)
    sigmoid = jnp.where(logits >= 0.0, 1.0, decay) / (1.0 + decay)
    coefficient = (scale * (sigmoid - matched)).astype(BF16)
    d_image = jnp.dot(coefficient, texts, preferred_element_type=F32)
    d_image_ref[...] = d_image.reshape(d_image_ref.shape).astype(BF16)
    d_text = tn_dot(coefficient, images)
    keep_ref[...] = d_text[: text_count // 2]
    send_ref[...] = d_text[text_count // 2 :].astype(BF16)
    per_image = jnp.sum(losses, axis=-1, keepdims=True)
    per_owner = jnp.sum(per_image.reshape(loaders, slots, 1), axis=0)
    loss_ref[...] = jnp.broadcast_to(per_owner, loss_ref.shape)


def back_body(
    owners, got_ref, unit_ref, invn_ref, full_in, x_in, stats_in, w_in, probe_ref, gain_ref, loss_ref,
    out_ref, full, x_ref, stats_ref, w_ref, normed_ref, scaled_ref, right, result, sems,
):
    slots, rows, width = x_ref.shape
    heads = probe_ref.shape[0]
    lanes = slots * heads
    cut = width // slots
    scale = 1.0 / math.sqrt(width // heads)
    chunk = width // 3
    patches = [
        pltpu.make_async_copy(x_in.at[0, source_of(owners, r, slots)], x_ref.at[r], sems.at[r])
        for r in range(slots)
    ]
    small = [
        pltpu.make_async_copy(stats_in, stats_ref, sems.at[slots]),
        pltpu.make_async_copy(w_in, w_ref, sems.at[slots + 1]),
    ]
    values = [
        pltpu.make_async_copy(
            full_in.at[pl.ds(c * chunk, chunk), :],
            full.at[pl.ds(c * chunk, chunk), :],
            sems.at[slots + 2 + c],
        )
        for c in range(3)
    ]
    for copy in small[:1] + patches + values + small[1:]:
        copy.start()
    d_image = jnp.sum(got_ref[...].astype(F32), axis=0)
    unit = unit_ref[...]
    along = jnp.sum(d_image * unit, axis=-1, keepdims=True)
    d_context = (d_image - unit * along) * invn_ref[:, 0:1]
    d_context = d_context.astype(BF16).astype(F32)
    spread = (d_context[:, None, :] * head_mask(heads, width)[None]).reshape(lanes, width).astype(BF16)
    gain = gain_ref[...]
    right[lanes:, :] = jnp.concatenate([probe_ref[...].astype(F32)] * slots, axis=0).astype(BF16)
    small[0].wait()
    for r in range(slots):
        patches[r].wait()
        at = slice(r * rows, (r + 1) * rows)
        normed = (x_ref[r].astype(F32) - stats_ref[at, 0:1]) * stats_ref[at, lanes // 2 : lanes // 2 + 1]
        normed_ref[at, :] = normed
        scaled_ref[at, :] = (normed * gain).astype(BF16)
    for c in range(3):
        values[c].wait()
        at = slice(c * chunk, (c + 1) * chunk)
        right[0:lanes, at] = nt_dot(spread, full[at, :]).astype(BF16)
    small[1].wait()
    scaled = scaled_ref[...]
    weights = w_ref[...]
    d_weights = nt_dot(scaled, right[0:lanes, :])
    centre = jnp.sum(weights * d_weights, axis=0, keepdims=True)
    d_scores = (weights * (d_weights - centre) * scale).astype(BF16)
    left = jnp.concatenate([weights.astype(BF16), d_scores], axis=1)
    gain_total = jnp.zeros((8, width), F32)
    sent = []
    half = slots // 2
    for g in range(2):
        d_scaled_half = jnp.dot(
            left[g * half * rows : (g + 1) * half * rows], right[...], preferred_element_type=F32
        )
        for k in range(half):
            r = g * half + k
            at = slice(r * rows, (r + 1) * rows)
            d_scaled = d_scaled_half[k * rows : (k + 1) * rows]
            normed = normed_ref[at, :]
            product = d_scaled * normed
            gain_total = gain_total + jnp.sum(product.reshape(rows // 8, 8, width), axis=0)
            grad_in = d_scaled * gain
            mean_a = jnp.sum(grad_in, axis=-1, keepdims=True) * (1.0 / width)
            mean_b = jnp.sum(product * gain, axis=-1, keepdims=True) * (1.0 / width)
            inv = stats_ref[at, lanes // 2 : lanes // 2 + 1]
            result[r, 0:rows, :] = (inv * (grad_in - mean_a - normed * mean_b)).astype(BF16)
        at = pl.ds(g * half, half)
        copy = pltpu.make_async_copy(
            result.at[at, pl.ds(0, rows), :], out_ref.at[at, pl.ds(0, rows), :], sems.at[slots + 5 + g]
        )
        copy.start()
        sent.append(copy)
    probe_total = jnp.sum(tn_dot(d_scores, scaled).reshape(slots, heads, width), axis=0)
    gain_sum = jnp.sum(gain_total, axis=0, keepdims=True)
    loss = loss_ref[...]
    high = loss.astype(BF16).astype(F32)
    middle = (loss - high).astype(BF16).astype(F32)
    low = loss - high - middle
    pad = jnp.zeros((8, 256 - cut), F32)
    for p in range(slots):
        at = slice(p * cut, (p + 1) * cut)
        losses = jnp.concatenate(
            [high[p : p + 1], middle[p : p + 1], low[p : p + 1], jnp.zeros((5, 128), F32)], axis=0
        )
        misc = jnp.concatenate(
            [
                probe_total[0:8, at],
                pad,
                probe_total[8:16, at],
                pad,
                jnp.broadcast_to(gain_sum[:, at], (8, cut)),
                pad,
                losses,
                jnp.zeros((8, width - 896), F32),
            ],
            axis=1,
        )
        result[p, rows : rows + 16, :] = jnp.concatenate([d_context, misc], axis=0).astype(BF16)
    tail = pl.ds(rows, 16)
    copy = pltpu.make_async_copy(
        result.at[:, tail, :], out_ref.at[:, tail, :], sems.at[slots + 7]
    )
    copy.start()
    for copy in sent + [copy]:
        copy.wait()


def last_body(got_ref, a_ref, row_ref, value_ref, probe_ref, gain_ref, loss_ref, tail, sems, *, texts):
    loaders, got_rows, width = got_ref.shape
    rows = row_ref.shape[2]
    heads, images, cut = a_ref.shape
    head_width = width // heads
    first = pltpu.make_async_copy(got_ref.at[:, pl.ds(rows, 16), :], tail, sems.at[0])
    first.start()
    second = pltpu.make_async_copy(got_ref.at[:, pl.ds(0, rows), :], row_ref.at[0], sems.at[1])
    second.start()
    first.wait()
    tails = [tail[s].astype(F32) for s in range(loaders)]
    d_context = jnp.concatenate([t[0:8] for t in tails], axis=0)
    mask = head_mask(heads, width)
    tiles = [None] * (width // 128)
    for h in range(heads):
        low, high = h * head_width // 128, -(-(h + 1) * head_width // 128)
        lanes = slice(low * 128, high * 128)
        part = tn_dot(a_ref[h], (d_context[:, lanes] * mask[h : h + 1, lanes]).astype(BF16))
        for t in range(low, high):
            piece = part[:, (t - low) * 128 : (t - low + 1) * 128]
            tiles[t] = piece if tiles[t] is None else tiles[t] + piece
    value_ref[0] = jnp.concatenate(tiles, axis=1).astype(BF16)
    misc = tails[0][8:16]
    for s in range(1, loaders):
        misc = misc + tails[s][8:16]
    probe_ref[...] = jnp.concatenate([misc[:, 0:cut], misc[:, 256 : 256 + cut]], axis=0).astype(BF16)
    gain_ref[...] = misc[0:1, 512 : 512 + cut].astype(BF16)
    loss_ref[...] = (misc[0:1, 768:769] + misc[1:2, 768:769] + misc[2:3, 768:769]) / texts
    second.wait()


def local(
    patches, counts, owners, captions, norm_gain, key_probe, value_weight, logit_scale, logit_bias
):
    _, slots, rows, width = patches.shape
    heads = key_probe.shape[1]
    peers = lax.axis_size("fsdp")
    ranks = lax.axis_size("dp")
    cut = width // peers
    core = lax.axis_index("dp") % 2
    place = lax.axis_index("fsdp").astype(jnp.int32).reshape(1)
    scalars = jnp.concatenate([logit_scale, logit_bias])
    gain = norm_gain.reshape(1, width)
    probe = key_probe.T
    shape = jax.ShapeDtypeStruct
    dma = pltpu.SemaphoreType.DMA

    start = core * (cut - SEND_ROWS)
    part = lax.dynamic_slice_in_dim(value_weight, start, SEND_ROWS, axis=0)
    mine = lax.all_to_all(
        jnp.broadcast_to(part[None], (peers, SEND_ROWS, width)), "fsdp", 0, 0, tiled=True
    )

    lanes = slots * heads
    stats, weights, pooled = call(
        pool_body,
        [
            (shape((slots * rows, lanes), F32), vspec()),
            (shape((slots * rows, lanes), F32), vspec()),
            (shape((lanes, width), BF16), vspec()),
        ],
        [sspec(), sspec(), vspec(), vspec(), vspec()],
        40_000_000,
        4_000_000,
        [pltpu.VMEM((slots * rows, width), BF16)],
        name="pool",
    )(owners[0], counts[0], patches[0], gain, probe)

    caption_f = captions[0].astype(F32)
    caption_inv = lax.rsqrt(jnp.sum(caption_f * caption_f, axis=-1, keepdims=True) + epsilon)
    caption_unit = caption_f * caption_inv
    texts, pooled = lax.optimization_barrier((caption_unit.astype(BF16), pooled))
    for bit in [bit for bit in TEXT_BITS[:4] if bit < ranks]:
        texts = jnp.concatenate([texts, swapped(texts, bit)], axis=0)
    mine, texts = lax.optimization_barrier((mine, texts))
    other = swapped(mine, 1)
    for bit in [bit for bit in TEXT_BITS[4:] if bit < ranks]:
        texts = jnp.concatenate([texts, swapped(texts, bit)], axis=0)
    full, unit, inv_norm, sent = call(
        image_body,
        [
            (shape((width, width), BF16), hspec()),
            (shape((slots, width), F32), vspec()),
            (shape((slots, 128), F32), vspec()),
            (shape((peers, heads + slots, width), BF16), vspec()),
        ],
        [vspec()] * 3,
        400_000_000,
        6_000_000,
        [pltpu.VMEM((width, width), BF16), dma(())],
        name="image",
        limit=VMEM_LARGE,
    )(mine, other, pooled)
    got = lax.all_to_all(sent, "fsdp", 0, 0, tiled=True)
    half = ranks * slots // 2
    d_image_part, keep, send, loss_sums = call(
        pair_body,
        [
            (shape((peers, slots, width), BF16), vspec()),
            (shape((half, width), F32), vspec()),
            (shape((half, width), BF16), vspec()),
            (shape((slots, 128), F32), vspec()),
        ],
        [sspec(), sspec(), vspec(), vspec()],
        120_000_000,
        2_000_000,
        name="pair",
    )(place, scalars, got, texts)
    d_image_got = lax.all_to_all(d_image_part, "fsdp", 0, 0, tiled=True)

    def fold(total, bit):
        if bit >= ranks:
            return total
        rest = total.shape[0] // 2
        return total[:rest] + swapped(total[rest:].astype(BF16), bit).astype(F32)

    d_text = keep + swapped(send, TEXT_BITS[4]).astype(F32)
    d_text = fold(d_text, TEXT_BITS[3])
    d_image_got, d_text = lax.optimization_barrier((d_image_got, d_text))
    d_text = fold(d_text, TEXT_BITS[2])

    outgoing = call(
        back_body,
        [(shape((peers, rows + 16, width), BF16), hspec())],
        [sspec()] + [vspec()] * 3 + [hspec()] * 4 + [vspec()] * 3,
        500_000_000,
        8_000_000,
        [
            pltpu.VMEM((width, width), BF16),
            pltpu.VMEM((slots, rows, width), BF16),
            pltpu.VMEM((slots * rows, lanes), F32),
            pltpu.VMEM((slots * rows, lanes), F32),
            pltpu.VMEM((slots * rows, width), F32),
            pltpu.VMEM((slots * rows, width), BF16),
            pltpu.VMEM((2 * lanes, width), BF16),
            pltpu.VMEM((peers, rows + 16, width), BF16),
            dma((slots + 8,)),
        ],
        name="back",
        limit=VMEM_LARGE,
    )(
        owners[0], d_image_got, unit, inv_norm, full, patches, stats, weights, probe, gain, loss_sums
    )[0]
    outgoing, d_text = lax.optimization_barrier((outgoing, d_text))
    arrived = lax.all_to_all(outgoing, "fsdp", 0, 0, tiled=True)
    d_caption = fold(fold(d_text, TEXT_BITS[1]), TEXT_BITS[0])

    pooled_got = (
        got[:, :heads]
        .reshape(peers, heads, slots, cut)
        .transpose(1, 0, 2, 3)
        .reshape(heads, peers * slots, cut)
    )
    batch = ranks * peers * slots

    def last(*refs):
        last_body(*refs, texts=batch)

    row_grad, value_grad, probe_t, gain_grad, loss_part = call(
        last,
        [
            (shape((1, slots, rows, width), BF16), hspec()),
            (shape((1, cut, width), BF16), vspec()),
            (shape((heads, cut), BF16), vspec()),
            (shape((1, cut), BF16), vspec()),
            (shape((1, 1), F32), vspec()),
        ],
        [hspec(), vspec()],
        400_000_000,
        3_000_000,
        [pltpu.VMEM((peers, 16, width), BF16), dma((2,))],
        name="last",
    )(arrived, pooled_got)

    text_grad = (
        (d_caption - caption_unit * jnp.sum(d_caption * caption_unit, axis=-1, keepdims=True))
        * caption_inv
    ).astype(BF16)
    return (loss_part, row_grad, text_grad[None], value_grad, probe_t.T[None], gain_grad)


def solution(mesh):
    placed = (
        P(("dp", "fsdp"), None, None, None),
        P(("dp", "fsdp"), None),
        P(("dp", "fsdp"), None),
        P(("dp", "fsdp"), None, None),
        P(),
        P(),
        P("fsdp", None),
        P(),
        P(),
    )
    return jax.shard_map(
        local,
        mesh=mesh,
        in_specs=placed,
        out_specs=(
            P("dp", "fsdp"),
            P(("dp", "fsdp"), None, None, None),
            P(("dp", "fsdp"), None, None),
            P("dp", "fsdp", None),
            P("dp", "fsdp", None),
            P("dp", "fsdp"),
        ),
        check_vma=False,
    )
```

time: 162 us -> 115 us (0.71)
  blocking collectives: 81.5 us -> 0 us
  starting transfers between devices: 12.5 us -> 43 us
  waiting for transfers between devices: 24 us -> 44.6 us
  local copies, waits for them, and re-layouts: 23.2 us -> 6.35 us
    all_to_all x2 -> x0, blocking collectives: 42.5 us -> none  [the longest x1 27.9 us: local(): lax.all_to_all(jnp.broadcast_to(part[None], (peers, SEND_ROWS, width)), '...]
    all_gather x1 -> x0, blocking collectives: 39 us -> none  [local(): texts = lax.all_gather(caption_unit.astype(BF16), 'dp', axis=0, tiled=True)]
    ppermute x1 -> x11, starting transfers between devices: 0.01 us -> 22.7 us  [swapped(): lax.ppermute(block, 'dp', [(i, i ^ bit) for i in range(lax.axis_size('dp'...]
    ppermute x1 -> x11, waiting for transfers between devices: 0.01 us -> 19.4 us  [swapped(): lax.ppermute(block, 'dp', [(i, i ^ bit) for i in range(lax.axis_size('dp'...]
    all_to_all x1, waiting for transfers between devices: 0.01 us -> 9.58 us  [local(): got = lax.all_to_all(sent, 'fsdp', 0, 0, tiled=True)]
    unnamed x42 -> x34, local copies, waits for them, and re-layouts: 13.7 us -> 4.27 us
    reshape x3 -> x0, local copies, waits for them, and re-layouts: 6.83 us -> none  [the longest x2 4.59 us: local(): pooled.reshape(slots, heads, peers, cut).transpose(2, 1, 0, 3)]
    all_to_all x1, waiting for transfers between devices: 13.8 us -> 8.51 us  [local(): arrived = lax.all_to_all(outgoing, 'fsdp', 0, 0, tiled=True)]
  transfers between devices with their start and end apart: 4 -> 15, of which waited for: 2 -> 11; matrix products, arithmetic and copies ran while one was open for 7% -> 2% of each run, Pallas kernels for 6% -> 12%
where the time goes in v2:
time: 115 us; the launch traced here: 114 us
  waiting for transfers between devices  44.6 us (39%)
  starting transfers between devices  43 us (37%)
  Pallas kernels  16.8 us (15%)
  local copies, waits for them, and re-layouts  6.35 us (6%)
  between operations  2.23 us (2%)
  other arithmetic  1.35 us (1%)
    ppermute x11, starting transfers between devices, swapped(): lax.ppermute(block, 'dp', [(i, i ^ bit) for i in range(lax.axis_size('dp'...  22.7 us
    ppermute x11, waiting for transfers between devices, swapped(): lax.ppermute(block, 'dp', [(i, i ^ bit) for i in range(lax.axis_size('dp'...  19.4 us
    all_to_all x1, waiting for transfers between devices, local(): got = lax.all_to_all(sent, 'fsdp', 0, 0, tiled=True)  9.58 us
    all_to_all x1, waiting for transfers between devices, local(): arrived = lax.all_to_all(outgoing, 'fsdp', 0, 0, tiled=True)  8.51 us
    all_to_all x1, starting transfers between devices, local(): got = lax.all_to_all(sent, 'fsdp', 0, 0, tiled=True)  7.22 us
    all_to_all x1, waiting for transfers between devices, local(): d_image_got = lax.all_to_all(d_image_part, 'fsdp', 0, 0, tiled=True)  7.08 us
    pallas_call x1, Pallas kernels, local(): call(back_body, [(shape((peers, rows + 16, width), BF16), hspec())], [ssp...  6.74 us
    all_to_all x1, starting transfers between devices, local(): lax.all_to_all(jnp.broadcast_to(part[None], (peers, SEND_ROWS, width)), '...  6.18 us
  transfers between devices with their start and end apart: 15, of which 11 were waited for; matrix products, arithmetic and copies ran while one was open for 2% of the time, Pallas kernels for 12%

profile of v2, /device:TPU:2, one launch (start us, length us, event | category | flops | bytes accessed | tf_op | source)
XLA Modules:
  0.0 114.3 jit_solution(6875887276242928120)
XLA Ops:
  2.9 6.2 %all-to-all-start = ((bf16[8,80,1152]{2,1,0:T(8,128)(2,1)}), bf16[8,80,1152]{2,1,0:T(8,128)(2,1)S(1)}, u32[]{:S(2)}, u32[]{:S(2)}) async-start(bf16[8,80,1152]{2,1,0:T(8,128)(2,1)} %broadcast_in_dim.6), calls=%async_computation | async-start | bytes 2949120 | tf_op jit(solution)/shard_map/all_to_all | solution.py:343
  9.4 2.1 %pool.1 = (f32[384,128]{1,0:T(8,128)S(1)}, f32[384,128]{1,0:T(8,128)S(1)}, bf16[128,1152]{1,0:T(8,128)(2,1)S(1)}) custom-call(s32[8]{0:T(128)S(1)} %bitcast.26, s32[8]{0:T(128)S(1)} %bitcast.27, bf16[8,48,1152]{2,1,0:T(8,128)(2,1)S(1)} %bitcast.21, f32[1,1152]{1,0:T(1,128)S(1)} %reshape.35.gain_ref, bf16[16,1152]{1,0:T(8,128)(2,1)S(1)} %bitcast.24), custom_call_target="tpu_custom_call" | custom-call | flops 40000000 | bytes 4000000 | tf_op jit(solution)/shard_map/pool/pallas_call | solution.py:348
  13.6 7.2 %collective-permute-start = (bf16[8,1152]{1,0:T(8,128)(2,1)S(1)}, bf16[8,1152]{1,0:T(8,128)(2,1)S(1)}, u32[]{:S(2)}, u32[]{:S(2)}) collective-permute-start(bf16[8,1152]{1,0:T(8,128)(2,1)S(1)} %fusion.2), channel_id=1, source_target_pairs={{0,64},{8,72},{16,80},{24,88},{32,96},{40,104},{48,112},{56,120},{... | collective-permute-start | bytes 55304 | tf_op jit(solution)/shard_map/ppermute | solution.py:23
  20.8 1.7 %collective-permute-done = bf16[8,1152]{1,0:T(8,128)(2,1)S(1)} collective-permute-done((bf16[8,1152]{1,0:T(8,128)(2,1)S(1)}, bf16[8,1152]{1,0:T(8,128)(2,1)S(1)}, u32[]{:S(2)}, u32[]{:S(2)}) %collective-permute-start) | collective-permute-done | bytes 18464 | tf_op jit(solution)/shard_map/ppermute | solution.py:23
  22.5 2.0 %collective-permute-start.1 = (bf16[16,1152]{1,0:T(8,128)(2,1)S(1)}, bf16[16,1152]{1,0:T(8,128)(2,1)S(1)}, u32[]{:S(2)}, u32[]{:S(2)}) collective-permute-start(bf16[16,1152]{1,0:T(8,128)(2,1)S(1)} %pad_maximum_fusion.3), channel_id=1, source_target_pairs={{0,32},{8,40},{16,48},{24,56},{32,0},{40,8},{48,16},{56,24},{64,96... | collective-permute-start | bytes 110600 | tf_op jit(solution)/shard_map/ppermute | solution.py:23
  24.6 2.8 %collective-permute-done.1 = bf16[16,1152]{1,0:T(8,128)(2,1)S(1)} collective-permute-done((bf16[16,1152]{1,0:T(8,128)(2,1)S(1)}, bf16[16,1152]{1,0:T(8,128)(2,1)S(1)}, u32[]{:S(2)}, u32[]{:S(2)}) %collective-permute-start.1) | collective-permute-done | bytes 36896 | tf_op jit(solution)/shard_map/ppermute | solution.py:23
  28.5 3.3 %collective-permute-done.2 = bf16[32,1152]{1,0:T(8,128)(2,1)S(1)} collective-permute-done((bf16[32,1152]{1,0:T(8,128)(2,1)S(1)}, bf16[32,1152]{1,0:T(8,128)(2,1)S(1)}, u32[]{:S(2)}, u32[]{:S(2)}) %collective-permute-start.2) | collective-permute-done | bytes 73760 | tf_op jit(solution)/shard_map/ppermute | solution.py:23
  31.8 1.5 %collective-permute-start.3 = (bf16[64,1152]{1,0:T(8,128)(2,1)S(1)}, bf16[64,1152]{1,0:T(8,128)(2,1)S(1)}, u32[]{:S(2)}, u32[]{:S(2)}) collective-permute-start(bf16[64,1152]{1,0:T(8,128)(2,1)S(1)} %pad_maximum_fusion.1), channel_id=1, source_target_pairs={{0,128},{8,136},{16,144},{24,152},{32,160},{40,168},{48,176},{56,1... | collective-permute-start | bytes 442376 | tf_op jit(solution)/shard_map/ppermute | solution.py:23
  33.3 3.7 %collective-permute-done.3 = bf16[64,1152]{1,0:T(8,128)(2,1)S(1)} collective-permute-done((bf16[64,1152]{1,0:T(8,128)(2,1)S(1)}, bf16[64,1152]{1,0:T(8,128)(2,1)S(1)}, u32[]{:S(2)}, u32[]{:S(2)}) %collective-permute-start.3) | collective-permute-done | bytes 147488 | tf_op jit(solution)/shard_map/ppermute | solution.py:23
  37.6 2.8 %collective-permute-done.4.other_ref = bf16[8,80,1152]{2,1,0:T(8,128)(2,1)S(1)} collective-permute-done((bf16[8,80,1152]{2,1,0:T(8,128)(2,1)S(1)}, bf16[8,80,1152]{2,1,0:T(8,128)(2,1)S(1)}, u32[]{:S(2)}, u32[]{:S(2)}) %collective-permute-start.4) | collective-permute-done | bytes 1474592 | tf_op jit(solution)/shard_map/ppermute | solution.py:23
  41.6 4.3 %image.1 = (bf16[1152,1152]{1,0:T(8,128)(2,1)}, f32[8,1152]{1,0:T(8,128)}, f32[8,128]{1,0:T(8,128)}, bf16[8,24,1152]{2,1,0:T(8,128)(2,1)}) custom-call(bf16[8,80,1152]{2,1,0:T(8,128)(2,1)} %copy-done.10, bf16[8,80,1152]{2,1,0:T(8,128)(2,1)} %copy-done.11, bf16[128,1152]{1,0:T(8,128)(2,1)} %copy-done.2), custom_call_target="tpu_custom_call" | custom-call | flops 400000000 | bytes 6000000 | tf_op jit(solution)/shard_map/image/pallas_call | solution.py:372
  45.9 7.2 %all-to-all-start.1 = ((bf16[8,24,1152]{2,1,0:T(8,128)(2,1)}), bf16[8,24,1152]{2,1,0:T(8,128)(2,1)S(1)}, u32[]{:S(2)}, u32[]{:S(2)}) async-start(bf16[8,24,1152]{2,1,0:T(8,128)(2,1)} %get-tuple-element.34), calls=%async_computation.1 | async-start | bytes 884736 | tf_op jit(solution)/shard_map/all_to_all | solution.py:387
  54.6 9.6 %all-to-all-done.1.got_ref = bf16[8,24,1152]{2,1,0:T(8,128)(2,1)S(1)} async-done(((bf16[8,24,1152]{2,1,0:T(8,128)(2,1)}), bf16[8,24,1152]{2,1,0:T(8,128)(2,1)S(1)}, u32[]{:S(2)}, u32[]{:S(2)}) %all-to-all-start.1) | async-done | bytes 442400 | tf_op jit(solution)/shard_map/all_to_all | solution.py:387
  64.2 1.9 %pair.1 = (bf16[8,8,1152]{2,1,0:T(8,128)(2,1)}, f32[128,1152]{1,0:T(8,128)S(1)}, bf16[128,1152]{1,0:T(8,128)(2,1)S(1)}, f32[8,128]{1,0:T(8,128)S(1)}) custom-call(s32[1]{0:T(128)} %bitcast.1.place, f32[2]{0:T(128)S(1)} %pad_maximum_fusion.4.scalars, bf16[8,24,1152]{2,1,0:T(8,128)(2,1)S(1)} %all-to-all-done.1.got_ref, ...), custom_call_target="tpu_custom_call" | custom-call | flops 120000000 | bytes 2000000 | tf_op jit(solution)/shard_map/pair/pallas_call | solution.py:389
  66.1 1.6 %collective-permute-done.6 = bf16[128,1152]{1,0:T(8,128)(2,1)S(1)} collective-permute-done((bf16[128,1152]{1,0:T(8,128)(2,1)S(1)}, bf16[128,1152]{1,0:T(8,128)(2,1)S(1)}, u32[]{:S(2)}, u32[]{:S(2)}) %collective-permute-start.6) | collective-permute-done | bytes 294944 | tf_op jit(solution)/shard_map/ppermute | solution.py:23
  69.3 3.4 %all-to-all-start.2 = ((bf16[8,8,1152]{2,1,0:T(8,128)(2,1)}), bf16[8,8,1152]{2,1,0:T(8,128)(2,1)S(1)}, u32[]{:S(2)}, u32[]{:S(2)}) async-start(bf16[8,8,1152]{2,1,0:T(8,128)(2,1)} %get-tuple-element.36), calls=%async_computation.2 | async-start | bytes 294912 | tf_op jit(solution)/shard_map/all_to_all | solution.py:402
  73.8 7.1 %all-to-all-done.2.got_ref = bf16[8,8,1152]{2,1,0:T(8,128)(2,1)S(1)} async-done(((bf16[8,8,1152]{2,1,0:T(8,128)(2,1)}), bf16[8,8,1152]{2,1,0:T(8,128)(2,1)S(1)}, u32[]{:S(2)}, u32[]{:S(2)}) %all-to-all-start.2) | async-done | bytes 147488 | tf_op jit(solution)/shard_map/all_to_all | solution.py:402
  82.0 6.7 %back.1 = bf16[8,64,1152]{2,1,0:T(8,128)(2,1)} custom-call(s32[8]{0:T(128)} %bitcast.25, bf16[8,8,1152]{2,1,0:T(8,128)(2,1)} %copy-done.12, f32[8,1152]{1,0:T(8,128)} %get-tuple-element.40.unit_ref, f32[8,128]{1,0:T(8,128)} %get-tuple-element.41.invn_ref, bf16[1152,1152]{1,0:T(8,128)(2,1)} %get-tuple-element.42.full_in, bf16[1,8,48,1152]{3,2,1,0:T(8,128)(2,1)} %x_in.1, ...), custom_call_target="tpu_custom_call" | custom-call | flops 500000000 | bytes 8000000 | tf_op jit(solution)/shard_map/back/pallas_call | solution.py:415
  88.8 3.1 %collective-permute-start.9 = (bf16[16,1152]{1,0:T(8,128)(2,1)S(1)}, bf16[16,1152]{1,0:T(8,128)(2,1)S(1)}, u32[]{:S(2)}, u32[]{:S(2)}) collective-permute-start(bf16[16,1152]{1,0:T(8,128)(2,1)S(1)} %slice.63), channel_id=1, source_target_pairs={{0,32},{8,40},{16,48},{24,56},{32,0},{40,8},{48,16},{56,24},{64,96... | collective-permute-start | bytes 110600 | tf_op jit(solution)/shard_map/ppermute | solution.py:23
  91.9 3.6 %all-to-all-start.3 = ((bf16[8,64,1152]{2,1,0:T(8,128)(2,1)}), bf16[8,64,1152]{2,1,0:T(8,128)(2,1)S(1)}, u32[]{:S(2)}, u32[]{:S(2)}) async-start(bf16[8,64,1152]{2,1,0:T(8,128)(2,1)} %back.1), calls=%async_computation.3 | async-start | bytes 2359296 | tf_op jit(solution)/shard_map/all_to_all | solution.py:438
  95.5 4.6 %collective-permute-start.10 = (bf16[8,1152]{1,0:T(8,128)(2,1)S(1)}, bf16[8,1152]{1,0:T(8,128)(2,1)S(1)}, u32[]{:S(2)}, u32[]{:S(2)}) collective-permute-start(bf16[8,1152]{1,0:T(8,128)(2,1)S(1)} %slice.64), channel_id=1, source_target_pairs={{0,64},{8,72},{16,80},{24,88},{32,96},{40,104},{48,112},{56,120},{... | collective-permute-start | bytes 55304 | tf_op jit(solution)/shard_map/ppermute | solution.py:23
  100.8 2.4 %collective-permute-done.10 = bf16[8,1152]{1,0:T(8,128)(2,1)S(1)} collective-permute-done((bf16[8,1152]{1,0:T(8,128)(2,1)S(1)}, bf16[8,1152]{1,0:T(8,128)(2,1)S(1)}, u32[]{:S(2)}, u32[]{:S(2)}) %collective-permute-start.10) | collective-permute-done | bytes 18464 | tf_op jit(solution)/shard_map/ppermute | solution.py:23
  104.1 8.5 %all-to-all-done.3.refs_0_ = bf16[8,64,1152]{2,1,0:T(8,128)(2,1)S(1)} async-done(((bf16[8,64,1152]{2,1,0:T(8,128)(2,1)}), bf16[8,64,1152]{2,1,0:T(8,128)(2,1)S(1)}, u32[]{:S(2)}, u32[]{:S(2)}) %all-to-all-start.3) | async-done | bytes 1179680 | tf_op jit(solution)/shard_map/all_to_all | solution.py:438
  112.6 1.7 %last.1 = (bf16[1,8,48,1152]{3,2,1,0:T(8,128)(2,1)}, bf16[1,144,1152]{2,1,0:T(8,128)(2,1)}, bf16[16,144]{1,0:T(8,128)(2,1)}, bf16[1,144]{1,0:T(2,128)(2,1)}, f32[1,1]{1,0:T(1,128)}) custom-call(bf16[8,64,1152]{2,1,0:T(8,128)(2,1)S(1)} %all-to-all-done.3.refs_0_, bf16[16,64,144]{2,1,0:T(8,128)(2,1)S(1)} %bitcast.22), custom_call_target="tpu_custom_call" | custom-call | flops 400000000 | bytes 3000000 | tf_op jit(solution)/shard_map/last/pallas_call | solution.py:452
  (70 shorter events, 13.0 us)
Async XLA Ops:
  2.9 6.2 %copy-start.13 = (bf16[1,8,1152]{2,1,0:T(8,128)(2,1)S(1)}, bf16[1,8,1152]{2,1,0:T(8,128)(2,1)}, u32[]{:S(2)}) copy-start(bf16[1,8,1152]{2,1,0:T(8,128)(2,1)} %param.12) | copy-start | bytes 55300
  2.9 6.4 %copy-start.14 = (f32[1152]{0:T(1024)S(1)}, f32[1152]{0:T(1024)}, u32[]{:S(2)}) copy-start(f32[1152]{0:T(1024)} %param.13) | copy-start | bytes 13828
  2.9 6.5 %copy-start.1 = (bf16[1,8,48,1152]{3,2,1,0:T(8,128)(2,1)S(1)}, bf16[1,8,48,1152]{3,2,1,0:T(8,128)(2,1)}, u32[]{:S(2)}) copy-start(bf16[1,8,48,1152]{3,2,1,0:T(8,128)(2,1)} %x_in.1) | copy-start | bytes 2654212
  2.9 6.5 %copy-start.5 = (bf16[1152,16]{0,1:T(8,128)(2,1)S(1)}, bf16[1152,16]{0,1:T(8,128)(2,1)}, u32[]{:S(2)}) copy-start(bf16[1152,16]{0,1:T(8,128)(2,1)} %param.14) | copy-start | bytes 110596
  2.9 6.5 %copy-start.8 = (s32[1,8]{1,0:T(1,128)S(1)}, s32[1,8]{1,0:T(1,128)}, u32[]{:S(2)}) copy-start(s32[1,8]{1,0:T(1,128)} %param.11) | copy-start | bytes 100
  2.9 6.5 %copy-start.9 = (s32[1,8]{1,0:T(1,128)S(1)}, s32[1,8]{1,0:T(1,128)}, u32[]{:S(2)}) copy-start(s32[1,8]{1,0:T(1,128)} %param.10) | copy-start | bytes 100
  2.9 34.1 %all-to-all-start = ((bf16[8,80,1152]{2,1,0:T(8,128)(2,1)}), bf16[8,80,1152]{2,1,0:T(8,128)(2,1)S(1)}, u32[]{:S(2)}, u32[]{:S(2)}) async-start(bf16[8,80,1152]{2,1,0:T(8,128)(2,1)} %broadcast_in_dim.6), calls=%async_computation | async-start | bytes 2949120 | tf_op jit(solution)/shard_map/all_to_all | solution.py:343
  9.3 36.6 %copy-start.6 = (f32[1,1152]{1,0:T(1,128)}, f32[1,1152]{1,0:T(1,128)S(1)}, u32[]{:S(2)}) copy-start(f32[1,1152]{1,0:T(1,128)S(1)} %reshape.35.gain_ref) | copy-start | bytes 13828
  13.6 8.9 %collective-permute-start = (bf16[8,1152]{1,0:T(8,128)(2,1)S(1)}, bf16[8,1152]{1,0:T(8,128)(2,1)S(1)}, u32[]{:S(2)}, u32[]{:S(2)}) collective-permute-start(bf16[8,1152]{1,0:T(8,128)(2,1)S(1)} %fusion.2), channel_id=1, source_target_pairs={{0,64},{8,72},{16,80},{24,88},{32,96},{40,104},{48,112},{56,120},{... | collective-permute-start | bytes 55304 | tf_op jit(solution)/shard_map/ppermute | solution.py:23
  22.5 4.9 %collective-permute-start.1 = (bf16[16,1152]{1,0:T(8,128)(2,1)S(1)}, bf16[16,1152]{1,0:T(8,128)(2,1)S(1)}, u32[]{:S(2)}, u32[]{:S(2)}) collective-permute-start(bf16[16,1152]{1,0:T(8,128)(2,1)S(1)} %pad_maximum_fusion.3), channel_id=1, source_target_pairs={{0,32},{8,40},{16,48},{24,56},{32,0},{40,8},{48,16},{56,24},{64,96... | collective-permute-start | bytes 110600 | tf_op jit(solution)/shard_map/ppermute | solution.py:23
  27.4 4.4 %collective-permute-start.2 = (bf16[32,1152]{1,0:T(8,128)(2,1)S(1)}, bf16[32,1152]{1,0:T(8,128)(2,1)S(1)}, u32[]{:S(2)}, u32[]{:S(2)}) collective-permute-start(bf16[32,1152]{1,0:T(8,128)(2,1)S(1)} %pad_maximum_fusion.2), channel_id=1, source_target_pairs={{0,16},{8,24},{16,0},{24,8},{32,48},{40,56},{48,32},{56,40},{64,80... | collective-permute-start | bytes 221192 | tf_op jit(solution)/shard_map/ppermute | solution.py:23
  31.8 5.2 %collective-permute-start.3 = (bf16[64,1152]{1,0:T(8,128)(2,1)S(1)}, bf16[64,1152]{1,0:T(8,128)(2,1)S(1)}, u32[]{:S(2)}, u32[]{:S(2)}) collective-permute-start(bf16[64,1152]{1,0:T(8,128)(2,1)S(1)} %pad_maximum_fusion.1), channel_id=1, source_target_pairs={{0,128},{8,136},{16,144},{24,152},{32,160},{40,168},{48,176},{56,1... | collective-permute-start | bytes 442376 | tf_op jit(solution)/shard_map/ppermute | solution.py:23
  37.0 3.4 %copy-start.10 = (bf16[8,80,1152]{2,1,0:T(8,128)(2,1)}, bf16[8,80,1152]{2,1,0:T(8,128)(2,1)S(1)}, u32[]{:S(2)}) copy-start(bf16[8,80,1152]{2,1,0:T(8,128)(2,1)S(1)} %all-to-all-done.mine_ref) | copy-start | bytes 4423684
  37.1 3.4 %collective-permute-start.4 = (bf16[8,80,1152]{2,1,0:T(8,128)(2,1)S(1)}, bf16[8,80,1152]{2,1,0:T(8,128)(2,1)S(1)}, u32[]{:S(2)}, u32[]{:S(2)}) collective-permute-start(bf16[8,80,1152]{2,1,0:T(8,128)(2,1)S(1)} %all-to-all-done.mine_ref), channel_id=1, source_target_pairs={{0,8},{8,0},{16,24},{24,16},{32,40},{40,32},{48,56},{56,48},{64,72... | collective-permute-start | bytes 4423688 | tf_op jit(solution)/shard_map/ppermute | solution.py:23
  37.2 17.4 %collective-permute-start.5 = (bf16[128,1152]{1,0:T(8,128)(2,1)S(1)}, bf16[128,1152]{1,0:T(8,128)(2,1)S(1)}, u32[]{:S(2)}, u32[]{:S(2)}) collective-permute-start(bf16[128,1152]{1,0:T(8,128)(2,1)S(1)} %constant_dynamic-update-slice_fusion), channel_id=1, source_target_pairs={{0,8},{8,0},{16,24},{24,16},{32,40},{40,32},{48,56},{56,48},{64,72... | collective-permute-start | bytes 884744 | tf_op jit(solution)/shard_map/ppermute | solution.py:23
  45.9 18.2 %all-to-all-start.1 = ((bf16[8,24,1152]{2,1,0:T(8,128)(2,1)}), bf16[8,24,1152]{2,1,0:T(8,128)(2,1)S(1)}, u32[]{:S(2)}, u32[]{:S(2)}) async-start(bf16[8,24,1152]{2,1,0:T(8,128)(2,1)} %get-tuple-element.34), calls=%async_computation.1 | async-start | bytes 884736 | tf_op jit(solution)/shard_map/all_to_all | solution.py:387
  66.1 7.7 %copy-start.7 = (f32[8,128]{1,0:T(8,128)}, f32[8,128]{1,0:T(8,128)S(1)}, u32[]{:S(2)}) copy-start(f32[8,128]{1,0:T(8,128)S(1)} %get-tuple-element.45.loss_ref) | copy-start | bytes 12292
  66.1 1.6 %collective-permute-start.6 = (bf16[128,1152]{1,0:T(8,128)(2,1)S(1)}, bf16[128,1152]{1,0:T(8,128)(2,1)S(1)}, u32[]{:S(2)}, u32[]{:S(2)}) collective-permute-start(bf16[128,1152]{1,0:T(8,128)(2,1)S(1)} %get-tuple-element.38), channel_id=1, source_target_pairs={{0,8},{8,0},{16,24},{24,16},{32,40},{40,32},{48,56},{56,48},{64,72... | collective-permute-start | bytes 884744 | tf_op jit(solution)/shard_map/ppermute | solution.py:23
  67.8 6.0 %collective-permute-start.7 = (bf16[64,1152]{1,0:T(8,128)(2,1)S(1)}, bf16[64,1152]{1,0:T(8,128)(2,1)S(1)}, u32[]{:S(2)}, u32[]{:S(2)}) collective-permute-start(bf16[64,1152]{1,0:T(8,128)(2,1)S(1)} %slice.61), channel_id=1, source_target_pairs={{0,128},{8,136},{16,144},{24,152},{32,160},{40,168},{48,176},{56,1... | collective-permute-start | bytes 442376 | tf_op jit(solution)/shard_map/ppermute | solution.py:23
  69.3 11.6 %all-to-all-start.2 = ((bf16[8,8,1152]{2,1,0:T(8,128)(2,1)}), bf16[8,8,1152]{2,1,0:T(8,128)(2,1)S(1)}, u32[]{:S(2)}, u32[]{:S(2)}) async-start(bf16[8,8,1152]{2,1,0:T(8,128)(2,1)} %get-tuple-element.36), calls=%async_computation.2 | async-start | bytes 294912 | tf_op jit(solution)/shard_map/all_to_all | solution.py:402
  80.9 7.9 %collective-permute-start.8 = (bf16[32,1152]{1,0:T(8,128)(2,1)S(1)}, bf16[32,1152]{1,0:T(8,128)(2,1)S(1)}, u32[]{:S(2)}, u32[]{:S(2)}) collective-permute-start(bf16[32,1152]{1,0:T(8,128)(2,1)S(1)} %slice.62), channel_id=1, source_target_pairs={{0,16},{8,24},{16,0},{24,8},{32,48},{40,56},{48,32},{56,40},{64,80... | collective-permute-start | bytes 221192 | tf_op jit(solution)/shard_map/ppermute | solution.py:23
  88.8 6.7 %collective-permute-start.9 = (bf16[16,1152]{1,0:T(8,128)(2,1)S(1)}, bf16[16,1152]{1,0:T(8,128)(2,1)S(1)}, u32[]{:S(2)}, u32[]{:S(2)}) collective-permute-start(bf16[16,1152]{1,0:T(8,128)(2,1)S(1)} %slice.63), channel_id=1, source_target_pairs={{0,32},{8,40},{16,48},{24,56},{32,0},{40,8},{48,16},{56,24},{64,96... | collective-permute-start | bytes 110600 | tf_op jit(solution)/shard_map/ppermute | solution.py:23
  91.9 20.8 %all-to-all-start.3 = ((bf16[8,64,1152]{2,1,0:T(8,128)(2,1)}), bf16[8,64,1152]{2,1,0:T(8,128)(2,1)S(1)}, u32[]{:S(2)}, u32[]{:S(2)}) async-start(bf16[8,64,1152]{2,1,0:T(8,128)(2,1)} %back.1), calls=%async_computation.3 | async-start | bytes 2359296 | tf_op jit(solution)/shard_map/all_to_all | solution.py:438
  95.5 7.8 %collective-permute-start.10 = (bf16[8,1152]{1,0:T(8,128)(2,1)S(1)}, bf16[8,1152]{1,0:T(8,128)(2,1)S(1)}, u32[]{:S(2)}, u32[]{:S(2)}) collective-permute-start(bf16[8,1152]{1,0:T(8,128)(2,1)S(1)} %slice.64), channel_id=1, source_target_pairs={{0,64},{8,72},{16,80},{24,88},{32,96},{40,104},{48,112},{56,120},{... | collective-permute-start | bytes 55304 | tf_op jit(solution)/shard_map/ppermute | solution.py:23
  (6 other events, 5.4 us)

commit v3 on v2

--- a/solution.py
+++ b/solution.py
@@ -12,11 +12,14 @@
 BF16 = jnp.bfloat16
 
 VMEM_LIMIT = 16 * 1024 * 1024
-VMEM_LARGE = 60_180_000
-SEND_ROWS = 80
-
-
-TEXT_BITS = (8, 4, 2, 16, 1)
+VMEM_LARGE = 60_000_000
+VMEM_IMAGE = 28_000_000
+STASH_ROWS = 15_616
+SEND_ROWS = 72
+
+
+Z_BITS = (8, 4, 12)
+NEXT_BIT, SIDE_BIT, CORE_BIT = 2, 16, 1
 
 
 def swapped(block, bit):
@@ -124,7 +127,7 @@
     def _():
         put(other_ref, mine_ref)
 
-    copy = pltpu.make_async_copy(full, full_out, sem)
+    copy = pltpu.make_async_copy(full, full_out.at[pl.ds(0, width), :], sem)
     copy.start()
     pooled = a_ref[...]
     wide = jnp.dot(pooled, full[...], preferred_element_type=F32).reshape(slots, heads, width)
@@ -146,12 +149,22 @@
     copy.wait()
 
 
-def pair_body(place, scalars, got_ref, text_ref, d_image_ref, keep_ref, send_ref, loss_ref):
+def caption_body(caption_ref, unit_ref, inv_ref, text_ref):
+    caption = caption_ref[...].astype(F32)
+    inv = lax.rsqrt(jnp.sum(caption * caption, axis=-1, keepdims=True) + epsilon)
+    unit = caption * inv
+    unit_ref[...] = unit
+    inv_ref[...] = jnp.broadcast_to(inv, inv_ref.shape)
+    text_ref[...] = unit.astype(BF16)
+
+
+def pair_body(place, scalars, got_ref, text_ref, d_image_ref, coefficient_ref, image_ref, loss_ref):
     loaders, got_rows, width = got_ref.shape
     slots = d_image_ref.shape[1]
     images = jnp.concatenate(
         [got_ref[s].astype(F32)[got_rows - slots :] for s in range(loaders)], axis=0
     ).astype(BF16)
+    image_ref[...] = images
     texts = text_ref[...]
     count = images.shape[0]
     text_count = texts.shape[0]
@@ -167,19 +180,40 @@
     losses = jnp.maximum(signed, 0.0) + jnp.log1p(decay)
     sigmoid = jnp.where(logits >= 0.0, 1.0, decay) / (1.0 + decay)
     coefficient = (scale * (sigmoid - matched)).astype(BF16)
+    coefficient_ref[...] = coefficient
     d_image = jnp.dot(coefficient, texts, preferred_element_type=F32)
     d_image_ref[...] = d_image.reshape(d_image_ref.shape).astype(BF16)
-    d_text = tn_dot(coefficient, images)
-    keep_ref[...] = d_text[: text_count // 2]
-    send_ref[...] = d_text[text_count // 2 :].astype(BF16)
     per_image = jnp.sum(losses, axis=-1, keepdims=True)
     per_owner = jnp.sum(per_image.reshape(loaders, slots, 1), axis=0)
     loss_ref[...] = jnp.broadcast_to(per_owner, loss_ref.shape)
 
 
+def text_body(coefficient_ref, image_ref, keep_ref, send_ref):
+    d_text = tn_dot(coefficient_ref[...], image_ref[...])
+    half = keep_ref.shape[0]
+    keep_ref[...] = d_text[:half]
+    send_ref[...] = d_text[half:].astype(BF16)
+
+
+def fold_body(total_ref, got_ref, keep_ref, send_ref):
+    total = total_ref[...] + got_ref[...].astype(F32)
+    half = keep_ref.shape[0]
+    keep_ref[...] = total[:half]
+    send_ref[...] = total[half:].astype(BF16)
+
+
+def split_body(total_ref, got_ref, keep_ref, *block_refs):
+    total = total_ref[...] + got_ref[...].astype(F32)
+    rows = keep_ref.shape[0]
+    keep_ref[...] = total[:rows]
+    for k, block_ref in enumerate(block_refs):
+        block_ref[...] = total[(k + 1) * rows : (k + 2) * rows].astype(BF16)
+
+
 def back_body(
-    owners, got_ref, unit_ref, invn_ref, full_in, x_in, stats_in, w_in, probe_ref, gain_ref, loss_ref,
-    out_ref, full, x_ref, stats_ref, w_ref, normed_ref, scaled_ref, right, result, sems,
+    owners, got_in, unit_in, invn_in, full_in, x_in, stats_in, w_in, probe_in, gain_in, loss_in,
+    out_ref, got_ref, unit_ref, invn_ref, probe_ref, gain_ref, loss_ref,
+    full, x_ref, stats_ref, w_ref, normed_ref, scaled_ref, right, result, sems, extra_sems,
 ):
     slots, rows, width = x_ref.shape
     heads = probe_ref.shape[0]
@@ -203,14 +237,30 @@
         )
         for c in range(3)
     ]
-    for copy in small[:1] + patches + values + small[1:]:
+    pairs = [
+        (got_in, got_ref),
+        (unit_in, unit_ref),
+        (invn_in, invn_ref),
+        (probe_in, probe_ref),
+        (gain_in, gain_ref),
+        (loss_in, loss_ref),
+    ]
+    extra = [
+        pltpu.make_async_copy(source, target, extra_sems.at[k])
+        for k, (source, target) in enumerate(pairs)
+    ]
+    for copy in extra[:3] + small[:1] + extra[3:5] + patches + values + small[1:] + extra[5:]:
         copy.start()
+    for copy in extra[:3]:
+        copy.wait()
     d_image = jnp.sum(got_ref[...].astype(F32), axis=0)
     unit = unit_ref[...]
     along = jnp.sum(d_image * unit, axis=-1, keepdims=True)
     d_context = (d_image - unit * along) * invn_ref[:, 0:1]
     d_context = d_context.astype(BF16).astype(F32)
     spread = (d_context[:, None, :] * head_mask(heads, width)[None]).reshape(lanes, width).astype(BF16)
+    for copy in extra[3:5]:
+        copy.wait()
     gain = gain_ref[...]
     right[lanes:, :] = jnp.concatenate([probe_ref[...].astype(F32)] * slots, axis=0).astype(BF16)
     small[0].wait()
@@ -258,6 +308,7 @@
         sent.append(copy)
     probe_total = jnp.sum(tn_dot(d_scores, scaled).reshape(slots, heads, width), axis=0)
     gain_sum = jnp.sum(gain_total, axis=0, keepdims=True)
+    extra[5].wait()
     loss = loss_ref[...]
     high = loss.astype(BF16).astype(F32)
     middle = (loss - high).astype(BF16).astype(F32)
@@ -359,20 +410,29 @@
         name="pool",
     )(owners[0], counts[0], patches[0], gain, probe)
 
-    caption_f = captions[0].astype(F32)
-    caption_inv = lax.rsqrt(jnp.sum(caption_f * caption_f, axis=-1, keepdims=True) + epsilon)
-    caption_unit = caption_f * caption_inv
-    texts, pooled = lax.optimization_barrier((caption_unit.astype(BF16), pooled))
-    for bit in [bit for bit in TEXT_BITS[:4] if bit < ranks]:
-        texts = jnp.concatenate([texts, swapped(texts, bit)], axis=0)
-    mine, texts = lax.optimization_barrier((mine, texts))
+    caption_unit, caption_inv, texts = call(
+        caption_body,
+        [
+            (shape((slots, width), F32), vspec()),
+            (shape((slots, 128), F32), vspec()),
+            (shape((slots, width), BF16), vspec()),
+        ],
+        [vspec()],
+        40_000_000,
+        4_000_000,
+        name="caption",
+    )(captions[0])
+    if ranks > 2:
+        for bit in (8, 4, 2):
+            texts = jnp.concatenate([texts, swapped(texts, bit)], axis=0)
+    mine, texts, pooled = lax.optimization_barrier((mine, texts, pooled))
     other = swapped(mine, 1)
-    for bit in [bit for bit in TEXT_BITS[4:] if bit < ranks]:
-        texts = jnp.concatenate([texts, swapped(texts, bit)], axis=0)
+    if ranks > 2:
+        side = swapped(texts, SIDE_BIT)
     full, unit, inv_norm, sent = call(
         image_body,
         [
-            (shape((width, width), BF16), hspec()),
+            (shape((STASH_ROWS, width), BF16), hspec()),
             (shape((slots, width), F32), vspec()),
             (shape((slots, 128), F32), vspec()),
             (shape((peers, heads + slots, width), BF16), vspec()),
@@ -382,43 +442,65 @@
         6_000_000,
         [pltpu.VMEM((width, width), BF16), dma(())],
         name="image",
-        limit=VMEM_LARGE,
+        limit=VMEM_IMAGE,
     )(mine, other, pooled)
+    if ranks > 2:
+        unit, side = lax.optimization_barrier((unit, side))
+        texts = jnp.concatenate([texts, side], axis=0)
     got = lax.all_to_all(sent, "fsdp", 0, 0, tiled=True)
-    half = ranks * slots // 2
-    d_image_part, keep, send, loss_sums = call(
+    texts = jnp.concatenate([texts, swapped(texts, CORE_BIT)], axis=0)
+    count = peers * slots
+    text_count = ranks * slots
+    d_image_part, coefficient, images, loss_sums = call(
         pair_body,
         [
             (shape((peers, slots, width), BF16), vspec()),
-            (shape((half, width), F32), vspec()),
-            (shape((half, width), BF16), vspec()),
+            (shape((count, text_count), BF16), vspec()),
+            (shape((count, width), BF16), vspec()),
             (shape((slots, 128), F32), vspec()),
         ],
         [sspec(), sspec(), vspec(), vspec()],
-        120_000_000,
+        80_000_000,
         2_000_000,
         name="pair",
     )(place, scalars, got, texts)
     d_image_got = lax.all_to_all(d_image_part, "fsdp", 0, 0, tiled=True)
 
-    def fold(total, bit):
+    def halves(rows_out):
+        return [
+            (shape((rows_out, width), F32), vspec()),
+            (shape((rows_out, width), BF16), vspec()),
+        ]
+
+    def fold(keep, send, bit):
         if bit >= ranks:
-            return total
-        rest = total.shape[0] // 2
-        return total[:rest] + swapped(total[rest:].astype(BF16), bit).astype(F32)
-
-    d_text = keep + swapped(send, TEXT_BITS[4]).astype(F32)
-    d_text = fold(d_text, TEXT_BITS[3])
-    d_image_got, d_text = lax.optimization_barrier((d_image_got, d_text))
-    d_text = fold(d_text, TEXT_BITS[2])
+            return keep, send
+        return call(
+            fold_body, halves(keep.shape[0] // 2), [vspec(), vspec()], 40_000_000, 1_000_000, name="fold"
+        )(keep, swapped(send, bit))
+
+    keep, send = call(
+        text_body, halves(text_count // 2), [vspec(), vspec()], 0, 0, name="text"
+    )(coefficient, images)
+    if ranks > 2:
+        keep, send = fold(keep, send, CORE_BIT)
+    d_image_got, keep, send = lax.optimization_barrier((d_image_got, keep, send))
+    if ranks > 2:
+        keep, send = fold(keep, send, SIDE_BIT)
 
     outgoing = call(
         back_body,
         [(shape((peers, rows + 16, width), BF16), hspec())],
-        [sspec()] + [vspec()] * 3 + [hspec()] * 4 + [vspec()] * 3,
+        [sspec()] + [hspec()] * 10,
         500_000_000,
         8_000_000,
         [
+            pltpu.VMEM((peers, slots, width), BF16),
+            pltpu.VMEM((slots, width), F32),
+            pltpu.VMEM((slots, 128), F32),
+            pltpu.VMEM((heads, width), BF16),
+            pltpu.VMEM((1, width), F32),
+            pltpu.VMEM((slots, 128), F32),
             pltpu.VMEM((width, width), BF16),
             pltpu.VMEM((slots, rows, width), BF16),
             pltpu.VMEM((slots * rows, lanes), F32),
@@ -428,15 +510,28 @@
             pltpu.VMEM((2 * lanes, width), BF16),
             pltpu.VMEM((peers, rows + 16, width), BF16),
             dma((slots + 8,)),
+            dma((6,)),
         ],
         name="back",
         limit=VMEM_LARGE,
     )(
         owners[0], d_image_got, unit, inv_norm, full, patches, stats, weights, probe, gain, loss_sums
     )[0]
-    outgoing, d_text = lax.optimization_barrier((outgoing, d_text))
+    outgoing, keep, send = lax.optimization_barrier((outgoing, keep, send))
     arrived = lax.all_to_all(outgoing, "fsdp", 0, 0, tiled=True)
-    d_caption = fold(fold(d_text, TEXT_BITS[1]), TEXT_BITS[0])
+    if ranks > 2:
+        d_caption, *blocks = call(
+            split_body,
+            [(shape((slots, width), F32), vspec())] + [(shape((slots, width), BF16), vspec())] * 3,
+            [vspec(), vspec()],
+            40_000_000,
+            1_000_000,
+            name="split",
+        )(keep, swapped(send, NEXT_BIT))
+        for block, bit in zip(blocks, Z_BITS):
+            d_caption = d_caption + swapped(block, bit).astype(F32)
+    else:
+        d_caption = keep + swapped(send, CORE_BIT).astype(F32)
 
     pooled_got = (
         got[:, :heads]
@@ -467,7 +562,7 @@
 
     text_grad = (
         (d_caption - caption_unit * jnp.sum(d_caption * caption_unit, axis=-1, keepdims=True))
-        * caption_inv
+        * caption_inv[:, 0:1]
     ).astype(BF16)
     return (loss_part, row_grad, text_grad[None], value_grad, probe_t.T[None], gain_grad)
 

time: 115 us -> 103 us (0.90); the launches traced: 114 us -> 101 us
  waiting for transfers between devices: 44.6 us -> 35.5 us
  starting transfers between devices: 43 us -> 40.6 us
    all_to_all x1, waiting for transfers between devices: 8.51 us -> 0.01 us  [local(): arrived = lax.all_to_all(outgoing, 'fsdp', 0, 0, tiled=True)]
    ppermute x11 -> x12, waiting for transfers between devices: 19.4 us -> 15.6 us  [swapped(): lax.ppermute(block, 'dp', [(i, i ^ bit) for i in range(lax.axis_size('dp'...]
    all_to_all x1, waiting for transfers between devices: 0.01 us -> 1.71 us  [local(): lax.all_to_all(jnp.broadcast_to(part[None], (peers, SEND_ROWS, width)), '...]
    all_to_all x1, starting transfers between devices: 7.22 us -> 5.59 us  [local(): got = lax.all_to_all(sent, 'fsdp', 0, 0, tiled=True)]
    all_to_all x1, waiting for transfers between devices: 7.08 us -> 8.4 us  [local(): d_image_got = lax.all_to_all(d_image_part, 'fsdp', 0, 0, tiled=True)]
    unnamed x34 -> x28, local copies, waits for them, and re-layouts: 4.27 us -> 3.18 us
    pallas_call x2 -> x7, Pallas kernels: 6.26 us -> 5.49 us  [the longest x1 3.1 us: local(): call(image_body, [(shape((STASH_ROWS, width), BF16), hspec()), (shape((sl...]
    ppermute x11 -> x12, starting transfers between devices: 22.7 us -> 21.9 us  [swapped(): lax.ppermute(block, 'dp', [(i, i ^ bit) for i in range(lax.axis_size('dp'...]
  transfers between devices with their start and end apart: 15 -> 16, of which waited for: 11 -> 9; matrix products, arithmetic and copies ran while one was open for 2% -> 2% of each run, Pallas kernels for 12% -> 12%
where the time goes in v3:
time: 103 us; the launch traced here: 101 us
  starting transfers between devices  40.6 us (39%)
  waiting for transfers between devices  35.5 us (34%)
  Pallas kernels  16.5 us (16%)
  local copies, waits for them, and re-layouts  5.22 us (5%)
  between operations  2.19 us (2%)
    ppermute x12, starting transfers between devices, swapped(): lax.ppermute(block, 'dp', [(i, i ^ bit) for i in range(lax.axis_size('dp'...  21.9 us
    ppermute x12, waiting for transfers between devices, swapped(): lax.ppermute(block, 'dp', [(i, i ^ bit) for i in range(lax.axis_size('dp'...  15.6 us
    all_to_all x1, waiting for transfers between devices, local(): got = lax.all_to_all(sent, 'fsdp', 0, 0, tiled=True)  9.79 us
    all_to_all x1, waiting for transfers between devices, local(): d_image_got = lax.all_to_all(d_image_part, 'fsdp', 0, 0, tiled=True)  8.4 us
    pallas_call x1, Pallas kernels, local(): call(back_body, [(shape((peers, rows + 16, width), BF16), hspec())], [ssp...  7.21 us
    all_to_all x1, starting transfers between devices, local(): lax.all_to_all(jnp.broadcast_to(part[None], (peers, SEND_ROWS, width)), '...  6.18 us
    all_to_all x1, starting transfers between devices, local(): got = lax.all_to_all(sent, 'fsdp', 0, 0, tiled=True)  5.59 us
    all_to_all x1, starting transfers between devices, local(): arrived = lax.all_to_all(outgoing, 'fsdp', 0, 0, tiled=True)  3.58 us
  transfers between devices with their start and end apart: 16, of which 9 were waited for; matrix products, arithmetic and copies ran while one was open for 2% of the time, Pallas kernels for 12%

profile of v3, /device:TPU:2, one launch (start us, length us, event | category | flops | bytes accessed | tf_op | source)
XLA Modules:
  0.0 101.1 jit_solution(17539972266098513684)
XLA Ops:
  1.6 1.2 %broadcast_in_dim.6 = bf16[8,72,1152]{2,1,0:T(8,128)(2,1)} broadcast(bf16[72,1152]{1,0:T(8,128)(2,1)S(1)} %constant_dynamic-slice_fusion), dimensions={1,2} | broadcast | bytes 1492992 | tf_op jit(solution)/shard_map/broadcast_in_dim | solution.py:395
  2.8 6.2 %all-to-all-start = ((bf16[8,72,1152]{2,1,0:T(8,128)(2,1)}), bf16[8,72,1152]{2,1,0:T(8,128)(2,1)S(1)}, u32[]{:S(2)}, u32[]{:S(2)}) async-start(bf16[8,72,1152]{2,1,0:T(8,128)(2,1)} %broadcast_in_dim.6), calls=%async_computation | async-start | bytes 2654208 | tf_op jit(solution)/shard_map/all_to_all | solution.py:394
  9.1 7.2 %collective-permute-start = (bf16[8,1152]{1,0:T(8,128)(2,1)S(1)}, bf16[8,1152]{1,0:T(8,128)(2,1)S(1)}, u32[]{:S(2)}, u32[]{:S(2)}) collective-permute-start(bf16[8,1152]{1,0:T(8,128)(2,1)S(1)} %get-tuple-element.46), channel_id=1, source_target_pairs={{0,64},{8,72},{16,80},{24,88},{32,96},{40,104},{48,112},{56,120},{... | collective-permute-start | bytes 55304 | tf_op jit(solution)/shard_map/ppermute | solution.py:26
  16.3 1.7 %collective-permute-done = bf16[8,1152]{1,0:T(8,128)(2,1)S(1)} collective-permute-done((bf16[8,1152]{1,0:T(8,128)(2,1)S(1)}, bf16[8,1152]{1,0:T(8,128)(2,1)S(1)}, u32[]{:S(2)}, u32[]{:S(2)}) %collective-permute-start) | collective-permute-done | bytes 18464 | tf_op jit(solution)/shard_map/ppermute | solution.py:26
  18.1 2.0 %collective-permute-start.1 = (bf16[16,1152]{1,0:T(8,128)(2,1)S(1)}, bf16[16,1152]{1,0:T(8,128)(2,1)S(1)}, u32[]{:S(2)}, u32[]{:S(2)}) collective-permute-start(bf16[16,1152]{1,0:T(8,128)(2,1)S(1)} %pad_maximum_fusion.4), channel_id=1, source_target_pairs={{0,32},{8,40},{16,48},{24,56},{32,0},{40,8},{48,16},{56,24},{64,96... | collective-permute-start | bytes 110600 | tf_op jit(solution)/shard_map/ppermute | solution.py:26
  20.1 2.8 %collective-permute-done.1 = bf16[16,1152]{1,0:T(8,128)(2,1)S(1)} collective-permute-done((bf16[16,1152]{1,0:T(8,128)(2,1)S(1)}, bf16[16,1152]{1,0:T(8,128)(2,1)S(1)}, u32[]{:S(2)}, u32[]{:S(2)}) %collective-permute-start.1) | collective-permute-done | bytes 36896 | tf_op jit(solution)/shard_map/ppermute | solution.py:26
  24.0 2.1 %pool.1 = (f32[384,128]{1,0:T(8,128)S(1)}, f32[384,128]{1,0:T(8,128)S(1)}, bf16[128,1152]{1,0:T(8,128)(2,1)S(1)}) custom-call(s32[8]{0:T(128)S(1)} %bitcast.21, s32[8]{0:T(128)S(1)} %bitcast.22, bf16[8,48,1152]{2,1,0:T(8,128)(2,1)S(1)} %bitcast.16, f32[1,1152]{1,0:T(1,128)S(1)} %reshape.27.gain_ref.gain_in, bf16[16,1152]{1,0:T(8,128)(2,1)S(1)} %bitcast.19), custom_call_target="tpu_custom_call" | custom-call | flops 40000000 | bytes 4000000 | tf_op jit(solution)/shard_map/pool/pallas_call | solution.py:399
  27.5 1.7 %all-to-all-done.mine_ref = bf16[8,72,1152]{2,1,0:T(8,128)(2,1)S(1)} async-done(((bf16[8,72,1152]{2,1,0:T(8,128)(2,1)}), bf16[8,72,1152]{2,1,0:T(8,128)(2,1)S(1)}, u32[]{:S(2)}, u32[]{:S(2)}) %all-to-all-start) | async-done | bytes 1327136 | tf_op jit(solution)/shard_map/all_to_all | solution.py:394
  29.2 1.4 %collective-permute-start.4 = (bf16[64,1152]{1,0:T(8,128)(2,1)S(1)}, bf16[64,1152]{1,0:T(8,128)(2,1)S(1)}, u32[]{:S(2)}, u32[]{:S(2)}) collective-permute-start(bf16[64,1152]{1,0:T(8,128)(2,1)S(1)} %pad_maximum_fusion.2), channel_id=1, source_target_pairs={{0,128},{8,136},{16,144},{24,152},{32,160},{40,168},{48,176},{56,1... | collective-permute-start | bytes 442376 | tf_op jit(solution)/shard_map/ppermute | solution.py:26
  30.7 1.6 %collective-permute-done.3.other_ref = bf16[8,72,1152]{2,1,0:T(8,128)(2,1)S(1)} collective-permute-done((bf16[8,72,1152]{2,1,0:T(8,128)(2,1)S(1)}, bf16[8,72,1152]{2,1,0:T(8,128)(2,1)S(1)}, u32[]{:S(2)}, u32[]{:S(2)}) %collective-permute-start.3) | collective-permute-done | bytes 1327136 | tf_op jit(solution)/shard_map/ppermute | solution.py:26
  32.3 3.1 %image.1 = (bf16[15616,1152]{1,0:T(8,128)(2,1)}, f32[8,1152]{1,0:T(8,128)S(1)}, f32[8,128]{1,0:T(8,128)S(1)}, bf16[8,24,1152]{2,1,0:T(8,128)(2,1)}) custom-call(bf16[8,72,1152]{2,1,0:T(8,128)(2,1)S(1)} %all-to-all-done.mine_ref, bf16[8,72,1152]{2,1,0:T(8,128)(2,1)S(1)} %collective-permute-done.3.other_ref, bf16[128,1152]{1,0:T(8,128)(2,1)S(1)} %get-tuple-element.49.a_ref), custom_call_target="tpu_custom_call" | custom-call | flops 400000000 | bytes 6000000 | tf_op jit(solution)/shard_map/image/pallas_call | solution.py:432
  36.3 5.6 %all-to-all-start.1 = ((bf16[8,24,1152]{2,1,0:T(8,128)(2,1)}), bf16[8,24,1152]{2,1,0:T(8,128)(2,1)S(1)}, u32[]{:S(2)}, u32[]{:S(2)}) async-start(bf16[8,24,1152]{2,1,0:T(8,128)(2,1)} %get-tuple-element.50), calls=%async_computation.1 | async-start | bytes 884736 | tf_op jit(solution)/shard_map/all_to_all | solution.py:450
  43.3 9.8 %all-to-all-done.1.got_ref = bf16[8,24,1152]{2,1,0:T(8,128)(2,1)S(1)} async-done(((bf16[8,24,1152]{2,1,0:T(8,128)(2,1)}), bf16[8,24,1152]{2,1,0:T(8,128)(2,1)S(1)}, u32[]{:S(2)}, u32[]{:S(2)}) %all-to-all-start.1) | async-done | bytes 442400 | tf_op jit(solution)/shard_map/all_to_all | solution.py:450
  53.1 1.9 %pair.1 = (bf16[8,8,1152]{2,1,0:T(8,128)(2,1)}, bf16[64,256]{1,0:T(8,128)(2,1)S(1)}, bf16[64,1152]{1,0:T(8,128)(2,1)S(1)}, f32[8,128]{1,0:T(8,128)S(1)}) custom-call(s32[1]{0:T(128)} %bitcast.1.place, f32[2]{0:T(128)S(1)} %pad_maximum_fusion.5.scalars, bf16[8,24,1152]{2,1,0:T(8,128)(2,1)S(1)} %all-to-all-done.1.got_ref, ...), custom_call_target="tpu_custom_call" | custom-call | flops 80000000 | bytes 2000000 | tf_op jit(solution)/shard_map/pair/pallas_call | solution.py:454
  55.5 3.4 %all-to-all-start.2 = ((bf16[8,8,1152]{2,1,0:T(8,128)(2,1)}), bf16[8,8,1152]{2,1,0:T(8,128)(2,1)S(1)}, u32[]{:S(2)}, u32[]{:S(2)}) async-start(bf16[8,8,1152]{2,1,0:T(8,128)(2,1)} %get-tuple-element.54), calls=%async_computation.2 | async-start | bytes 294912 | tf_op jit(solution)/shard_map/all_to_all | solution.py:467
  59.0 8.4 %all-to-all-done.2.got_in = bf16[8,8,1152]{2,1,0:T(8,128)(2,1)S(1)} async-done(((bf16[8,8,1152]{2,1,0:T(8,128)(2,1)}), bf16[8,8,1152]{2,1,0:T(8,128)(2,1)S(1)}, u32[]{:S(2)}, u32[]{:S(2)}) %all-to-all-start.2) | async-done | bytes 147488 | tf_op jit(solution)/shard_map/all_to_all | solution.py:467
  67.4 1.4 %collective-permute-start.7 = (bf16[64,1152]{1,0:T(8,128)(2,1)S(1)}, bf16[64,1152]{1,0:T(8,128)(2,1)S(1)}, u32[]{:S(2)}, u32[]{:S(2)}) collective-permute-start(bf16[64,1152]{1,0:T(8,128)(2,1)S(1)} %get-tuple-element.69), channel_id=1, source_target_pairs={{0,128},{8,136},{16,144},{24,152},{32,160},{40,168},{48,176},{56,1... | collective-permute-start | bytes 442376 | tf_op jit(solution)/shard_map/ppermute | solution.py:26
  68.8 7.2 %back.1 = bf16[8,64,1152]{2,1,0:T(8,128)(2,1)} custom-call(s32[8]{0:T(128)} %bitcast.20, bf16[8,8,1152]{2,1,0:T(8,128)(2,1)} %copy-done.12, f32[8,1152]{1,0:T(8,128)} %copy-done.6, f32[8,128]{1,0:T(8,128)} %copy-done.7, bf16[15616,1152]{1,0:T(8,128)(2,1)} %get-tuple-element.64.full_in, bf16[1,8,48,1152]{3,2,1,0:T(8,128)(2,1)} %x_in.1, f32[384,128]{1,0:T(8,128)} %copy-done.2, ...), custom_call_target="tpu_custom_call" | custom-call | flops 500000000 | bytes 8000000 | tf_op jit(solution)/shard_map/back/pallas_call | solution.py:491
  76.1 3.6 %all-to-all-start.3 = ((bf16[8,64,1152]{2,1,0:T(8,128)(2,1)}), bf16[8,64,1152]{2,1,0:T(8,128)(2,1)S(1)}, u32[]{:S(2)}, u32[]{:S(2)}) async-start(bf16[8,64,1152]{2,1,0:T(8,128)(2,1)} %back.1), calls=%async_computation.3 | async-start | bytes 2359296 | tf_op jit(solution)/shard_map/all_to_all | solution.py:521
  80.8 3.4 %collective-permute-done.8.got_ref = bf16[32,1152]{1,0:T(8,128)(2,1)S(1)} collective-permute-done((bf16[32,1152]{1,0:T(8,128)(2,1)S(1)}, bf16[32,1152]{1,0:T(8,128)(2,1)S(1)}, u32[]{:S(2)}, u32[]{:S(2)}) %collective-permute-start.8) | collective-permute-done | bytes 73760 | tf_op jit(solution)/shard_map/ppermute | solution.py:26
  84.2 3.0 %collective-permute-start.10 = (bf16[8,1152]{1,0:T(8,128)(2,1)S(1)}, bf16[8,1152]{1,0:T(8,128)(2,1)S(1)}, u32[]{:S(2)}, u32[]{:S(2)}) collective-permute-start(bf16[8,1152]{1,0:T(8,128)(2,1)S(1)} %get-tuple-element.79), channel_id=1, source_target_pairs={{0,32},{8,40},{16,48},{24,56},{32,0},{40,8},{48,16},{56,24},{64,96... | collective-permute-start | bytes 55304 | tf_op jit(solution)/shard_map/ppermute | solution.py:26
  87.1 3.6 %collective-permute-start.11 = (bf16[8,1152]{1,0:T(8,128)(2,1)S(1)}, bf16[8,1152]{1,0:T(8,128)(2,1)S(1)}, u32[]{:S(2)}, u32[]{:S(2)}) collective-permute-start(bf16[8,1152]{1,0:T(8,128)(2,1)S(1)} %get-tuple-element.80), channel_id=1, source_target_pairs={{0,96},{8,104},{16,112},{24,120},{32,64},{40,72},{48,80},{56,88},{... | collective-permute-start | bytes 55304 | tf_op jit(solution)/shard_map/ppermute | solution.py:26
  93.1 5.5 %collective-permute-done.9 = bf16[8,1152]{1,0:T(8,128)(2,1)S(1)} collective-permute-done((bf16[8,1152]{1,0:T(8,128)(2,1)S(1)}, bf16[8,1152]{1,0:T(8,128)(2,1)S(1)}, u32[]{:S(2)}, u32[]{:S(2)}) %collective-permute-start.9) | collective-permute-done | bytes 18464 | tf_op jit(solution)/shard_map/ppermute | solution.py:26
  99.4 1.7 %last.1 = (bf16[1,8,48,1152]{3,2,1,0:T(8,128)(2,1)}, bf16[1,144,1152]{2,1,0:T(8,128)(2,1)}, bf16[16,144]{1,0:T(8,128)(2,1)}, bf16[1,144]{1,0:T(2,128)(2,1)}, f32[1,1]{1,0:T(1,128)}) custom-call(bf16[8,64,1152]{2,1,0:T(8,128)(2,1)S(1)} %all-to-all-done.3.refs_0_, bf16[16,64,144]{2,1,0:T(8,128)(2,1)S(1)} %bitcast.17), custom_call_target="tpu_custom_call" | custom-call | flops 400000000 | bytes 3000000 | tf_op jit(solution)/shard_map/last/pallas_call | solution.py:547
  (61 shorter events, 9.4 us)
Async XLA Ops:
  2.8 6.2 %copy-start.11 = (bf16[1,8,1152]{2,1,0:T(8,128)(2,1)S(1)}, bf16[1,8,1152]{2,1,0:T(8,128)(2,1)}, u32[]{:S(2)}) copy-start(bf16[1,8,1152]{2,1,0:T(8,128)(2,1)} %param.12) | copy-start | bytes 55300
  2.8 21.2 %copy-start.13 = (f32[1152]{0:T(1024)S(1)}, f32[1152]{0:T(1024)}, u32[]{:S(2)}) copy-start(f32[1152]{0:T(1024)} %param.13) | copy-start | bytes 13828
  2.8 21.2 %copy-start.1 = (bf16[1,8,48,1152]{3,2,1,0:T(8,128)(2,1)S(1)}, bf16[1,8,48,1152]{3,2,1,0:T(8,128)(2,1)}, u32[]{:S(2)}) copy-start(bf16[1,8,48,1152]{3,2,1,0:T(8,128)(2,1)} %x_in.1) | copy-start | bytes 2654212
  2.8 21.2 %copy-start.4 = (bf16[1152,16]{0,1:T(8,128)(2,1)S(1)}, bf16[1152,16]{0,1:T(8,128)(2,1)}, u32[]{:S(2)}) copy-start(bf16[1152,16]{0,1:T(8,128)(2,1)} %param.14) | copy-start | bytes 110596
  2.8 21.2 %copy-start.9 = (s32[1,8]{1,0:T(1,128)S(1)}, s32[1,8]{1,0:T(1,128)}, u32[]{:S(2)}) copy-start(s32[1,8]{1,0:T(1,128)} %param.11) | copy-start | bytes 100
  2.8 21.2 %copy-start.10 = (s32[1,8]{1,0:T(1,128)S(1)}, s32[1,8]{1,0:T(1,128)}, u32[]{:S(2)}) copy-start(s32[1,8]{1,0:T(1,128)} %param.10) | copy-start | bytes 100
  2.8 26.4 %all-to-all-start = ((bf16[8,72,1152]{2,1,0:T(8,128)(2,1)}), bf16[8,72,1152]{2,1,0:T(8,128)(2,1)S(1)}, u32[]{:S(2)}, u32[]{:S(2)}) async-start(bf16[8,72,1152]{2,1,0:T(8,128)(2,1)} %broadcast_in_dim.6), calls=%async_computation | async-start | bytes 2654208 | tf_op jit(solution)/shard_map/all_to_all | solution.py:394
  9.1 8.9 %collective-permute-start = (bf16[8,1152]{1,0:T(8,128)(2,1)S(1)}, bf16[8,1152]{1,0:T(8,128)(2,1)S(1)}, u32[]{:S(2)}, u32[]{:S(2)}) collective-permute-start(bf16[8,1152]{1,0:T(8,128)(2,1)S(1)} %get-tuple-element.46), channel_id=1, source_target_pairs={{0,64},{8,72},{16,80},{24,88},{32,96},{40,104},{48,112},{56,120},{... | collective-permute-start | bytes 55304 | tf_op jit(solution)/shard_map/ppermute | solution.py:26
  18.1 4.9 %collective-permute-start.1 = (bf16[16,1152]{1,0:T(8,128)(2,1)S(1)}, bf16[16,1152]{1,0:T(8,128)(2,1)S(1)}, u32[]{:S(2)}, u32[]{:S(2)}) collective-permute-start(bf16[16,1152]{1,0:T(8,128)(2,1)S(1)} %pad_maximum_fusion.4), channel_id=1, source_target_pairs={{0,32},{8,40},{16,48},{24,56},{32,0},{40,8},{48,16},{56,24},{64,96... | collective-permute-start | bytes 110600 | tf_op jit(solution)/shard_map/ppermute | solution.py:26
  22.9 4.6 %collective-permute-start.2 = (bf16[32,1152]{1,0:T(8,128)(2,1)S(1)}, bf16[32,1152]{1,0:T(8,128)(2,1)S(1)}, u32[]{:S(2)}, u32[]{:S(2)}) collective-permute-start(bf16[32,1152]{1,0:T(8,128)(2,1)S(1)} %pad_maximum_fusion.3), channel_id=1, source_target_pairs={{0,16},{8,24},{16,0},{24,8},{32,48},{40,56},{48,32},{56,40},{64,80... | collective-permute-start | bytes 221192 | tf_op jit(solution)/shard_map/ppermute | solution.py:26
  24.0 11.4 %copy-start.5 = (f32[1,1152]{1,0:T(1,128)}, f32[1,1152]{1,0:T(1,128)S(1)}, u32[]{:S(2)}) copy-start(f32[1,1152]{1,0:T(1,128)S(1)} %reshape.27.gain_ref.gain_in) | copy-start | bytes 13828
  29.2 3.1 %collective-permute-start.3 = (bf16[8,72,1152]{2,1,0:T(8,128)(2,1)S(1)}, bf16[8,72,1152]{2,1,0:T(8,128)(2,1)S(1)}, u32[]{:S(2)}, u32[]{:S(2)}) collective-permute-start(bf16[8,72,1152]{2,1,0:T(8,128)(2,1)S(1)} %all-to-all-done.mine_ref), channel_id=1, source_target_pairs={{0,8},{8,0},{16,24},{24,16},{32,40},{40,32},{48,56},{56,48},{64,72... | collective-permute-start | bytes 3981320 | tf_op jit(solution)/shard_map/ppermute | solution.py:26
  29.2 6.8 %collective-permute-start.4 = (bf16[64,1152]{1,0:T(8,128)(2,1)S(1)}, bf16[64,1152]{1,0:T(8,128)(2,1)S(1)}, u32[]{:S(2)}, u32[]{:S(2)}) collective-permute-start(bf16[64,1152]{1,0:T(8,128)(2,1)S(1)} %pad_maximum_fusion.2), channel_id=1, source_target_pairs={{0,128},{8,136},{16,144},{24,152},{32,160},{40,168},{48,176},{56,1... | collective-permute-start | bytes 442376 | tf_op jit(solution)/shard_map/ppermute | solution.py:26
  36.0 7.3 %copy-start.6 = (f32[8,1152]{1,0:T(8,128)}, f32[8,1152]{1,0:T(8,128)S(1)}, u32[]{:S(2)}) copy-start(f32[8,1152]{1,0:T(8,128)S(1)} %get-tuple-element.62.unit_in) | copy-start | bytes 110596
  36.0 7.2 %collective-permute-start.5 = (bf16[128,1152]{1,0:T(8,128)(2,1)S(1)}, bf16[128,1152]{1,0:T(8,128)(2,1)S(1)}, u32[]{:S(2)}, u32[]{:S(2)}) collective-permute-start(bf16[128,1152]{1,0:T(8,128)(2,1)S(1)} %pad_maximum_fusion.1), channel_id=1, source_target_pairs={{0,8},{8,0},{16,24},{24,16},{32,40},{40,32},{48,56},{56,48},{64,72... | collective-permute-start | bytes 884744 | tf_op jit(solution)/shard_map/ppermute | solution.py:26
  36.3 16.8 %all-to-all-start.1 = ((bf16[8,24,1152]{2,1,0:T(8,128)(2,1)}), bf16[8,24,1152]{2,1,0:T(8,128)(2,1)S(1)}, u32[]{:S(2)}, u32[]{:S(2)}) async-start(bf16[8,24,1152]{2,1,0:T(8,128)(2,1)} %get-tuple-element.50), calls=%async_computation.1 | async-start | bytes 884736 | tf_op jit(solution)/shard_map/all_to_all | solution.py:450
  55.5 3.4 %collective-permute-start.6 = (bf16[128,1152]{1,0:T(8,128)(2,1)S(1)}, bf16[128,1152]{1,0:T(8,128)(2,1)S(1)}, u32[]{:S(2)}, u32[]{:S(2)}) collective-permute-start(bf16[128,1152]{1,0:T(8,128)(2,1)S(1)} %get-tuple-element.58), channel_id=1, source_target_pairs={{0,8},{8,0},{16,24},{24,16},{32,40},{40,32},{48,56},{56,48},{64,72... | collective-permute-start | bytes 884744 | tf_op jit(solution)/shard_map/ppermute | solution.py:26
  55.5 11.9 %all-to-all-start.2 = ((bf16[8,8,1152]{2,1,0:T(8,128)(2,1)}), bf16[8,8,1152]{2,1,0:T(8,128)(2,1)S(1)}, u32[]{:S(2)}, u32[]{:S(2)}) async-start(bf16[8,8,1152]{2,1,0:T(8,128)(2,1)} %get-tuple-element.54), calls=%async_computation.2 | async-start | bytes 294912 | tf_op jit(solution)/shard_map/all_to_all | solution.py:467
  67.4 8.7 %collective-permute-start.7 = (bf16[64,1152]{1,0:T(8,128)(2,1)S(1)}, bf16[64,1152]{1,0:T(8,128)(2,1)S(1)}, u32[]{:S(2)}, u32[]{:S(2)}) collective-permute-start(bf16[64,1152]{1,0:T(8,128)(2,1)S(1)} %get-tuple-element.69), channel_id=1, source_target_pairs={{0,128},{8,136},{16,144},{24,152},{32,160},{40,168},{48,176},{56,1... | collective-permute-start | bytes 442376 | tf_op jit(solution)/shard_map/ppermute | solution.py:26
  76.1 23.3 %all-to-all-start.3 = ((bf16[8,64,1152]{2,1,0:T(8,128)(2,1)}), bf16[8,64,1152]{2,1,0:T(8,128)(2,1)S(1)}, u32[]{:S(2)}, u32[]{:S(2)}) async-start(bf16[8,64,1152]{2,1,0:T(8,128)(2,1)} %back.1), calls=%async_computation.3 | async-start | bytes 2359296 | tf_op jit(solution)/shard_map/all_to_all | solution.py:521
  79.7 4.4 %collective-permute-start.8 = (bf16[32,1152]{1,0:T(8,128)(2,1)S(1)}, bf16[32,1152]{1,0:T(8,128)(2,1)S(1)}, u32[]{:S(2)}, u32[]{:S(2)}) collective-permute-start(bf16[32,1152]{1,0:T(8,128)(2,1)S(1)} %get-tuple-element.76), channel_id=1, source_target_pairs={{0,16},{8,24},{16,0},{24,8},{32,48},{40,56},{48,32},{56,40},{64,80... | collective-permute-start | bytes 221192 | tf_op jit(solution)/shard_map/ppermute | solution.py:26
  84.2 8.4 %collective-permute-start.10 = (bf16[8,1152]{1,0:T(8,128)(2,1)S(1)}, bf16[8,1152]{1,0:T(8,128)(2,1)S(1)}, u32[]{:S(2)}, u32[]{:S(2)}) collective-permute-start(bf16[8,1152]{1,0:T(8,128)(2,1)S(1)} %get-tuple-element.79), channel_id=1, source_target_pairs={{0,32},{8,40},{16,48},{24,56},{32,0},{40,8},{48,16},{56,24},{64,96... | collective-permute-start | bytes 55304 | tf_op jit(solution)/shard_map/ppermute | solution.py:26
  87.1 6.0 %collective-permute-start.11 = (bf16[8,1152]{1,0:T(8,128)(2,1)S(1)}, bf16[8,1152]{1,0:T(8,128)(2,1)S(1)}, u32[]{:S(2)}, u32[]{:S(2)}) collective-permute-start(bf16[8,1152]{1,0:T(8,128)(2,1)S(1)} %get-tuple-element.80), channel_id=1, source_target_pairs={{0,96},{8,104},{16,112},{24,120},{32,64},{40,72},{48,80},{56,88},{... | collective-permute-start | bytes 55304 | tf_op jit(solution)/shard_map/ppermute | solution.py:26
  90.7 7.9 %collective-permute-start.9 = (bf16[8,1152]{1,0:T(8,128)(2,1)S(1)}, bf16[8,1152]{1,0:T(8,128)(2,1)S(1)}, u32[]{:S(2)}, u32[]{:S(2)}) collective-permute-start(bf16[8,1152]{1,0:T(8,128)(2,1)S(1)} %get-tuple-element.78), channel_id=1, source_target_pairs={{0,64},{8,72},{16,80},{24,88},{32,96},{40,104},{48,112},{56,120},{... | collective-permute-start | bytes 55304 | tf_op jit(solution)/shard_map/ppermute | solution.py:26
  (6 other events, 5.0 us)

commit v4 on v3

--- a/solution.py
+++ b/solution.py
@@ -14,6 +14,7 @@
 VMEM_LIMIT = 16 * 1024 * 1024
 VMEM_LARGE = 60_000_000
 VMEM_IMAGE = 28_000_000
+UNIT_ROWS = 48
 STASH_ROWS = 15_616
 SEND_ROWS = 72
 
@@ -66,6 +67,12 @@
     return lax.dot_general(a, b, (((0,), (0,)), ((), ())), preferred_element_type=F32)
 
 
+def terms(value):
+    high = value.astype(BF16).astype(F32)
+    middle = (value - high).astype(BF16).astype(F32)
+    return [high, middle, value - high - middle]
+
+
 def head_mask(heads, width):
     head_width = width // heads
     low = lax.broadcasted_iota(jnp.int32, (heads, width), 0) * head_width
@@ -73,7 +80,7 @@
     return ((column >= low) & (column < low + head_width)).astype(F32)
 
 
-def pool_body(owners, counts, x_ref, gain_ref, probe_ref, stats_ref, w_ref, a_ref, scaled_ref):
+def pool_body(owners, counts, x_ref, gain_ref, probe_ref, side_ref, a_ref, scaled_ref):
     slots, rows, width = x_ref.shape
     heads = probe_ref.shape[0]
     scale = 1.0 / math.sqrt(width // heads)
@@ -90,7 +97,7 @@
         var = jnp.sum(centered * centered, axis=-1, keepdims=True) * (1.0 / width)
         inv = lax.rsqrt(var + epsilon)
         scaled_ref[r * rows : (r + 1) * rows, :] = ((centered * inv) * gain).astype(BF16)
-        stats_ref[r * rows : (r + 1) * rows, :] = jnp.where(column < lanes // 2, mean, inv)
+        side_ref[r * rows : (r + 1) * rows, 0:lanes] = jnp.where(column < lanes // 2, mean, inv)
         own = (column >= r * heads) & (column < (r + 1) * heads)
         masks.append(jnp.where(own & (patch < counts[source]), 1.0, 0.0))
     valid = jnp.concatenate(masks, axis=0) > 0.5
@@ -100,15 +107,15 @@
     highest = jnp.max(jnp.where(valid, scores, -jnp.inf), axis=0, keepdims=True)
     raised = jnp.where(valid, jnp.exp(jnp.where(valid, scores - highest, 0.0)), 0.0)
     weights = raised / jnp.sum(raised, axis=0, keepdims=True)
-    w_ref[...] = weights
+    side_ref[:, lanes:] = weights
     a_ref[...] = tn_dot(weights.astype(BF16), scaled).astype(BF16)
 
 
 def image_body(
-    mine_ref, other_ref, a_ref, full_out, unit_ref, inv_ref, out_ref, full, sem
+    mine_ref, other_ref, a_ref, full_out, out_ref, full, sems
 ):
     shards, part_rows, width = mine_ref.shape
-    slots = unit_ref.shape[0]
+    slots = shards
     heads = a_ref.shape[0] // slots
     cut = width // shards
     rest = cut - part_rows
@@ -127,15 +134,19 @@
     def _():
         put(other_ref, mine_ref)
 
-    copy = pltpu.make_async_copy(full, full_out.at[pl.ds(0, width), :], sem)
-    copy.start()
+    copies = [
+        pltpu.make_async_copy(full.at[at, :], full_out.at[at, :], sems.at[k])
+        for k, at in enumerate([pl.ds(0, width), pl.ds(width, UNIT_ROWS)])
+    ]
+    copies[0].start()
     pooled = a_ref[...]
-    wide = jnp.dot(pooled, full[...], preferred_element_type=F32).reshape(slots, heads, width)
+    wide = jnp.dot(pooled, full[0:width, :], preferred_element_type=F32).reshape(slots, heads, width)
     context = jnp.sum(wide * head_mask(heads, width)[None], axis=1)
     inv = lax.rsqrt(jnp.sum(context * context, axis=-1, keepdims=True) + epsilon)
     unit = context * inv
-    unit_ref[...] = unit
-    inv_ref[...] = jnp.broadcast_to(inv, inv_ref.shape)
+    kept = terms(unit) + terms(jnp.broadcast_to(inv, unit.shape))
+    full[width:, :] = jnp.concatenate(kept, axis=0).astype(BF16)
+    copies[1].start()
     wide_pooled = pooled.astype(F32)
     for p in range(shards):
         moved = jnp.concatenate(
@@ -146,7 +157,8 @@
             axis=1,
         )
         out_ref[p] = jnp.concatenate([moved, unit], axis=0).astype(BF16)
-    copy.wait()
+    for copy in copies:
+        copy.wait()
 
 
 def caption_body(caption_ref, unit_ref, inv_ref, text_ref):
@@ -211,72 +223,57 @@
 
 
 def back_body(
-    owners, got_in, unit_in, invn_in, full_in, x_in, stats_in, w_in, probe_in, gain_in, loss_in,
-    out_ref, got_ref, unit_ref, invn_ref, probe_ref, gain_ref, loss_ref,
-    full, x_ref, stats_ref, w_ref, normed_ref, scaled_ref, right, result, sems, extra_sems,
+    owners, got_in, full_in, x_in, side_in, const_in, loss_in, out_ref,
+    got_ref, full, x_ref, side_ref, const_ref, loss_ref, normed_ref, scaled_ref, right, result, sems,
 ):
     slots, rows, width = x_ref.shape
-    heads = probe_ref.shape[0]
-    lanes = slots * heads
+    lanes = side_ref.shape[1] // 2
+    heads = lanes // slots
     cut = width // slots
     scale = 1.0 / math.sqrt(width // heads)
     chunk = width // 3
-    patches = [
-        pltpu.make_async_copy(x_in.at[0, source_of(owners, r, slots)], x_ref.at[r], sems.at[r])
-        for r in range(slots)
+    rows_of = [pl.ds(width, UNIT_ROWS)] + [pl.ds(c * chunk, chunk) for c in range(3)]
+    pairs = [
+        (full_in.at[rows_of[0], :], full.at[rows_of[0], :]),
+        (got_in, got_ref),
+        (side_in, side_ref),
+        (const_in, const_ref),
+        (x_in.at[0], x_ref),
     ]
-    small = [
-        pltpu.make_async_copy(stats_in, stats_ref, sems.at[slots]),
-        pltpu.make_async_copy(w_in, w_ref, sems.at[slots + 1]),
+    pairs += [(full_in.at[at, :], full.at[at, :]) for at in rows_of[1:]]
+    pairs += [(loss_in, loss_ref)]
+    copies = [
+        pltpu.make_async_copy(source, target, sems.at[k]) for k, (source, target) in enumerate(pairs)
     ]
-    values = [
-        pltpu.make_async_copy(
-            full_in.at[pl.ds(c * chunk, chunk), :],
-            full.at[pl.ds(c * chunk, chunk), :],
-            sems.at[slots + 2 + c],
-        )
-        for c in range(3)
-    ]
-    pairs = [
-        (got_in, got_ref),
-        (unit_in, unit_ref),
-        (invn_in, invn_ref),
-        (probe_in, probe_ref),
-        (gain_in, gain_ref),
-        (loss_in, loss_ref),
-    ]
-    extra = [
-        pltpu.make_async_copy(source, target, extra_sems.at[k])
-        for k, (source, target) in enumerate(pairs)
-    ]
-    for copy in extra[:3] + small[:1] + extra[3:5] + patches + values + small[1:] + extra[5:]:
+    for copy in copies:
         copy.start()
-    for copy in extra[:3]:
-        copy.wait()
+    copies[0].wait()
+    copies[1].wait()
     d_image = jnp.sum(got_ref[...].astype(F32), axis=0)
-    unit = unit_ref[...]
+    kept = full[width:, :].astype(F32)
+    unit = kept[0:slots] + kept[slots : 2 * slots] + kept[2 * slots : 3 * slots]
+    inv_norm = kept[3 * slots : 4 * slots] + kept[4 * slots : 5 * slots] + kept[5 * slots :]
     along = jnp.sum(d_image * unit, axis=-1, keepdims=True)
-    d_context = (d_image - unit * along) * invn_ref[:, 0:1]
+    d_context = (d_image - unit * along) * inv_norm
     d_context = d_context.astype(BF16).astype(F32)
     spread = (d_context[:, None, :] * head_mask(heads, width)[None]).reshape(lanes, width).astype(BF16)
-    for copy in extra[3:5]:
-        copy.wait()
-    gain = gain_ref[...]
-    right[lanes:, :] = jnp.concatenate([probe_ref[...].astype(F32)] * slots, axis=0).astype(BF16)
-    small[0].wait()
+    copies[2].wait()
+    copies[3].wait()
+    gain = const_ref[heads : heads + 1, :]
+    right[lanes:, :] = jnp.concatenate([const_ref[0:heads, :]] * slots, axis=0).astype(BF16)
+    copies[4].wait()
     for r in range(slots):
-        patches[r].wait()
         at = slice(r * rows, (r + 1) * rows)
-        normed = (x_ref[r].astype(F32) - stats_ref[at, 0:1]) * stats_ref[at, lanes // 2 : lanes // 2 + 1]
+        x = x_ref[source_of(owners, r, slots)].astype(F32)
+        normed = (x - side_ref[at, 0:1]) * side_ref[at, lanes // 2 : lanes // 2 + 1]
         normed_ref[at, :] = normed
         scaled_ref[at, :] = (normed * gain).astype(BF16)
     for c in range(3):
-        values[c].wait()
+        copies[5 + c].wait()
         at = slice(c * chunk, (c + 1) * chunk)
         right[0:lanes, at] = nt_dot(spread, full[at, :]).astype(BF16)
-    small[1].wait()
     scaled = scaled_ref[...]
-    weights = w_ref[...]
+    weights = side_ref[:, lanes:]
     d_weights = nt_dot(scaled, right[0:lanes, :])
     centre = jnp.sum(weights * d_weights, axis=0, keepdims=True)
     d_scores = (weights * (d_weights - centre) * scale).astype(BF16)
@@ -298,21 +295,18 @@
             grad_in = d_scaled * gain
             mean_a = jnp.sum(grad_in, axis=-1, keepdims=True) * (1.0 / width)
             mean_b = jnp.sum(product * gain, axis=-1, keepdims=True) * (1.0 / width)
-            inv = stats_ref[at, lanes // 2 : lanes // 2 + 1]
+            inv = side_ref[at, lanes // 2 : lanes // 2 + 1]
             result[r, 0:rows, :] = (inv * (grad_in - mean_a - normed * mean_b)).astype(BF16)
         at = pl.ds(g * half, half)
         copy = pltpu.make_async_copy(
-            result.at[at, pl.ds(0, rows), :], out_ref.at[at, pl.ds(0, rows), :], sems.at[slots + 5 + g]
+            result.at[at, pl.ds(0, rows), :], out_ref.at[at, pl.ds(0, rows), :], sems.at[9 + g]
         )
         copy.start()
         sent.append(copy)
     probe_total = jnp.sum(tn_dot(d_scores, scaled).reshape(slots, heads, width), axis=0)
     gain_sum = jnp.sum(gain_total, axis=0, keepdims=True)
-    extra[5].wait()
-    loss = loss_ref[...]
-    high = loss.astype(BF16).astype(F32)
-    middle = (loss - high).astype(BF16).astype(F32)
-    low = loss - high - middle
+    copies[8].wait()
+    high, middle, low = terms(loss_ref[...])
     pad = jnp.zeros((8, 256 - cut), F32)
     for p in range(slots):
         at = slice(p * cut, (p + 1) * cut)
@@ -335,7 +329,7 @@
         result[p, rows : rows + 16, :] = jnp.concatenate([d_context, misc], axis=0).astype(BF16)
     tail = pl.ds(rows, 16)
     copy = pltpu.make_async_copy(
-        result.at[:, tail, :], out_ref.at[:, tail, :], sems.at[slots + 7]
+        result.at[:, tail, :], out_ref.at[:, tail, :], sems.at[11]
     )
     copy.start()
     for copy in sent + [copy]:
@@ -396,11 +390,10 @@
     )
 
     lanes = slots * heads
-    stats, weights, pooled = call(
+    side, pooled = call(
         pool_body,
         [
-            (shape((slots * rows, lanes), F32), vspec()),
-            (shape((slots * rows, lanes), F32), vspec()),
+            (shape((slots * rows, 2 * lanes), F32), vspec()),
             (shape((lanes, width), BF16), vspec()),
         ],
         [sspec(), sspec(), vspec(), vspec(), vspec()],
@@ -428,25 +421,23 @@
     mine, texts, pooled = lax.optimization_barrier((mine, texts, pooled))
     other = swapped(mine, 1)
     if ranks > 2:
-        side = swapped(texts, SIDE_BIT)
-    full, unit, inv_norm, sent = call(
+        flank = swapped(texts, SIDE_BIT)
+    full, sent = call(
         image_body,
         [
             (shape((STASH_ROWS, width), BF16), hspec()),
-            (shape((slots, width), F32), vspec()),
-            (shape((slots, 128), F32), vspec()),
             (shape((peers, heads + slots, width), BF16), vspec()),
         ],
         [vspec()] * 3,
         400_000_000,
         6_000_000,
-        [pltpu.VMEM((width, width), BF16), dma(())],
+        [pltpu.VMEM((width + UNIT_ROWS, width), BF16), dma((2,))],
         name="image",
         limit=VMEM_IMAGE,
     )(mine, other, pooled)
     if ranks > 2:
-        unit, side = lax.optimization_barrier((unit, side))
-        texts = jnp.concatenate([texts, side], axis=0)
+        full, flank = lax.optimization_barrier((full, flank))
+        texts = jnp.concatenate([texts, flank], axis=0)
     got = lax.all_to_all(sent, "fsdp", 0, 0, tiled=True)
     texts = jnp.concatenate([texts, swapped(texts, CORE_BIT)], axis=0)
     count = peers * slots
@@ -484,39 +475,32 @@
     )(coefficient, images)
     if ranks > 2:
         keep, send = fold(keep, send, CORE_BIT)
-    d_image_got, keep, send = lax.optimization_barrier((d_image_got, keep, send))
     if ranks > 2:
         keep, send = fold(keep, send, SIDE_BIT)
 
+    const = jnp.concatenate([probe.astype(F32), jnp.broadcast_to(gain, (8, width))], axis=0)
     outgoing = call(
         back_body,
         [(shape((peers, rows + 16, width), BF16), hspec())],
-        [sspec()] + [hspec()] * 10,
+        [sspec()] + [hspec()] * 6,
         500_000_000,
         8_000_000,
         [
             pltpu.VMEM((peers, slots, width), BF16),
-            pltpu.VMEM((slots, width), F32),
+            pltpu.VMEM((width + UNIT_ROWS, width), BF16),
+            pltpu.VMEM((slots, rows, width), BF16),
+            pltpu.VMEM((slots * rows, 2 * lanes), F32),
+            pltpu.VMEM((heads + 8, width), F32),
             pltpu.VMEM((slots, 128), F32),
-            pltpu.VMEM((heads, width), BF16),
-            pltpu.VMEM((1, width), F32),
-            pltpu.VMEM((slots, 128), F32),
-            pltpu.VMEM((width, width), BF16),
-            pltpu.VMEM((slots, rows, width), BF16),
-            pltpu.VMEM((slots * rows, lanes), F32),
-            pltpu.VMEM((slots * rows, lanes), F32),
             pltpu.VMEM((slots * rows, width), F32),
             pltpu.VMEM((slots * rows, width), BF16),
             pltpu.VMEM((2 * lanes, width), BF16),
             pltpu.VMEM((peers, rows + 16, width), BF16),
-            dma((slots + 8,)),
-            dma((6,)),
+            dma((12,)),
         ],
         name="back",
         limit=VMEM_LARGE,
-    )(
-        owners[0], d_image_got, unit, inv_norm, full, patches, stats, weights, probe, gain, loss_sums
-    )[0]
+    )(owners[0], d_image_got, full, patches, side, const, loss_sums)[0]
     outgoing, keep, send = lax.optimization_barrier((outgoing, keep, send))
     arrived = lax.all_to_all(outgoing, "fsdp", 0, 0, tiled=True)
     if ranks > 2:
@@ -528,10 +512,9 @@
             1_000_000,
             name="split",
         )(keep, swapped(send, NEXT_BIT))
-        for block, bit in zip(blocks, Z_BITS):
-            d_caption = d_caption + swapped(block, bit).astype(F32)
+        blocks = [swapped(block, bit) for block, bit in zip(blocks, Z_BITS)]
     else:
-        d_caption = keep + swapped(send, CORE_BIT).astype(F32)
+        d_caption, blocks = keep, [swapped(send, CORE_BIT)]
 
     pooled_got = (
         got[:, :heads]
@@ -560,6 +543,9 @@
         name="last",
     )(arrived, pooled_got)
 
+    loss_part, blocks = lax.optimization_barrier((loss_part, blocks))
+    for block in blocks:
+        d_caption = d_caption + block.astype(F32)
     text_grad = (
         (d_caption - caption_unit * jnp.sum(d_caption * caption_unit, axis=-1, keepdims=True))
         * caption_inv[:, 0:1]

time: 103 us -> 98.9 us (0.960); the launches traced: 101 us -> 98.2 us
  waiting for transfers between devices: 35.5 us -> 33.7 us
  Pallas kernels: 16.5 us -> 15.4 us
    ppermute x12, waiting for transfers between devices: 15.6 us -> 9.13 us  [swapped(): lax.ppermute(block, 'dp', [(i, i ^ bit) for i in range(lax.axis_size('dp'...]
    all_to_all x1, waiting for transfers between devices: 0.01 us -> 6.15 us  [local(): arrived = lax.all_to_all(outgoing, 'fsdp', 0, 0, tiled=True)]
    all_to_all x1, waiting for transfers between devices: 8.4 us -> 6.57 us  [local(): d_image_got = lax.all_to_all(d_image_part, 'fsdp', 0, 0, tiled=True)]
    pallas_call x1, Pallas kernels: 7.21 us -> 6.04 us  [local(): call(back_body, [(shape((peers, rows + 16, width), BF16), hspec())], [ssp...]
    unnamed x28 -> x20, local copies, waits for them, and re-layouts: 3.18 us -> 2.64 us
  transfers between devices with their start and end apart: 16 -> 16, of which waited for: 9 -> 10; matrix products, arithmetic and copies ran while one was open for 2% -> 2% of each run, Pallas kernels for 12% -> 13%
where the time goes in v4:
time: 98.9 us; the launch traced here: 98.2 us
  starting transfers between devices  40.7 us (41%)
  waiting for transfers between devices  33.7 us (34%)
  Pallas kernels  15.4 us (16%)
  local copies, waits for them, and re-layouts  4.7 us (5%)
  between operations  2.18 us (2%)
  other arithmetic  1.65 us (2%)
    ppermute x12, starting transfers between devices, swapped(): lax.ppermute(block, 'dp', [(i, i ^ bit) for i in range(lax.axis_size('dp'...  22.2 us
    all_to_all x1, waiting for transfers between devices, local(): got = lax.all_to_all(sent, 'fsdp', 0, 0, tiled=True)  9.88 us
    ppermute x12, waiting for transfers between devices, swapped(): lax.ppermute(block, 'dp', [(i, i ^ bit) for i in range(lax.axis_size('dp'...  9.13 us
    all_to_all x1, waiting for transfers between devices, local(): d_image_got = lax.all_to_all(d_image_part, 'fsdp', 0, 0, tiled=True)  6.57 us
    all_to_all x1, starting transfers between devices, local(): lax.all_to_all(jnp.broadcast_to(part[None], (peers, SEND_ROWS, width)), '...  6.18 us
    all_to_all x1, waiting for transfers between devices, local(): arrived = lax.all_to_all(outgoing, 'fsdp', 0, 0, tiled=True)  6.15 us
    pallas_call x1, Pallas kernels, local(): call(back_body, [(shape((peers, rows + 16, width), BF16), hspec())], [ssp...  6.04 us
    all_to_all x1, starting transfers between devices, local(): got = lax.all_to_all(sent, 'fsdp', 0, 0, tiled=True)  5.35 us
  transfers between devices with their start and end apart: 16, of which 10 were waited for; matrix products, arithmetic and copies ran while one was open for 2% of the time, Pallas kernels for 13%

profile of v4, /device:TPU:2, one launch (start us, length us, event | category | flops | bytes accessed | tf_op | source)
XLA Modules:
  0.0 98.2 jit_solution(5700394643221236819)
XLA Ops:
  2.8 6.2 %all-to-all-start = ((bf16[8,72,1152]{2,1,0:T(8,128)(2,1)}), bf16[8,72,1152]{2,1,0:T(8,128)(2,1)S(1)}, u32[]{:S(2)}, u32[]{:S(2)}) async-start(bf16[8,72,1152]{2,1,0:T(8,128)(2,1)} %broadcast_in_dim.8), calls=%async_computation | async-start | bytes 2654208 | tf_op jit(solution)/shard_map/all_to_all | solution.py:388
  9.1 7.2 %collective-permute-start = (bf16[8,1152]{1,0:T(8,128)(2,1)S(1)}, bf16[8,1152]{1,0:T(8,128)(2,1)S(1)}, u32[]{:S(2)}, u32[]{:S(2)}) collective-permute-start(bf16[8,1152]{1,0:T(8,128)(2,1)S(1)} %get-tuple-element.44), channel_id=1, source_target_pairs={{0,64},{8,72},{16,80},{24,88},{32,96},{40,104},{48,112},{56,120},{... | collective-permute-start | bytes 55304 | tf_op jit(solution)/shard_map/ppermute | solution.py:27
  16.3 1.7 %collective-permute-done = bf16[8,1152]{1,0:T(8,128)(2,1)S(1)} collective-permute-done((bf16[8,1152]{1,0:T(8,128)(2,1)S(1)}, bf16[8,1152]{1,0:T(8,128)(2,1)S(1)}, u32[]{:S(2)}, u32[]{:S(2)}) %collective-permute-start) | collective-permute-done | bytes 18464 | tf_op jit(solution)/shard_map/ppermute | solution.py:27
  18.1 2.0 %collective-permute-start.1 = (bf16[16,1152]{1,0:T(8,128)(2,1)S(1)}, bf16[16,1152]{1,0:T(8,128)(2,1)S(1)}, u32[]{:S(2)}, u32[]{:S(2)}) collective-permute-start(bf16[16,1152]{1,0:T(8,128)(2,1)S(1)} %pad_maximum_fusion.5), channel_id=1, source_target_pairs={{0,32},{8,40},{16,48},{24,56},{32,0},{40,8},{48,16},{56,24},{64,96... | collective-permute-start | bytes 110600 | tf_op jit(solution)/shard_map/ppermute | solution.py:27
  20.1 2.8 %collective-permute-done.1 = bf16[16,1152]{1,0:T(8,128)(2,1)S(1)} collective-permute-done((bf16[16,1152]{1,0:T(8,128)(2,1)S(1)}, bf16[16,1152]{1,0:T(8,128)(2,1)S(1)}, u32[]{:S(2)}, u32[]{:S(2)}) %collective-permute-start.1) | collective-permute-done | bytes 36896 | tf_op jit(solution)/shard_map/ppermute | solution.py:27
  24.0 2.1 %pool.1 = (f32[384,256]{1,0:T(8,128)S(1)}, bf16[128,1152]{1,0:T(8,128)(2,1)S(1)}) custom-call(s32[8]{0:T(128)S(1)} %bitcast.21, s32[8]{0:T(128)S(1)} %bitcast.22, bf16[8,48,1152]{2,1,0:T(8,128)(2,1)S(1)} %bitcast.17, f32[1,1152]{1,0:T(1,128)S(1)} %reshape.28.gain_ref, bf16[16,1152]{1,0:T(8,128)(2,1)S(1)} %bitcast.19), custom_call_target="tpu_custom_call" | custom-call | flops 40000000 | bytes 4000000 | tf_op jit(solution)/shard_map/pool/pallas_call | solution.py:393
  27.3 1.9 %all-to-all-done.mine_ref = bf16[8,72,1152]{2,1,0:T(8,128)(2,1)S(1)} async-done(((bf16[8,72,1152]{2,1,0:T(8,128)(2,1)}), bf16[8,72,1152]{2,1,0:T(8,128)(2,1)S(1)}, u32[]{:S(2)}, u32[]{:S(2)}) %all-to-all-start) | async-done | bytes 1327136 | tf_op jit(solution)/shard_map/all_to_all | solution.py:388
  29.3 1.4 %collective-permute-start.4 = (bf16[64,1152]{1,0:T(8,128)(2,1)S(1)}, bf16[64,1152]{1,0:T(8,128)(2,1)S(1)}, u32[]{:S(2)}, u32[]{:S(2)}) collective-permute-start(bf16[64,1152]{1,0:T(8,128)(2,1)S(1)} %pad_maximum_fusion.2), channel_id=1, source_target_pairs={{0,128},{8,136},{16,144},{24,152},{32,160},{40,168},{48,176},{56,1... | collective-permute-start | bytes 442376 | tf_op jit(solution)/shard_map/ppermute | solution.py:27
  30.7 1.6 %collective-permute-done.3.other_ref = bf16[8,72,1152]{2,1,0:T(8,128)(2,1)S(1)} collective-permute-done((bf16[8,72,1152]{2,1,0:T(8,128)(2,1)S(1)}, bf16[8,72,1152]{2,1,0:T(8,128)(2,1)S(1)}, u32[]{:S(2)}, u32[]{:S(2)}) %collective-permute-start.3) | collective-permute-done | bytes 1327136 | tf_op jit(solution)/shard_map/ppermute | solution.py:27
  32.3 3.1 %image.1 = (bf16[15616,1152]{1,0:T(8,128)(2,1)}, bf16[8,24,1152]{2,1,0:T(8,128)(2,1)}) custom-call(bf16[8,72,1152]{2,1,0:T(8,128)(2,1)S(1)} %all-to-all-done.mine_ref, bf16[8,72,1152]{2,1,0:T(8,128)(2,1)S(1)} %collective-permute-done.3.other_ref, bf16[128,1152]{1,0:T(8,128)(2,1)S(1)} %get-tuple-element.47.a_ref), custom_call_target="tpu_custom_call" | custom-call | flops 400000000 | bytes 6000000 | tf_op jit(solution)/shard_map/image/pallas_call | solution.py:425
  35.7 5.4 %all-to-all-start.1 = ((bf16[8,24,1152]{2,1,0:T(8,128)(2,1)}), bf16[8,24,1152]{2,1,0:T(8,128)(2,1)S(1)}, u32[]{:S(2)}, u32[]{:S(2)}) async-start(bf16[8,24,1152]{2,1,0:T(8,128)(2,1)} %get-tuple-element.48), calls=%async_computation.1 | async-start | bytes 884736 | tf_op jit(solution)/shard_map/all_to_all | solution.py:441
  42.5 9.9 %all-to-all-done.1.got_ref = bf16[8,24,1152]{2,1,0:T(8,128)(2,1)S(1)} async-done(((bf16[8,24,1152]{2,1,0:T(8,128)(2,1)}), bf16[8,24,1152]{2,1,0:T(8,128)(2,1)S(1)}, u32[]{:S(2)}, u32[]{:S(2)}) %all-to-all-start.1) | async-done | bytes 442400 | tf_op jit(solution)/shard_map/all_to_all | solution.py:441
  52.4 1.9 %pair.1 = (bf16[8,8,1152]{2,1,0:T(8,128)(2,1)}, bf16[64,256]{1,0:T(8,128)(2,1)S(1)}, bf16[64,1152]{1,0:T(8,128)(2,1)S(1)}, f32[8,128]{1,0:T(8,128)S(1)}) custom-call(s32[1]{0:T(128)} %bitcast.1.place, f32[2]{0:T(128)S(1)} %pad_maximum_fusion.6.scalars, bf16[8,24,1152]{2,1,0:T(8,128)(2,1)S(1)} %all-to-all-done.1.got_ref, ...), custom_call_target="tpu_custom_call" | custom-call | flops 80000000 | bytes 2000000 | tf_op jit(solution)/shard_map/pair/pallas_call | solution.py:445
  54.8 3.4 %all-to-all-start.2 = ((bf16[8,8,1152]{2,1,0:T(8,128)(2,1)}), bf16[8,8,1152]{2,1,0:T(8,128)(2,1)S(1)}, u32[]{:S(2)}, u32[]{:S(2)}) async-start(bf16[8,8,1152]{2,1,0:T(8,128)(2,1)} %get-tuple-element.52), calls=%async_computation.2 | async-start | bytes 294912 | tf_op jit(solution)/shard_map/all_to_all | solution.py:458
  58.3 1.5 %collective-permute-start.7 = (bf16[64,1152]{1,0:T(8,128)(2,1)S(1)}, bf16[64,1152]{1,0:T(8,128)(2,1)S(1)}, u32[]{:S(2)}, u32[]{:S(2)}) collective-permute-start(bf16[64,1152]{1,0:T(8,128)(2,1)S(1)} %get-tuple-element.61), channel_id=1, source_target_pairs={{0,128},{8,136},{16,144},{24,152},{32,160},{40,168},{48,176},{56,1... | collective-permute-start | bytes 442376 | tf_op jit(solution)/shard_map/ppermute | solution.py:27
  60.5 6.6 %all-to-all-done.2.got_in = bf16[8,8,1152]{2,1,0:T(8,128)(2,1)S(1)} async-done(((bf16[8,8,1152]{2,1,0:T(8,128)(2,1)}), bf16[8,8,1152]{2,1,0:T(8,128)(2,1)S(1)}, u32[]{:S(2)}, u32[]{:S(2)}) %all-to-all-start.2) | async-done | bytes 147488 | tf_op jit(solution)/shard_map/all_to_all | solution.py:458
  67.7 6.0 %back.1 = bf16[8,64,1152]{2,1,0:T(8,128)(2,1)} custom-call(s32[8]{0:T(128)} %bitcast.20, bf16[8,8,1152]{2,1,0:T(8,128)(2,1)} %copy-done.8, bf16[15616,1152]{1,0:T(8,128)(2,1)} %get-tuple-element.53.full_in, bf16[1,8,48,1152]{3,2,1,0:T(8,128)(2,1)} %x_in.1, f32[384,256]{1,0:T(8,128)} %copy-done.2, f32[24,1152]{1,0:T(8,128)} %pad_maximum_fusion.3.const_in, ...), custom_call_target="tpu_custom_call" | custom-call | flops 500000000 | bytes 8000000 | tf_op jit(solution)/shard_map/back/pallas_call | solution.py:482
  73.8 3.6 %all-to-all-start.3 = ((bf16[8,64,1152]{2,1,0:T(8,128)(2,1)}), bf16[8,64,1152]{2,1,0:T(8,128)(2,1)S(1)}, u32[]{:S(2)}, u32[]{:S(2)}) async-start(bf16[8,64,1152]{2,1,0:T(8,128)(2,1)} %back.1), calls=%async_computation.3 | async-start | bytes 2359296 | tf_op jit(solution)/shard_map/all_to_all | solution.py:505
  77.4 1.3 %collective-permute-start.8 = (bf16[32,1152]{1,0:T(8,128)(2,1)S(1)}, bf16[32,1152]{1,0:T(8,128)(2,1)S(1)}, u32[]{:S(2)}, u32[]{:S(2)}) collective-permute-start(bf16[32,1152]{1,0:T(8,128)(2,1)S(1)} %get-tuple-element.67), channel_id=1, source_target_pairs={{0,16},{8,24},{16,0},{24,8},{32,48},{40,56},{48,32},{56,40},{64,80... | collective-permute-start | bytes 221192 | tf_op jit(solution)/shard_map/ppermute | solution.py:27
  79.6 2.5 %collective-permute-done.8.got_ref = bf16[32,1152]{1,0:T(8,128)(2,1)S(1)} collective-permute-done((bf16[32,1152]{1,0:T(8,128)(2,1)S(1)}, bf16[32,1152]{1,0:T(8,128)(2,1)S(1)}, u32[]{:S(2)}, u32[]{:S(2)}) %collective-permute-start.8) | collective-permute-done | bytes 73760 | tf_op jit(solution)/shard_map/ppermute | solution.py:27
  82.1 2.6 %collective-permute-start.10 = (bf16[8,1152]{1,0:T(8,128)(2,1)S(1)}, bf16[8,1152]{1,0:T(8,128)(2,1)S(1)}, u32[]{:S(2)}, u32[]{:S(2)}) collective-permute-start(bf16[8,1152]{1,0:T(8,128)(2,1)S(1)} %get-tuple-element.69), channel_id=1, source_target_pairs={{0,32},{8,40},{16,48},{24,56},{32,0},{40,8},{48,16},{56,24},{64,96... | collective-permute-start | bytes 55304 | tf_op jit(solution)/shard_map/ppermute | solution.py:27
  84.7 4.0 %collective-permute-start.11 = (bf16[8,1152]{1,0:T(8,128)(2,1)S(1)}, bf16[8,1152]{1,0:T(8,128)(2,1)S(1)}, u32[]{:S(2)}, u32[]{:S(2)}) collective-permute-start(bf16[8,1152]{1,0:T(8,128)(2,1)S(1)} %get-tuple-element.70), channel_id=1, source_target_pairs={{0,96},{8,104},{16,112},{24,120},{32,64},{40,72},{48,80},{56,88},{... | collective-permute-start | bytes 55304 | tf_op jit(solution)/shard_map/ppermute | solution.py:27
  89.6 6.1 %all-to-all-done.3.refs_0_ = bf16[8,64,1152]{2,1,0:T(8,128)(2,1)S(1)} async-done(((bf16[8,64,1152]{2,1,0:T(8,128)(2,1)}), bf16[8,64,1152]{2,1,0:T(8,128)(2,1)S(1)}, u32[]{:S(2)}, u32[]{:S(2)}) %all-to-all-start.3) | async-done | bytes 1179680 | tf_op jit(solution)/shard_map/all_to_all | solution.py:505
  95.7 1.7 %last.1 = (bf16[1,8,48,1152]{3,2,1,0:T(8,128)(2,1)}, bf16[1,144,1152]{2,1,0:T(8,128)(2,1)}, bf16[16,144]{1,0:T(8,128)(2,1)}, bf16[1,144]{1,0:T(2,128)(2,1)}, f32[1,1]{1,0:T(1,128)}) custom-call(bf16[8,64,1152]{2,1,0:T(8,128)(2,1)S(1)} %all-to-all-done.3.refs_0_, bf16[16,64,144]{2,1,0:T(8,128)(2,1)S(1)} %bitcast.18), custom_call_target="tpu_custom_call" | custom-call | flops 400000000 | bytes 3000000 | tf_op jit(solution)/shard_map/last/pallas_call | solution.py:530
  (56 shorter events, 9.5 us)
Async XLA Ops:
  0.6 1.0 copy-start
  2.8 6.2 %copy-start.7 = (bf16[1,8,1152]{2,1,0:T(8,128)(2,1)S(1)}, bf16[1,8,1152]{2,1,0:T(8,128)(2,1)}, u32[]{:S(2)}) copy-start(bf16[1,8,1152]{2,1,0:T(8,128)(2,1)} %param.12) | copy-start | bytes 55300
  2.8 21.2 %copy-start.9 = (f32[1152]{0:T(1024)S(1)}, f32[1152]{0:T(1024)}, u32[]{:S(2)}) copy-start(f32[1152]{0:T(1024)} %param.13) | copy-start | bytes 13828
  2.8 21.2 %copy-start.1 = (bf16[1,8,48,1152]{3,2,1,0:T(8,128)(2,1)S(1)}, bf16[1,8,48,1152]{3,2,1,0:T(8,128)(2,1)}, u32[]{:S(2)}) copy-start(bf16[1,8,48,1152]{3,2,1,0:T(8,128)(2,1)} %x_in.1) | copy-start | bytes 2654212
  2.8 21.2 %copy-start.3 = (bf16[1152,16]{0,1:T(8,128)(2,1)S(1)}, bf16[1152,16]{0,1:T(8,128)(2,1)}, u32[]{:S(2)}) copy-start(bf16[1152,16]{0,1:T(8,128)(2,1)} %param.14) | copy-start | bytes 110596
  2.8 21.2 %copy-start.5 = (s32[1,8]{1,0:T(1,128)S(1)}, s32[1,8]{1,0:T(1,128)}, u32[]{:S(2)}) copy-start(s32[1,8]{1,0:T(1,128)} %param.11) | copy-start | bytes 100
  2.8 21.2 %copy-start.6 = (s32[1,8]{1,0:T(1,128)S(1)}, s32[1,8]{1,0:T(1,128)}, u32[]{:S(2)}) copy-start(s32[1,8]{1,0:T(1,128)} %param.10) | copy-start | bytes 100
  2.8 26.4 %all-to-all-start = ((bf16[8,72,1152]{2,1,0:T(8,128)(2,1)}), bf16[8,72,1152]{2,1,0:T(8,128)(2,1)S(1)}, u32[]{:S(2)}, u32[]{:S(2)}) async-start(bf16[8,72,1152]{2,1,0:T(8,128)(2,1)} %broadcast_in_dim.8), calls=%async_computation | async-start | bytes 2654208 | tf_op jit(solution)/shard_map/all_to_all | solution.py:388
  9.1 8.9 %collective-permute-start = (bf16[8,1152]{1,0:T(8,128)(2,1)S(1)}, bf16[8,1152]{1,0:T(8,128)(2,1)S(1)}, u32[]{:S(2)}, u32[]{:S(2)}) collective-permute-start(bf16[8,1152]{1,0:T(8,128)(2,1)S(1)} %get-tuple-element.44), channel_id=1, source_target_pairs={{0,64},{8,72},{16,80},{24,88},{32,96},{40,104},{48,112},{56,120},{... | collective-permute-start | bytes 55304 | tf_op jit(solution)/shard_map/ppermute | solution.py:27
  18.1 4.9 %collective-permute-start.1 = (bf16[16,1152]{1,0:T(8,128)(2,1)S(1)}, bf16[16,1152]{1,0:T(8,128)(2,1)S(1)}, u32[]{:S(2)}, u32[]{:S(2)}) collective-permute-start(bf16[16,1152]{1,0:T(8,128)(2,1)S(1)} %pad_maximum_fusion.5), channel_id=1, source_target_pairs={{0,32},{8,40},{16,48},{24,56},{32,0},{40,8},{48,16},{56,24},{64,96... | collective-permute-start | bytes 110600 | tf_op jit(solution)/shard_map/ppermute | solution.py:27
  22.9 4.4 %collective-permute-start.2 = (bf16[32,1152]{1,0:T(8,128)(2,1)S(1)}, bf16[32,1152]{1,0:T(8,128)(2,1)S(1)}, u32[]{:S(2)}, u32[]{:S(2)}) collective-permute-start(bf16[32,1152]{1,0:T(8,128)(2,1)S(1)} %pad_maximum_fusion.4), channel_id=1, source_target_pairs={{0,16},{8,24},{16,0},{24,8},{32,48},{40,56},{48,32},{56,40},{64,80... | collective-permute-start | bytes 221192 | tf_op jit(solution)/shard_map/ppermute | solution.py:27
  26.1 0.8 copy-start.2
  29.3 3.1 %collective-permute-start.3 = (bf16[8,72,1152]{2,1,0:T(8,128)(2,1)S(1)}, bf16[8,72,1152]{2,1,0:T(8,128)(2,1)S(1)}, u32[]{:S(2)}, u32[]{:S(2)}) collective-permute-start(bf16[8,72,1152]{2,1,0:T(8,128)(2,1)S(1)} %all-to-all-done.mine_ref), channel_id=1, source_target_pairs={{0,8},{8,0},{16,24},{24,16},{32,40},{40,32},{48,56},{56,48},{64,72... | collective-permute-start | bytes 3981320 | tf_op jit(solution)/shard_map/ppermute | solution.py:27
  29.3 6.3 %collective-permute-start.4 = (bf16[64,1152]{1,0:T(8,128)(2,1)S(1)}, bf16[64,1152]{1,0:T(8,128)(2,1)S(1)}, u32[]{:S(2)}, u32[]{:S(2)}) collective-permute-start(bf16[64,1152]{1,0:T(8,128)(2,1)S(1)} %pad_maximum_fusion.2), channel_id=1, source_target_pairs={{0,128},{8,136},{16,144},{24,152},{32,160},{40,168},{48,176},{56,1... | collective-permute-start | bytes 442376 | tf_op jit(solution)/shard_map/ppermute | solution.py:27
  35.5 6.9 %collective-permute-start.5 = (bf16[128,1152]{1,0:T(8,128)(2,1)S(1)}, bf16[128,1152]{1,0:T(8,128)(2,1)S(1)}, u32[]{:S(2)}, u32[]{:S(2)}) collective-permute-start(bf16[128,1152]{1,0:T(8,128)(2,1)S(1)} %pad_maximum_fusion.1), channel_id=1, source_target_pairs={{0,8},{8,0},{16,24},{24,16},{32,40},{40,32},{48,56},{56,48},{64,72... | collective-permute-start | bytes 884744 | tf_op jit(solution)/shard_map/ppermute | solution.py:27
  35.7 16.7 %all-to-all-start.1 = ((bf16[8,24,1152]{2,1,0:T(8,128)(2,1)}), bf16[8,24,1152]{2,1,0:T(8,128)(2,1)S(1)}, u32[]{:S(2)}, u32[]{:S(2)}) async-start(bf16[8,24,1152]{2,1,0:T(8,128)(2,1)} %get-tuple-element.48), calls=%async_computation.1 | async-start | bytes 884736 | tf_op jit(solution)/shard_map/all_to_all | solution.py:441
  54.8 3.4 %collective-permute-start.6 = (bf16[128,1152]{1,0:T(8,128)(2,1)S(1)}, bf16[128,1152]{1,0:T(8,128)(2,1)S(1)}, u32[]{:S(2)}, u32[]{:S(2)}) collective-permute-start(bf16[128,1152]{1,0:T(8,128)(2,1)S(1)} %get-tuple-element.59), channel_id=1, source_target_pairs={{0,8},{8,0},{16,24},{24,16},{32,40},{40,32},{48,56},{56,48},{64,72... | collective-permute-start | bytes 884744 | tf_op jit(solution)/shard_map/ppermute | solution.py:27
  54.8 12.2 %all-to-all-start.2 = ((bf16[8,8,1152]{2,1,0:T(8,128)(2,1)}), bf16[8,8,1152]{2,1,0:T(8,128)(2,1)S(1)}, u32[]{:S(2)}, u32[]{:S(2)}) async-start(bf16[8,8,1152]{2,1,0:T(8,128)(2,1)} %get-tuple-element.52), calls=%async_computation.2 | async-start | bytes 294912 | tf_op jit(solution)/shard_map/all_to_all | solution.py:458
  58.3 15.5 %collective-permute-start.7 = (bf16[64,1152]{1,0:T(8,128)(2,1)S(1)}, bf16[64,1152]{1,0:T(8,128)(2,1)S(1)}, u32[]{:S(2)}, u32[]{:S(2)}) collective-permute-start(bf16[64,1152]{1,0:T(8,128)(2,1)S(1)} %get-tuple-element.61), channel_id=1, source_target_pairs={{0,128},{8,136},{16,144},{24,152},{32,160},{40,168},{48,176},{56,1... | collective-permute-start | bytes 442376 | tf_op jit(solution)/shard_map/ppermute | solution.py:27
  73.8 21.9 %all-to-all-start.3 = ((bf16[8,64,1152]{2,1,0:T(8,128)(2,1)}), bf16[8,64,1152]{2,1,0:T(8,128)(2,1)S(1)}, u32[]{:S(2)}, u32[]{:S(2)}) async-start(bf16[8,64,1152]{2,1,0:T(8,128)(2,1)} %back.1), calls=%async_computation.3 | async-start | bytes 2359296 | tf_op jit(solution)/shard_map/all_to_all | solution.py:505
  77.4 4.6 %collective-permute-start.8 = (bf16[32,1152]{1,0:T(8,128)(2,1)S(1)}, bf16[32,1152]{1,0:T(8,128)(2,1)S(1)}, u32[]{:S(2)}, u32[]{:S(2)}) collective-permute-start(bf16[32,1152]{1,0:T(8,128)(2,1)S(1)} %get-tuple-element.67), channel_id=1, source_target_pairs={{0,16},{8,24},{16,0},{24,8},{32,48},{40,56},{48,32},{56,40},{64,80... | collective-permute-start | bytes 221192 | tf_op jit(solution)/shard_map/ppermute | solution.py:27
  82.1 15.3 %collective-permute-start.10 = (bf16[8,1152]{1,0:T(8,128)(2,1)S(1)}, bf16[8,1152]{1,0:T(8,128)(2,1)S(1)}, u32[]{:S(2)}, u32[]{:S(2)}) collective-permute-start(bf16[8,1152]{1,0:T(8,128)(2,1)S(1)} %get-tuple-element.69), channel_id=1, source_target_pairs={{0,32},{8,40},{16,48},{24,56},{32,0},{40,8},{48,16},{56,24},{64,96... | collective-permute-start | bytes 55304 | tf_op jit(solution)/shard_map/ppermute | solution.py:27
  84.7 12.7 %collective-permute-start.11 = (bf16[8,1152]{1,0:T(8,128)(2,1)S(1)}, bf16[8,1152]{1,0:T(8,128)(2,1)S(1)}, u32[]{:S(2)}, u32[]{:S(2)}) collective-permute-start(bf16[8,1152]{1,0:T(8,128)(2,1)S(1)} %get-tuple-element.70), channel_id=1, source_target_pairs={{0,96},{8,104},{16,112},{24,120},{32,64},{40,72},{48,80},{56,88},{... | collective-permute-start | bytes 55304 | tf_op jit(solution)/shard_map/ppermute | solution.py:27
  88.6 8.8 %collective-permute-start.9 = (bf16[8,1152]{1,0:T(8,128)(2,1)S(1)}, bf16[8,1152]{1,0:T(8,128)(2,1)S(1)}, u32[]{:S(2)}, u32[]{:S(2)}) collective-permute-start(bf16[8,1152]{1,0:T(8,128)(2,1)S(1)} %get-tuple-element.68), channel_id=1, source_target_pairs={{0,64},{8,72},{16,80},{24,88},{32,96},{40,104},{48,112},{56,120},{... | collective-permute-start | bytes 55304 | tf_op jit(solution)/shard_map/ppermute | solution.py:27
  (2 other events, 1.3 us)

commit v5 on v4

--- a/solution.py
+++ b/solution.py
@@ -14,7 +14,7 @@
 VMEM_LIMIT = 16 * 1024 * 1024
 VMEM_LARGE = 60_000_000
 VMEM_IMAGE = 28_000_000
-UNIT_ROWS = 48
+KEPT_ROWS = 96
 STASH_ROWS = 15_616
 SEND_ROWS = 72
 
@@ -112,7 +112,7 @@
 
 
 def image_body(
-    mine_ref, other_ref, a_ref, full_out, out_ref, full, sems
+    mine_ref, other_ref, a_ref, gain_ref, probe_ref, full_out, out_ref, full, sems
 ):
     shards, part_rows, width = mine_ref.shape
     slots = shards
@@ -136,7 +136,7 @@
 
     copies = [
         pltpu.make_async_copy(full.at[at, :], full_out.at[at, :], sems.at[k])
-        for k, at in enumerate([pl.ds(0, width), pl.ds(width, UNIT_ROWS)])
+        for k, at in enumerate([pl.ds(0, width), pl.ds(width, KEPT_ROWS)])
     ]
     copies[0].start()
     pooled = a_ref[...]
@@ -145,6 +145,8 @@
     inv = lax.rsqrt(jnp.sum(context * context, axis=-1, keepdims=True) + epsilon)
     unit = context * inv
     kept = terms(unit) + terms(jnp.broadcast_to(inv, unit.shape))
+    kept += terms(jnp.broadcast_to(gain_ref[...], unit.shape)) + [jnp.zeros_like(unit)]
+    kept += [probe_ref[...].astype(F32)]
     full[width:, :] = jnp.concatenate(kept, axis=0).astype(BF16)
     copies[1].start()
     wide_pooled = pooled.astype(F32)
@@ -222,9 +224,18 @@
         block_ref[...] = total[(k + 1) * rows : (k + 2) * rows].astype(BF16)
 
 
+def finish_body(total_ref, unit_ref, inv_ref, *refs):
+    d_caption = total_ref[...]
+    for block_ref in refs[:-1]:
+        d_caption = d_caption + block_ref[...].astype(F32)
+    unit = unit_ref[...]
+    along = jnp.sum(d_caption * unit, axis=-1, keepdims=True)
+    refs[-1][...] = ((d_caption - unit * along) * inv_ref[:, 0:1]).astype(BF16)
+
+
 def back_body(
-    owners, got_in, full_in, x_in, side_in, const_in, loss_in, out_ref,
-    got_ref, full, x_ref, side_ref, const_ref, loss_ref, normed_ref, scaled_ref, right, result, sems,
+    owners_in, got_in, full_in, x_in, side_in, loss_in, out_ref,
+    owners, got_ref, full, x_ref, side_ref, loss_ref, normed_ref, scaled_ref, right, result, sems,
 ):
     slots, rows, width = x_ref.shape
     lanes = side_ref.shape[1] // 2
@@ -232,12 +243,12 @@
     cut = width // slots
     scale = 1.0 / math.sqrt(width // heads)
     chunk = width // 3
-    rows_of = [pl.ds(width, UNIT_ROWS)] + [pl.ds(c * chunk, chunk) for c in range(3)]
+    rows_of = [pl.ds(width, KEPT_ROWS)] + [pl.ds(c * chunk, chunk) for c in range(3)]
     pairs = [
         (full_in.at[rows_of[0], :], full.at[rows_of[0], :]),
         (got_in, got_ref),
+        (owners_in, owners),
         (side_in, side_ref),
-        (const_in, const_ref),
         (x_in.at[0], x_ref),
     ]
     pairs += [(full_in.at[at, :], full.at[at, :]) for at in rows_of[1:]]
@@ -251,16 +262,18 @@
     copies[1].wait()
     d_image = jnp.sum(got_ref[...].astype(F32), axis=0)
     kept = full[width:, :].astype(F32)
-    unit = kept[0:slots] + kept[slots : 2 * slots] + kept[2 * slots : 3 * slots]
-    inv_norm = kept[3 * slots : 4 * slots] + kept[4 * slots : 5 * slots] + kept[5 * slots :]
+
+    def whole(first):
+        return kept[first : first + 8] + kept[first + 8 : first + 16] + kept[first + 16 : first + 24]
+
+    unit, inv_norm, gain = whole(0), whole(24), whole(48)[0:1]
     along = jnp.sum(d_image * unit, axis=-1, keepdims=True)
     d_context = (d_image - unit * along) * inv_norm
     d_context = d_context.astype(BF16).astype(F32)
+    right[lanes:, :] = jnp.concatenate([kept[80 : 80 + heads]] * slots, axis=0).astype(BF16)
     spread = (d_context[:, None, :] * head_mask(heads, width)[None]).reshape(lanes, width).astype(BF16)
     copies[2].wait()
     copies[3].wait()
-    gain = const_ref[heads : heads + 1, :]
-    right[lanes:, :] = jnp.concatenate([const_ref[0:heads, :]] * slots, axis=0).astype(BF16)
     copies[4].wait()
     for r in range(slots):
         at = slice(r * rows, (r + 1) * rows)
@@ -420,26 +433,24 @@
             texts = jnp.concatenate([texts, swapped(texts, bit)], axis=0)
     mine, texts, pooled = lax.optimization_barrier((mine, texts, pooled))
     other = swapped(mine, 1)
-    if ranks > 2:
-        flank = swapped(texts, SIDE_BIT)
+    bits = [bit for bit in (SIDE_BIT, CORE_BIT, SIDE_BIT + CORE_BIT) if bit < ranks]
+    flanks = [swapped(texts, bit) for bit in bits]
     full, sent = call(
         image_body,
         [
             (shape((STASH_ROWS, width), BF16), hspec()),
             (shape((peers, heads + slots, width), BF16), vspec()),
         ],
-        [vspec()] * 3,
+        [vspec()] * 5,
         400_000_000,
         6_000_000,
-        [pltpu.VMEM((width + UNIT_ROWS, width), BF16), dma((2,))],
+        [pltpu.VMEM((width + KEPT_ROWS, width), BF16), dma((2,))],
         name="image",
         limit=VMEM_IMAGE,
-    )(mine, other, pooled)
-    if ranks > 2:
-        full, flank = lax.optimization_barrier((full, flank))
-        texts = jnp.concatenate([texts, flank], axis=0)
+    )(mine, other, pooled, gain, probe)
+    full, flanks = lax.optimization_barrier((full, flanks))
     got = lax.all_to_all(sent, "fsdp", 0, 0, tiled=True)
-    texts = jnp.concatenate([texts, swapped(texts, CORE_BIT)], axis=0)
+    texts = jnp.concatenate([texts] + flanks, axis=0)
     count = peers * slots
     text_count = ranks * slots
     d_image_part, coefficient, images, loss_sums = call(
@@ -478,19 +489,18 @@
     if ranks > 2:
         keep, send = fold(keep, send, SIDE_BIT)
 
-    const = jnp.concatenate([probe.astype(F32), jnp.broadcast_to(gain, (8, width))], axis=0)
     outgoing = call(
         back_body,
         [(shape((peers, rows + 16, width), BF16), hspec())],
-        [sspec()] + [hspec()] * 6,
+        [hspec()] * 6,
         500_000_000,
         8_000_000,
         [
+            pltpu.SMEM((slots,), jnp.int32),
             pltpu.VMEM((peers, slots, width), BF16),
-            pltpu.VMEM((width + UNIT_ROWS, width), BF16),
+            pltpu.VMEM((width + KEPT_ROWS, width), BF16),
             pltpu.VMEM((slots, rows, width), BF16),
             pltpu.VMEM((slots * rows, 2 * lanes), F32),
-            pltpu.VMEM((heads + 8, width), F32),
             pltpu.VMEM((slots, 128), F32),
             pltpu.VMEM((slots * rows, width), F32),
             pltpu.VMEM((slots * rows, width), BF16),
@@ -499,8 +509,8 @@
             dma((12,)),
         ],
         name="back",
-        limit=VMEM_LARGE,
-    )(owners[0], d_image_got, full, patches, side, const, loss_sums)[0]
+        limit=40_000_000,
+    )(owners[0], d_image_got, full, patches, side, loss_sums)[0]
     outgoing, keep, send = lax.optimization_barrier((outgoing, keep, send))
     arrived = lax.all_to_all(outgoing, "fsdp", 0, 0, tiled=True)
     if ranks > 2:
@@ -544,12 +554,14 @@
     )(arrived, pooled_got)
 
     loss_part, blocks = lax.optimization_barrier((loss_part, blocks))
-    for block in blocks:
-        d_caption = d_caption + block.astype(F32)
-    text_grad = (
-        (d_caption - caption_unit * jnp.sum(d_caption * caption_unit, axis=-1, keepdims=True))
-        * caption_inv[:, 0:1]
-    ).astype(BF16)
+    text_grad = call(
+        finish_body,
+        [(shape((slots, width), BF16), vspec())],
+        [vspec()] * (3 + len(blocks)),
+        0,
+        0,
+        name="finish",
+    )(d_caption, caption_unit, caption_inv, *blocks)[0]
     return (loss_part, row_grad, text_grad[None], value_grad, probe_t.T[None], gain_grad)
 
 

time: 98.9 us -> 96.6 us (0.977)
  local copies, waits for them, and re-layouts: 4.7 us -> 2.92 us
  waiting for transfers between devices: 33.7 us -> 32.5 us
    unnamed x20 -> x14, local copies, waits for them, and re-layouts: 2.64 us -> 0.98 us
    all_to_all x1, waiting for transfers between devices: 9.88 us -> 8.52 us  [local(): got = lax.all_to_all(sent, 'fsdp', 0, 0, tiled=True)]
    ppermute x12 -> x13, starting transfers between devices: 22.2 us -> 22.7 us  [swapped(): lax.ppermute(block, 'dp', [(i, i ^ bit) for i in range(lax.axis_size('dp'...]
    ppermute x12 -> x13, waiting for transfers between devices: 9.13 us -> 9.24 us  [swapped(): lax.ppermute(block, 'dp', [(i, i ^ bit) for i in range(lax.axis_size('dp'...]
    pallas_call x1 -> x2, Pallas kernels: 6.04 us -> 5.98 us  [the longest x1 5.28 us: local(): call(back_body, [(shape((peers, rows + 16, width), BF16), hspec())], [hsp...]
  transfers between devices with their start and end apart: 16 -> 17, of which waited for: 10 -> 9; matrix products, arithmetic and copies ran while one was open for 2% -> 2% of each run, Pallas kernels for 13% -> 13%
where the time goes in v5:
time: 96.6 us; the launch traced here: 95.4 us
  starting transfers between devices  41.2 us (43%)
  waiting for transfers between devices  32.5 us (34%)
  Pallas kernels  15.4 us (16%)
  local copies, waits for them, and re-layouts  2.92 us (3%)
  between operations  2.16 us (2%)
  other arithmetic  1.2 us (1%)
    ppermute x13, starting transfers between devices, swapped(): lax.ppermute(block, 'dp', [(i, i ^ bit) for i in range(lax.axis_size('dp'...  22.7 us
    ppermute x13, waiting for transfers between devices, swapped(): lax.ppermute(block, 'dp', [(i, i ^ bit) for i in range(lax.axis_size('dp'...  9.24 us
    all_to_all x1, waiting for transfers between devices, local(): got = lax.all_to_all(sent, 'fsdp', 0, 0, tiled=True)  8.52 us
    all_to_all x1, waiting for transfers between devices, local(): d_image_got = lax.all_to_all(d_image_part, 'fsdp', 0, 0, tiled=True)  6.63 us
    all_to_all x1, waiting for transfers between devices, local(): arrived = lax.all_to_all(outgoing, 'fsdp', 0, 0, tiled=True)  6.21 us
    all_to_all x1, starting transfers between devices, local(): lax.all_to_all(jnp.broadcast_to(part[None], (peers, SEND_ROWS, width)), '...  6.18 us
    all_to_all x1, starting transfers between devices, local(): got = lax.all_to_all(sent, 'fsdp', 0, 0, tiled=True)  5.37 us
    pallas_call x1, Pallas kernels, local(): call(back_body, [(shape((peers, rows + 16, width), BF16), hspec())], [hsp...  5.28 us
  transfers between devices with their start and end apart: 17, of which 9 were waited for; matrix products, arithmetic and copies ran while one was open for 2% of the time, Pallas kernels for 13%

profile of v5, /device:TPU:2, one launch (start us, length us, event | category | flops | bytes accessed | tf_op | source)
XLA Modules:
  0.0 95.4 jit_solution(6354941228284147774)
XLA Ops:
  1.6 1.2 %broadcast_in_dim.12 = bf16[8,72,1152]{2,1,0:T(8,128)(2,1)} broadcast(bf16[72,1152]{1,0:T(8,128)(2,1)S(1)} %constant_dynamic-slice_fusion), dimensions={1,2} | broadcast | bytes 1492992 | tf_op jit(solution)/shard_map/broadcast_in_dim | solution.py:402
  2.8 6.2 %all-to-all-start = ((bf16[8,72,1152]{2,1,0:T(8,128)(2,1)}), bf16[8,72,1152]{2,1,0:T(8,128)(2,1)S(1)}, u32[]{:S(2)}, u32[]{:S(2)}) async-start(bf16[8,72,1152]{2,1,0:T(8,128)(2,1)} %broadcast_in_dim.12), calls=%async_computation | async-start | bytes 2654208 | tf_op jit(solution)/shard_map/all_to_all | solution.py:401
  9.1 7.2 %collective-permute-start = (bf16[8,1152]{1,0:T(8,128)(2,1)S(1)}, bf16[8,1152]{1,0:T(8,128)(2,1)S(1)}, u32[]{:S(2)}, u32[]{:S(2)}) collective-permute-start(bf16[8,1152]{1,0:T(8,128)(2,1)S(1)} %get-tuple-element.46), channel_id=1, source_target_pairs={{0,64},{8,72},{16,80},{24,88},{32,96},{40,104},{48,112},{56,120},{... | collective-permute-start | bytes 55304 | tf_op jit(solution)/shard_map/ppermute | solution.py:27
  16.3 1.7 %collective-permute-done = bf16[8,1152]{1,0:T(8,128)(2,1)S(1)} collective-permute-done((bf16[8,1152]{1,0:T(8,128)(2,1)S(1)}, bf16[8,1152]{1,0:T(8,128)(2,1)S(1)}, u32[]{:S(2)}, u32[]{:S(2)}) %collective-permute-start) | collective-permute-done | bytes 18464 | tf_op jit(solution)/shard_map/ppermute | solution.py:27
  18.1 2.0 %collective-permute-start.1 = (bf16[16,1152]{1,0:T(8,128)(2,1)S(1)}, bf16[16,1152]{1,0:T(8,128)(2,1)S(1)}, u32[]{:S(2)}, u32[]{:S(2)}) collective-permute-start(bf16[16,1152]{1,0:T(8,128)(2,1)S(1)} %pad_maximum_fusion.3), channel_id=1, source_target_pairs={{0,32},{8,40},{16,48},{24,56},{32,0},{40,8},{48,16},{56,24},{64,96... | collective-permute-start | bytes 110600 | tf_op jit(solution)/shard_map/ppermute | solution.py:27
  20.1 2.8 %collective-permute-done.1 = bf16[16,1152]{1,0:T(8,128)(2,1)S(1)} collective-permute-done((bf16[16,1152]{1,0:T(8,128)(2,1)S(1)}, bf16[16,1152]{1,0:T(8,128)(2,1)S(1)}, u32[]{:S(2)}, u32[]{:S(2)}) %collective-permute-start.1) | collective-permute-done | bytes 36896 | tf_op jit(solution)/shard_map/ppermute | solution.py:27
  24.0 2.1 %pool.1 = (f32[384,256]{1,0:T(8,128)S(1)}, bf16[128,1152]{1,0:T(8,128)(2,1)S(1)}) custom-call(s32[8]{0:T(128)S(1)} %bitcast.19, s32[8]{0:T(128)S(1)} %bitcast.21, bf16[8,48,1152]{2,1,0:T(8,128)(2,1)S(1)} %bitcast.15, f32[1,1152]{1,0:T(1,128)S(1)} %reshape.26.gain_ref, bf16[16,1152]{1,0:T(8,128)(2,1)S(1)} %bitcast.17), custom_call_target="tpu_custom_call" | custom-call | flops 40000000 | bytes 4000000 | tf_op jit(solution)/shard_map/pool/pallas_call | solution.py:406
  27.3 1.9 %all-to-all-done.mine_ref = bf16[8,72,1152]{2,1,0:T(8,128)(2,1)S(1)} async-done(((bf16[8,72,1152]{2,1,0:T(8,128)(2,1)}), bf16[8,72,1152]{2,1,0:T(8,128)(2,1)S(1)}, u32[]{:S(2)}, u32[]{:S(2)}) %all-to-all-start) | async-done | bytes 1327136 | tf_op jit(solution)/shard_map/all_to_all | solution.py:401
  29.3 1.4 %collective-permute-start.4 = (bf16[64,1152]{1,0:T(8,128)(2,1)S(1)}, bf16[64,1152]{1,0:T(8,128)(2,1)}, u32[]{:S(2)}, u32[]{:S(2)}) collective-permute-start(bf16[64,1152]{1,0:T(8,128)(2,1)S(1)} %pad_maximum_fusion.1), channel_id=1, source_target_pairs={{0,128},{8,136},{16,144},{24,152},{32,160},{40,168},{48,176},{56,1... | collective-permute-start | bytes 442376 | tf_op jit(solution)/shard_map/ppermute | solution.py:27
  32.3 2.6 %image.1 = (bf16[15616,1152]{1,0:T(8,128)(2,1)}, bf16[8,24,1152]{2,1,0:T(8,128)(2,1)}) custom-call(bf16[8,72,1152]{2,1,0:T(8,128)(2,1)S(1)} %all-to-all-done.mine_ref, bf16[8,72,1152]{2,1,0:T(8,128)(2,1)S(1)} %collective-permute-done.3.other_ref, bf16[128,1152]{1,0:T(8,128)(2,1)S(1)} %get-tuple-element.49.a_ref, f32[1,1152]{1,0:T(1,128)S(1)} %reshape.26.gain_ref, ...), custom_call_target="tpu_custom_call" | custom-call | flops 400000000 | bytes 6000000 | tf_op jit(solution)/shard_map/image/pallas_call | solution.py:438
  34.9 5.4 %all-to-all-start.1 = ((bf16[8,24,1152]{2,1,0:T(8,128)(2,1)}), bf16[8,24,1152]{2,1,0:T(8,128)(2,1)S(1)}, u32[]{:S(2)}, u32[]{:S(2)}) async-start(bf16[8,24,1152]{2,1,0:T(8,128)(2,1)} %get-tuple-element.50), calls=%async_computation.1 | async-start | bytes 884736 | tf_op jit(solution)/shard_map/all_to_all | solution.py:452
  42.7 8.5 %all-to-all-done.1.got_ref = bf16[8,24,1152]{2,1,0:T(8,128)(2,1)S(1)} async-done(((bf16[8,24,1152]{2,1,0:T(8,128)(2,1)}), bf16[8,24,1152]{2,1,0:T(8,128)(2,1)S(1)}, u32[]{:S(2)}, u32[]{:S(2)}) %all-to-all-start.1) | async-done | bytes 442400 | tf_op jit(solution)/shard_map/all_to_all | solution.py:452
  51.3 1.9 %pair.1 = (bf16[8,8,1152]{2,1,0:T(8,128)(2,1)}, bf16[64,256]{1,0:T(8,128)(2,1)S(1)}, bf16[64,1152]{1,0:T(8,128)(2,1)S(1)}, f32[8,128]{1,0:T(8,128)S(1)}) custom-call(s32[1]{0:T(128)} %bitcast.1.place, f32[2]{0:T(128)S(1)} %pad_maximum_fusion.4.scalars, bf16[8,24,1152]{2,1,0:T(8,128)(2,1)S(1)} %all-to-all-done.1.got_ref, ...), custom_call_target="tpu_custom_call" | custom-call | flops 80000000 | bytes 2000000 | tf_op jit(solution)/shard_map/pair/pallas_call | solution.py:456
  53.6 3.4 %all-to-all-start.2 = ((bf16[8,8,1152]{2,1,0:T(8,128)(2,1)}), bf16[8,8,1152]{2,1,0:T(8,128)(2,1)S(1)}, u32[]{:S(2)}, u32[]{:S(2)}) async-start(bf16[8,8,1152]{2,1,0:T(8,128)(2,1)} %get-tuple-element.56), calls=%async_computation.2 | async-start | bytes 294912 | tf_op jit(solution)/shard_map/all_to_all | solution.py:469
  57.7 1.4 %collective-permute-start.8 = (bf16[64,1152]{1,0:T(8,128)(2,1)}, bf16[64,1152]{1,0:T(8,128)(2,1)S(1)}, u32[]{:S(2)}, u32[]{:S(2)}) collective-permute-start(bf16[64,1152]{1,0:T(8,128)(2,1)} %get-tuple-element.65), channel_id=1, source_target_pairs={{0,128},{8,136},{16,144},{24,152},{32,160},{40,168},{48,176},{56,1... | collective-permute-start | bytes 442376 | tf_op jit(solution)/shard_map/ppermute | solution.py:27
  59.1 6.6 %all-to-all-done.2.got_in = bf16[8,8,1152]{2,1,0:T(8,128)(2,1)S(1)} async-done(((bf16[8,8,1152]{2,1,0:T(8,128)(2,1)}), bf16[8,8,1152]{2,1,0:T(8,128)(2,1)S(1)}, u32[]{:S(2)}, u32[]{:S(2)}) %all-to-all-start.2) | async-done | bytes 147488 | tf_op jit(solution)/shard_map/all_to_all | solution.py:469
  65.7 5.3 %back.1 = bf16[8,64,1152]{2,1,0:T(8,128)(2,1)} custom-call(s32[8]{0:T(128)S(1)} %bitcast.20, bf16[8,8,1152]{2,1,0:T(8,128)(2,1)S(1)} %all-to-all-done.2.got_in, bf16[15616,1152]{1,0:T(8,128)(2,1)} %get-tuple-element.57.full_in, bf16[1,8,48,1152]{3,2,1,0:T(8,128)(2,1)S(1)} %copy-done.1, f32[384,256]{1,0:T(8,128)S(1)} %get-tuple-element.58.side_in, ...), custom_call_target="tpu_custom_call" | custom-call | flops 500000000 | bytes 8000000 | tf_op jit(solution)/shard_map/back/pallas_call | solution.py:492
  71.1 3.6 %all-to-all-start.3 = ((bf16[8,64,1152]{2,1,0:T(8,128)(2,1)}), bf16[8,64,1152]{2,1,0:T(8,128)(2,1)S(1)}, u32[]{:S(2)}, u32[]{:S(2)}) async-start(bf16[8,64,1152]{2,1,0:T(8,128)(2,1)} %back.1), calls=%async_computation.3 | async-start | bytes 2359296 | tf_op jit(solution)/shard_map/all_to_all | solution.py:515
  74.6 1.3 %collective-permute-start.9 = (bf16[32,1152]{1,0:T(8,128)(2,1)S(1)}, bf16[32,1152]{1,0:T(8,128)(2,1)S(1)}, u32[]{:S(2)}, u32[]{:S(2)}) collective-permute-start(bf16[32,1152]{1,0:T(8,128)(2,1)S(1)} %get-tuple-element.71), channel_id=1, source_target_pairs={{0,16},{8,24},{16,0},{24,8},{32,48},{40,56},{48,32},{56,40},{64,80... | collective-permute-start | bytes 221192 | tf_op jit(solution)/shard_map/ppermute | solution.py:27
  76.7 2.6 %collective-permute-done.9.got_ref = bf16[32,1152]{1,0:T(8,128)(2,1)S(1)} collective-permute-done((bf16[32,1152]{1,0:T(8,128)(2,1)S(1)}, bf16[32,1152]{1,0:T(8,128)(2,1)S(1)}, u32[]{:S(2)}, u32[]{:S(2)}) %collective-permute-start.9) | collective-permute-done | bytes 73760 | tf_op jit(solution)/shard_map/ppermute | solution.py:27
  79.3 6.0 %collective-permute-start.10 = (bf16[8,1152]{1,0:T(8,128)(2,1)S(1)}, bf16[8,1152]{1,0:T(8,128)(2,1)S(1)}, u32[]{:S(2)}, u32[]{:S(2)}) collective-permute-start(bf16[8,1152]{1,0:T(8,128)(2,1)S(1)} %get-tuple-element.72), channel_id=1, source_target_pairs={{0,64},{8,72},{16,80},{24,88},{32,96},{40,104},{48,112},{56,120},{... | collective-permute-start | bytes 55304 | tf_op jit(solution)/shard_map/ppermute | solution.py:27
  85.3 1.5 %collective-permute-start.11 = (bf16[8,1152]{1,0:T(8,128)(2,1)S(1)}, bf16[8,1152]{1,0:T(8,128)(2,1)S(1)}, u32[]{:S(2)}, u32[]{:S(2)}) collective-permute-start(bf16[8,1152]{1,0:T(8,128)(2,1)S(1)} %get-tuple-element.73), channel_id=1, source_target_pairs={{0,32},{8,40},{16,48},{24,56},{32,0},{40,8},{48,16},{56,24},{64,96... | collective-permute-start | bytes 55304 | tf_op jit(solution)/shard_map/ppermute | solution.py:27
  86.8 6.2 %all-to-all-done.3.refs_0_ = bf16[8,64,1152]{2,1,0:T(8,128)(2,1)S(1)} async-done(((bf16[8,64,1152]{2,1,0:T(8,128)(2,1)}), bf16[8,64,1152]{2,1,0:T(8,128)(2,1)S(1)}, u32[]{:S(2)}, u32[]{:S(2)}) %all-to-all-start.3) | async-done | bytes 1179680 | tf_op jit(solution)/shard_map/all_to_all | solution.py:515
  93.0 1.7 %last.1 = (bf16[1,8,48,1152]{3,2,1,0:T(8,128)(2,1)}, bf16[1,144,1152]{2,1,0:T(8,128)(2,1)}, bf16[16,144]{1,0:T(8,128)(2,1)}, bf16[1,144]{1,0:T(2,128)(2,1)}, f32[1,1]{1,0:T(1,128)}) custom-call(bf16[8,64,1152]{2,1,0:T(8,128)(2,1)S(1)} %all-to-all-done.3.refs_0_, bf16[16,64,144]{2,1,0:T(8,128)(2,1)S(1)} %bitcast.16), custom_call_target="tpu_custom_call" | custom-call | flops 400000000 | bytes 3000000 | tf_op jit(solution)/shard_map/last/pallas_call | solution.py:540
  (46 shorter events, 8.8 us)
Async XLA Ops:
  0.6 1.0 %copy-start = (bf16[144,1152]{1,0:T(8,128)(2,1)S(1)}, bf16[144,1152]{1,0:T(8,128)(2,1)}, u32[]{:S(2)}) copy-start(bf16[144,1152]{1,0:T(8,128)(2,1)} %param.15) | copy-start | bytes 995332
  2.8 6.2 %copy-start.5 = (bf16[1,8,1152]{2,1,0:T(8,128)(2,1)S(1)}, bf16[1,8,1152]{2,1,0:T(8,128)(2,1)}, u32[]{:S(2)}) copy-start(bf16[1,8,1152]{2,1,0:T(8,128)(2,1)} %param.12) | copy-start | bytes 55300
  2.8 21.2 %copy-start.6 = (f32[1152]{0:T(1024)S(1)}, f32[1152]{0:T(1024)}, u32[]{:S(2)}) copy-start(f32[1152]{0:T(1024)} %param.13) | copy-start | bytes 13828
  2.8 21.2 %copy-start.1 = (bf16[1,8,48,1152]{3,2,1,0:T(8,128)(2,1)S(1)}, bf16[1,8,48,1152]{3,2,1,0:T(8,128)(2,1)}, u32[]{:S(2)}) copy-start(bf16[1,8,48,1152]{3,2,1,0:T(8,128)(2,1)} %x_in.1) | copy-start | bytes 2654212
  2.8 21.2 %copy-start.2 = (bf16[1152,16]{0,1:T(8,128)(2,1)S(1)}, bf16[1152,16]{0,1:T(8,128)(2,1)}, u32[]{:S(2)}) copy-start(bf16[1152,16]{0,1:T(8,128)(2,1)} %param.14) | copy-start | bytes 110596
  2.8 21.2 %copy-start.3 = (s32[1,8]{1,0:T(1,128)S(1)}, s32[1,8]{1,0:T(1,128)}, u32[]{:S(2)}) copy-start(s32[1,8]{1,0:T(1,128)} %param.11) | copy-start | bytes 100
  2.8 21.2 %copy-start.4 = (s32[1,8]{1,0:T(1,128)S(1)}, s32[1,8]{1,0:T(1,128)}, u32[]{:S(2)}) copy-start(s32[1,8]{1,0:T(1,128)} %param.10) | copy-start | bytes 100
  2.8 26.4 %all-to-all-start = ((bf16[8,72,1152]{2,1,0:T(8,128)(2,1)}), bf16[8,72,1152]{2,1,0:T(8,128)(2,1)S(1)}, u32[]{:S(2)}, u32[]{:S(2)}) async-start(bf16[8,72,1152]{2,1,0:T(8,128)(2,1)} %broadcast_in_dim.12), calls=%async_computation | async-start | bytes 2654208 | tf_op jit(solution)/shard_map/all_to_all | solution.py:401
  9.1 8.9 %collective-permute-start = (bf16[8,1152]{1,0:T(8,128)(2,1)S(1)}, bf16[8,1152]{1,0:T(8,128)(2,1)S(1)}, u32[]{:S(2)}, u32[]{:S(2)}) collective-permute-start(bf16[8,1152]{1,0:T(8,128)(2,1)S(1)} %get-tuple-element.46), channel_id=1, source_target_pairs={{0,64},{8,72},{16,80},{24,88},{32,96},{40,104},{48,112},{56,120},{... | collective-permute-start | bytes 55304 | tf_op jit(solution)/shard_map/ppermute | solution.py:27
  18.1 4.9 %collective-permute-start.1 = (bf16[16,1152]{1,0:T(8,128)(2,1)S(1)}, bf16[16,1152]{1,0:T(8,128)(2,1)S(1)}, u32[]{:S(2)}, u32[]{:S(2)}) collective-permute-start(bf16[16,1152]{1,0:T(8,128)(2,1)S(1)} %pad_maximum_fusion.3), channel_id=1, source_target_pairs={{0,32},{8,40},{16,48},{24,56},{32,0},{40,8},{48,16},{56,24},{64,96... | collective-permute-start | bytes 110600 | tf_op jit(solution)/shard_map/ppermute | solution.py:27
  22.9 4.4 %collective-permute-start.2 = (bf16[32,1152]{1,0:T(8,128)(2,1)S(1)}, bf16[32,1152]{1,0:T(8,128)(2,1)S(1)}, u32[]{:S(2)}, u32[]{:S(2)}) collective-permute-start(bf16[32,1152]{1,0:T(8,128)(2,1)S(1)} %pad_maximum_fusion.2), channel_id=1, source_target_pairs={{0,16},{8,24},{16,0},{24,8},{32,48},{40,56},{48,32},{56,40},{64,80... | collective-permute-start | bytes 221192 | tf_op jit(solution)/shard_map/ppermute | solution.py:27
  29.2 3.1 %collective-permute-start.3 = (bf16[8,72,1152]{2,1,0:T(8,128)(2,1)S(1)}, bf16[8,72,1152]{2,1,0:T(8,128)(2,1)S(1)}, u32[]{:S(2)}, u32[]{:S(2)}) collective-permute-start(bf16[8,72,1152]{2,1,0:T(8,128)(2,1)S(1)} %all-to-all-done.mine_ref), channel_id=1, source_target_pairs={{0,8},{8,0},{16,24},{24,16},{32,40},{40,32},{48,56},{56,48},{64,72... | collective-permute-start | bytes 3981320 | tf_op jit(solution)/shard_map/ppermute | solution.py:27
  29.3 12.4 %collective-permute-start.4 = (bf16[64,1152]{1,0:T(8,128)(2,1)S(1)}, bf16[64,1152]{1,0:T(8,128)(2,1)}, u32[]{:S(2)}, u32[]{:S(2)}) collective-permute-start(bf16[64,1152]{1,0:T(8,128)(2,1)S(1)} %pad_maximum_fusion.1), channel_id=1, source_target_pairs={{0,128},{8,136},{16,144},{24,152},{32,160},{40,168},{48,176},{56,1... | collective-permute-start | bytes 442376 | tf_op jit(solution)/shard_map/ppermute | solution.py:27
  30.7 10.9 %collective-permute-start.5 = (bf16[64,1152]{1,0:T(8,128)(2,1)S(1)}, bf16[64,1152]{1,0:T(8,128)(2,1)}, u32[]{:S(2)}, u32[]{:S(2)}) collective-permute-start(bf16[64,1152]{1,0:T(8,128)(2,1)S(1)} %pad_maximum_fusion.1), channel_id=1, source_target_pairs={{0,8},{8,0},{16,24},{24,16},{32,40},{40,32},{48,56},{56,48},{64,72... | collective-permute-start | bytes 442376 | tf_op jit(solution)/shard_map/ppermute | solution.py:27
  30.9 10.7 %collective-permute-start.6 = (bf16[64,1152]{1,0:T(8,128)(2,1)S(1)}, bf16[64,1152]{1,0:T(8,128)(2,1)}, u32[]{:S(2)}, u32[]{:S(2)}) collective-permute-start(bf16[64,1152]{1,0:T(8,128)(2,1)S(1)} %pad_maximum_fusion.1), channel_id=1, source_target_pairs={{0,136},{8,128},{16,152},{24,144},{32,168},{40,160},{48,184},{56,1... | collective-permute-start | bytes 442376 | tf_op jit(solution)/shard_map/ppermute | solution.py:27
  34.9 16.4 %all-to-all-start.1 = ((bf16[8,24,1152]{2,1,0:T(8,128)(2,1)}), bf16[8,24,1152]{2,1,0:T(8,128)(2,1)S(1)}, u32[]{:S(2)}, u32[]{:S(2)}) async-start(bf16[8,24,1152]{2,1,0:T(8,128)(2,1)} %get-tuple-element.50), calls=%async_computation.1 | async-start | bytes 884736 | tf_op jit(solution)/shard_map/all_to_all | solution.py:452
  53.5 3.5 %collective-permute-start.7 = (bf16[128,1152]{1,0:T(8,128)(2,1)S(1)}, bf16[128,1152]{1,0:T(8,128)(2,1)S(1)}, u32[]{:S(2)}, u32[]{:S(2)}) collective-permute-start(bf16[128,1152]{1,0:T(8,128)(2,1)S(1)} %get-tuple-element.63), channel_id=1, source_target_pairs={{0,8},{8,0},{16,24},{24,16},{32,40},{40,32},{48,56},{56,48},{64,72... | collective-permute-start | bytes 884744 | tf_op jit(solution)/shard_map/ppermute | solution.py:27
  53.6 12.2 %all-to-all-start.2 = ((bf16[8,8,1152]{2,1,0:T(8,128)(2,1)}), bf16[8,8,1152]{2,1,0:T(8,128)(2,1)S(1)}, u32[]{:S(2)}, u32[]{:S(2)}) async-start(bf16[8,8,1152]{2,1,0:T(8,128)(2,1)} %get-tuple-element.56), calls=%async_computation.2 | async-start | bytes 294912 | tf_op jit(solution)/shard_map/all_to_all | solution.py:469
  57.7 13.3 %collective-permute-start.8 = (bf16[64,1152]{1,0:T(8,128)(2,1)}, bf16[64,1152]{1,0:T(8,128)(2,1)S(1)}, u32[]{:S(2)}, u32[]{:S(2)}) collective-permute-start(bf16[64,1152]{1,0:T(8,128)(2,1)} %get-tuple-element.65), channel_id=1, source_target_pairs={{0,128},{8,136},{16,144},{24,152},{32,160},{40,168},{48,176},{56,1... | collective-permute-start | bytes 442376 | tf_op jit(solution)/shard_map/ppermute | solution.py:27
  71.1 21.9 %all-to-all-start.3 = ((bf16[8,64,1152]{2,1,0:T(8,128)(2,1)}), bf16[8,64,1152]{2,1,0:T(8,128)(2,1)S(1)}, u32[]{:S(2)}, u32[]{:S(2)}) async-start(bf16[8,64,1152]{2,1,0:T(8,128)(2,1)} %back.1), calls=%async_computation.3 | async-start | bytes 2359296 | tf_op jit(solution)/shard_map/all_to_all | solution.py:515
  74.6 4.6 %collective-permute-start.9 = (bf16[32,1152]{1,0:T(8,128)(2,1)S(1)}, bf16[32,1152]{1,0:T(8,128)(2,1)S(1)}, u32[]{:S(2)}, u32[]{:S(2)}) collective-permute-start(bf16[32,1152]{1,0:T(8,128)(2,1)S(1)} %get-tuple-element.71), channel_id=1, source_target_pairs={{0,16},{8,24},{16,0},{24,8},{32,48},{40,56},{48,32},{56,40},{64,80... | collective-permute-start | bytes 221192 | tf_op jit(solution)/shard_map/ppermute | solution.py:27
  79.3 15.4 %collective-permute-start.10 = (bf16[8,1152]{1,0:T(8,128)(2,1)S(1)}, bf16[8,1152]{1,0:T(8,128)(2,1)S(1)}, u32[]{:S(2)}, u32[]{:S(2)}) collective-permute-start(bf16[8,1152]{1,0:T(8,128)(2,1)S(1)} %get-tuple-element.72), channel_id=1, source_target_pairs={{0,64},{8,72},{16,80},{24,88},{32,96},{40,104},{48,112},{56,120},{... | collective-permute-start | bytes 55304 | tf_op jit(solution)/shard_map/ppermute | solution.py:27
  85.3 9.4 %collective-permute-start.11 = (bf16[8,1152]{1,0:T(8,128)(2,1)S(1)}, bf16[8,1152]{1,0:T(8,128)(2,1)S(1)}, u32[]{:S(2)}, u32[]{:S(2)}) collective-permute-start(bf16[8,1152]{1,0:T(8,128)(2,1)S(1)} %get-tuple-element.73), channel_id=1, source_target_pairs={{0,32},{8,40},{16,48},{24,56},{32,0},{40,8},{48,16},{56,24},{64,96... | collective-permute-start | bytes 55304 | tf_op jit(solution)/shard_map/ppermute | solution.py:27
  86.8 7.9 %collective-permute-start.12 = (bf16[8,1152]{1,0:T(8,128)(2,1)S(1)}, bf16[8,1152]{1,0:T(8,128)(2,1)S(1)}, u32[]{:S(2)}, u32[]{:S(2)}) collective-permute-start(bf16[8,1152]{1,0:T(8,128)(2,1)S(1)} %get-tuple-element.74), channel_id=1, source_target_pairs={{0,96},{8,104},{16,112},{24,120},{32,64},{40,72},{48,80},{56,88},{... | collective-permute-start | bytes 55304 | tf_op jit(solution)/shard_map/ppermute | solution.py:27

commit v6 on v5

--- a/solution.py
+++ b/solution.py
@@ -172,13 +172,12 @@
     text_ref[...] = unit.astype(BF16)
 
 
-def pair_body(place, scalars, got_ref, text_ref, d_image_ref, coefficient_ref, image_ref, loss_ref):
+def pair_body(place, scalars, got_ref, text_ref, d_image_ref, keep_ref, send_ref, loss_ref):
     loaders, got_rows, width = got_ref.shape
     slots = d_image_ref.shape[1]
     images = jnp.concatenate(
         [got_ref[s].astype(F32)[got_rows - slots :] for s in range(loaders)], axis=0
     ).astype(BF16)
-    image_ref[...] = images
     texts = text_ref[...]
     count = images.shape[0]
     text_count = texts.shape[0]
@@ -194,19 +193,15 @@
     losses = jnp.maximum(signed, 0.0) + jnp.log1p(decay)
     sigmoid = jnp.where(logits >= 0.0, 1.0, decay) / (1.0 + decay)
     coefficient = (scale * (sigmoid - matched)).astype(BF16)
-    coefficient_ref[...] = coefficient
     d_image = jnp.dot(coefficient, texts, preferred_element_type=F32)
     d_image_ref[...] = d_image.reshape(d_image_ref.shape).astype(BF16)
+    d_text = tn_dot(coefficient, images)
+    half = keep_ref.shape[0]
+    keep_ref[...] = d_text[:half]
+    send_ref[...] = d_text[half:].astype(BF16)
     per_image = jnp.sum(losses, axis=-1, keepdims=True)
     per_owner = jnp.sum(per_image.reshape(loaders, slots, 1), axis=0)
     loss_ref[...] = jnp.broadcast_to(per_owner, loss_ref.shape)
-
-
-def text_body(coefficient_ref, image_ref, keep_ref, send_ref):
-    d_text = tn_dot(coefficient_ref[...], image_ref[...])
-    half = keep_ref.shape[0]
-    keep_ref[...] = d_text[:half]
-    send_ref[...] = d_text[half:].astype(BF16)
 
 
 def fold_body(total_ref, got_ref, keep_ref, send_ref):
@@ -222,15 +217,6 @@
     keep_ref[...] = total[:rows]
     for k, block_ref in enumerate(block_refs):
         block_ref[...] = total[(k + 1) * rows : (k + 2) * rows].astype(BF16)
-
-
-def finish_body(total_ref, unit_ref, inv_ref, *refs):
-    d_caption = total_ref[...]
-    for block_ref in refs[:-1]:
-        d_caption = d_caption + block_ref[...].astype(F32)
-    unit = unit_ref[...]
-    along = jnp.sum(d_caption * unit, axis=-1, keepdims=True)
-    refs[-1][...] = ((d_caption - unit * along) * inv_ref[:, 0:1]).astype(BF16)
 
 
 def back_body(
@@ -349,7 +335,10 @@
         copy.wait()
 
 
-def last_body(got_ref, a_ref, row_ref, value_ref, probe_ref, gain_ref, loss_ref, tail, sems, *, texts):
+def last_body(
+    got_ref, a_ref, total_ref, unit_ref, inv_ref, *refs, blocks, texts
+):
+    row_ref, value_ref, probe_ref, gain_ref, loss_ref, text_ref, tail, sems = refs[blocks:]
     loaders, got_rows, width = got_ref.shape
     rows = row_ref.shape[2]
     heads, images, cut = a_ref.shape
@@ -377,6 +366,12 @@
     probe_ref[...] = jnp.concatenate([misc[:, 0:cut], misc[:, 256 : 256 + cut]], axis=0).astype(BF16)
     gain_ref[...] = misc[0:1, 512 : 512 + cut].astype(BF16)
     loss_ref[...] = (misc[0:1, 768:769] + misc[1:2, 768:769] + misc[2:3, 768:769]) / texts
+    d_caption = total_ref[...]
+    for block_ref in refs[:blocks]:
+        d_caption = d_caption + block_ref[...].astype(F32)
+    unit = unit_ref[...]
+    along = jnp.sum(d_caption * unit, axis=-1, keepdims=True)
+    text_ref[...] = ((d_caption - unit * along) * inv_ref[:, 0:1]).astype(BF16)
     second.wait()
 
 
@@ -451,14 +446,13 @@
     full, flanks = lax.optimization_barrier((full, flanks))
     got = lax.all_to_all(sent, "fsdp", 0, 0, tiled=True)
     texts = jnp.concatenate([texts] + flanks, axis=0)
-    count = peers * slots
     text_count = ranks * slots
-    d_image_part, coefficient, images, loss_sums = call(
+    d_image_part, keep, send, loss_sums = call(
         pair_body,
         [
             (shape((peers, slots, width), BF16), vspec()),
-            (shape((count, text_count), BF16), vspec()),
-            (shape((count, width), BF16), vspec()),
+            (shape((text_count // 2, width), F32), vspec()),
+            (shape((text_count // 2, width), BF16), vspec()),
             (shape((slots, 128), F32), vspec()),
         ],
         [sspec(), sspec(), vspec(), vspec()],
@@ -481,9 +475,6 @@
             fold_body, halves(keep.shape[0] // 2), [vspec(), vspec()], 40_000_000, 1_000_000, name="fold"
         )(keep, swapped(send, bit))
 
-    keep, send = call(
-        text_body, halves(text_count // 2), [vspec(), vspec()], 0, 0, name="text"
-    )(coefficient, images)
     if ranks > 2:
         keep, send = fold(keep, send, CORE_BIT)
     if ranks > 2:
@@ -535,9 +526,9 @@
     batch = ranks * peers * slots
 
     def last(*refs):
-        last_body(*refs, texts=batch)
-
-    row_grad, value_grad, probe_t, gain_grad, loss_part = call(
+        last_body(*refs, blocks=len(blocks), texts=batch)
+
+    row_grad, value_grad, probe_t, gain_grad, loss_part, text_grad = call(
         last,
         [
             (shape((1, slots, rows, width), BF16), hspec()),
@@ -545,23 +536,15 @@
             (shape((heads, cut), BF16), vspec()),
             (shape((1, cut), BF16), vspec()),
             (shape((1, 1), F32), vspec()),
+            (shape((slots, width), BF16), vspec()),
         ],
-        [hspec(), vspec()],
+        [hspec()] + [vspec()] * (4 + len(blocks)),
         400_000_000,
         3_000_000,
         [pltpu.VMEM((peers, 16, width), BF16), dma((2,))],
         name="last",
-    )(arrived, pooled_got)
-
-    loss_part, blocks = lax.optimization_barrier((loss_part, blocks))
-    text_grad = call(
-        finish_body,
-        [(shape((slots, width), BF16), vspec())],
-        [vspec()] * (3 + len(blocks)),
-        0,
-        0,
-        name="finish",
-    )(d_caption, caption_unit, caption_inv, *blocks)[0]
+    )(arrived, pooled_got, d_caption, caption_unit, caption_inv, *blocks)
+
     return (loss_part, row_grad, text_grad[None], value_grad, probe_t.T[None], gain_grad)
 
 

time: 96.6 us -> 96.4 us (level)
  waiting for transfers between devices: 32.5 us -> 31.4 us
    ppermute x13, waiting for transfers between devices: 9.24 us -> 15.1 us  [swapped(): lax.ppermute(block, 'dp', [(i, i ^ bit) for i in range(lax.axis_size('dp'...]
    all_to_all x1, waiting for transfers between devices: 6.21 us -> 0.91 us  [local(): arrived = lax.all_to_all(outgoing, 'fsdp', 0, 0, tiled=True)]
    all_to_all x1, waiting for transfers between devices: 6.63 us -> 5.61 us  [local(): d_image_got = lax.all_to_all(d_image_part, 'fsdp', 0, 0, tiled=True)]
    pallas_call x3 -> x1, Pallas kernels: 2.91 us -> 2.21 us  [local(): call(pair_body, [(shape((peers, slots, width), BF16), vspec()), (shape((t...]
  transfers between devices with their start and end apart: 17 -> 17, of which waited for: 9 -> 11; matrix products, arithmetic and copies ran while one was open for 2% -> 3% of each run, Pallas kernels for 13% -> 11%
where the time goes in v6:
time: 96.4 us; the launch traced here: 95.3 us
  starting transfers between devices  41.5 us (43%)
  waiting for transfers between devices  31.4 us (33%)
  Pallas kernels  14.8 us (15%)
  local copies, waits for them, and re-layouts  3.63 us (4%)
  between operations  2.14 us (2%)
  other arithmetic  1.93 us (2%)
    ppermute x13, starting transfers between devices, swapped(): lax.ppermute(block, 'dp', [(i, i ^ bit) for i in range(lax.axis_size('dp'...  22.4 us
    ppermute x13, waiting for transfers between devices, swapped(): lax.ppermute(block, 'dp', [(i, i ^ bit) for i in range(lax.axis_size('dp'...  15.1 us
    all_to_all x1, waiting for transfers between devices, local(): got = lax.all_to_all(sent, 'fsdp', 0, 0, tiled=True)  8.45 us
    all_to_all x1, starting transfers between devices, local(): lax.all_to_all(jnp.broadcast_to(part[None], (peers, SEND_ROWS, width)), '...  6.18 us
    all_to_all x1, starting transfers between devices, local(): got = lax.all_to_all(sent, 'fsdp', 0, 0, tiled=True)  5.93 us
    all_to_all x1, waiting for transfers between devices, local(): d_image_got = lax.all_to_all(d_image_part, 'fsdp', 0, 0, tiled=True)  5.61 us
    pallas_call x1, Pallas kernels, local(): call(back_body, [(shape((peers, rows + 16, width), BF16), hspec())], [hsp...  5.33 us
    all_to_all x1, starting transfers between devices, local(): arrived = lax.all_to_all(outgoing, 'fsdp', 0, 0, tiled=True)  3.58 us
  transfers between devices with their start and end apart: 17, of which 11 were waited for; matrix products, arithmetic and copies ran while one was open for 3% of the time, Pallas kernels for 11%

profile of v6, /device:TPU:2, one launch (start us, length us, event | category | flops | bytes accessed | tf_op | source)
XLA Modules:
  0.0 95.3 jit_solution(2804947907407075942)
XLA Ops:
  2.8 6.2 %all-to-all-start = ((bf16[8,72,1152]{2,1,0:T(8,128)(2,1)}), bf16[8,72,1152]{2,1,0:T(8,128)(2,1)S(1)}, u32[]{:S(2)}, u32[]{:S(2)}) async-start(bf16[8,72,1152]{2,1,0:T(8,128)(2,1)} %broadcast_in_dim.12), calls=%async_computation | async-start | bytes 2654208 | tf_op jit(solution)/shard_map/all_to_all | solution.py:396
  9.1 7.2 %collective-permute-start = (bf16[8,1152]{1,0:T(8,128)(2,1)S(1)}, bf16[8,1152]{1,0:T(8,128)(2,1)S(1)}, u32[]{:S(2)}, u32[]{:S(2)}) collective-permute-start(bf16[8,1152]{1,0:T(8,128)(2,1)S(1)} %get-tuple-element.41), channel_id=1, source_target_pairs={{0,64},{8,72},{16,80},{24,88},{32,96},{40,104},{48,112},{56,120},{... | collective-permute-start | bytes 55304 | tf_op jit(solution)/shard_map/ppermute | solution.py:27
  16.3 1.7 %collective-permute-done = bf16[8,1152]{1,0:T(8,128)(2,1)S(1)} collective-permute-done((bf16[8,1152]{1,0:T(8,128)(2,1)S(1)}, bf16[8,1152]{1,0:T(8,128)(2,1)S(1)}, u32[]{:S(2)}, u32[]{:S(2)}) %collective-permute-start) | collective-permute-done | bytes 18464 | tf_op jit(solution)/shard_map/ppermute | solution.py:27
  18.1 2.0 %collective-permute-start.1 = (bf16[16,1152]{1,0:T(8,128)(2,1)S(1)}, bf16[16,1152]{1,0:T(8,128)(2,1)S(1)}, u32[]{:S(2)}, u32[]{:S(2)}) collective-permute-start(bf16[16,1152]{1,0:T(8,128)(2,1)S(1)} %pad_maximum_fusion.3), channel_id=1, source_target_pairs={{0,32},{8,40},{16,48},{24,56},{32,0},{40,8},{48,16},{56,24},{64,96... | collective-permute-start | bytes 110600 | tf_op jit(solution)/shard_map/ppermute | solution.py:27
  20.1 2.8 %collective-permute-done.1 = bf16[16,1152]{1,0:T(8,128)(2,1)S(1)} collective-permute-done((bf16[16,1152]{1,0:T(8,128)(2,1)S(1)}, bf16[16,1152]{1,0:T(8,128)(2,1)S(1)}, u32[]{:S(2)}, u32[]{:S(2)}) %collective-permute-start.1) | collective-permute-done | bytes 36896 | tf_op jit(solution)/shard_map/ppermute | solution.py:27
  24.0 2.1 %pool.1 = (f32[384,256]{1,0:T(8,128)S(1)}, bf16[128,1152]{1,0:T(8,128)(2,1)S(1)}) custom-call(s32[8]{0:T(128)S(1)} %bitcast.19, s32[8]{0:T(128)S(1)} %bitcast.21, bf16[8,48,1152]{2,1,0:T(8,128)(2,1)S(1)} %bitcast.15, f32[1,1152]{1,0:T(1,128)S(1)} %reshape.26.gain_ref, bf16[16,1152]{1,0:T(8,128)(2,1)S(1)} %bitcast.17), custom_call_target="tpu_custom_call" | custom-call | flops 40000000 | bytes 4000000 | tf_op jit(solution)/shard_map/pool/pallas_call | solution.py:401
  28.0 1.3 %all-to-all-done.mine_ref = bf16[8,72,1152]{2,1,0:T(8,128)(2,1)S(1)} async-done(((bf16[8,72,1152]{2,1,0:T(8,128)(2,1)}), bf16[8,72,1152]{2,1,0:T(8,128)(2,1)S(1)}, u32[]{:S(2)}, u32[]{:S(2)}) %all-to-all-start) | async-done | bytes 1327136 | tf_op jit(solution)/shard_map/all_to_all | solution.py:396
  29.2 1.4 %collective-permute-start.4 = (bf16[64,1152]{1,0:T(8,128)(2,1)}, bf16[64,1152]{1,0:T(8,128)(2,1)}, u32[]{:S(2)}, u32[]{:S(2)}) collective-permute-start(bf16[64,1152]{1,0:T(8,128)(2,1)} %pad_maximum_fusion.1), channel_id=1, source_target_pairs={{0,128},{8,136},{16,144},{24,152},{32,160},{40,168},{48,176},{56,1... | collective-permute-start | bytes 442376 | tf_op jit(solution)/shard_map/ppermute | solution.py:27
  32.3 2.6 %image.1 = (bf16[15616,1152]{1,0:T(8,128)(2,1)}, bf16[8,24,1152]{2,1,0:T(8,128)(2,1)}) custom-call(bf16[8,72,1152]{2,1,0:T(8,128)(2,1)S(1)} %all-to-all-done.mine_ref, bf16[8,72,1152]{2,1,0:T(8,128)(2,1)S(1)} %collective-permute-done.3.other_ref, bf16[128,1152]{1,0:T(8,128)(2,1)S(1)} %get-tuple-element.44.a_ref, f32[1,1152]{1,0:T(1,128)S(1)} %reshape.26.gain_ref, ...), custom_call_target="tpu_custom_call" | custom-call | flops 400000000 | bytes 6000000 | tf_op jit(solution)/shard_map/image/pallas_call | solution.py:433
  34.9 5.9 %all-to-all-start.1 = ((bf16[8,24,1152]{2,1,0:T(8,128)(2,1)}), bf16[8,24,1152]{2,1,0:T(8,128)(2,1)S(1)}, u32[]{:S(2)}, u32[]{:S(2)}) async-start(bf16[8,24,1152]{2,1,0:T(8,128)(2,1)} %get-tuple-element.45), calls=%async_computation.1 | async-start | bytes 884736 | tf_op jit(solution)/shard_map/all_to_all | solution.py:447
  42.2 1.2 %pad_maximum_fusion.text_ref = bf16[256,1152]{1,0:T(8,128)(2,1)S(1)} fusion(bf16[64,1152]{1,0:T(8,128)(2,1)} %collective-permute-done.6, bf16[64,1152]{1,0:T(8,128)(2,1)} %collective-permute-done.5, bf16[64,1152]{1,0:T(8,128)(2,1)} %collective-permute-done.4, bf16[64,1152]{1,0:T(8,128)(2,1)} %pad_maximum_fusion.1), kind=kLoop, calls=%fused_computation | loop fusion | flops 2359296 | bytes 1179648 | tf_op jit(solution)/shard_map/concatenate | solution.py:448
  43.4 8.4 %all-to-all-done.1.got_ref = bf16[8,24,1152]{2,1,0:T(8,128)(2,1)S(1)} async-done(((bf16[8,24,1152]{2,1,0:T(8,128)(2,1)}), bf16[8,24,1152]{2,1,0:T(8,128)(2,1)S(1)}, u32[]{:S(2)}, u32[]{:S(2)}) %all-to-all-start.1) | async-done | bytes 442400 | tf_op jit(solution)/shard_map/all_to_all | solution.py:447
  51.8 2.2 %pair.1 = (bf16[8,8,1152]{2,1,0:T(8,128)(2,1)}, f32[128,1152]{1,0:T(8,128)S(1)}, bf16[128,1152]{1,0:T(8,128)(2,1)}, f32[8,128]{1,0:T(8,128)S(1)}) custom-call(s32[1]{0:T(128)} %bitcast.1.place, f32[2]{0:T(128)S(1)} %pad_maximum_fusion.4.scalars, bf16[8,24,1152]{2,1,0:T(8,128)(2,1)S(1)} %all-to-all-done.1.got_ref, bf16[256,1152]{1,0:T(8,128)(2,1)S(1)} %pad_maximum_fusion.text_ref), custom_call_target="tpu_custom_call" | custom-call | flops 80000000 | bytes 2000000 | tf_op jit(solution)/shard_map/pair/pallas_call | solution.py:450
  54.0 3.4 %all-to-all-start.2 = ((bf16[8,8,1152]{2,1,0:T(8,128)(2,1)}), bf16[8,8,1152]{2,1,0:T(8,128)(2,1)S(1)}, u32[]{:S(2)}, u32[]{:S(2)}) async-start(bf16[8,8,1152]{2,1,0:T(8,128)(2,1)} %get-tuple-element.51), calls=%async_computation.2 | async-start | bytes 294912 | tf_op jit(solution)/shard_map/all_to_all | solution.py:463
  58.8 1.4 %collective-permute-start.8 = (bf16[64,1152]{1,0:T(8,128)(2,1)}, bf16[64,1152]{1,0:T(8,128)(2,1)S(1)}, u32[]{:S(2)}, u32[]{:S(2)}) collective-permute-start(bf16[64,1152]{1,0:T(8,128)(2,1)} %get-tuple-element.58), channel_id=1, source_target_pairs={{0,128},{8,136},{16,144},{24,152},{32,160},{40,168},{48,176},{56,1... | collective-permute-start | bytes 442376 | tf_op jit(solution)/shard_map/ppermute | solution.py:27
  60.3 5.6 %all-to-all-done.2.got_in = bf16[8,8,1152]{2,1,0:T(8,128)(2,1)S(1)} async-done(((bf16[8,8,1152]{2,1,0:T(8,128)(2,1)}), bf16[8,8,1152]{2,1,0:T(8,128)(2,1)S(1)}, u32[]{:S(2)}, u32[]{:S(2)}) %all-to-all-start.2) | async-done | bytes 147488 | tf_op jit(solution)/shard_map/all_to_all | solution.py:463
  65.9 5.3 %back.1 = bf16[8,64,1152]{2,1,0:T(8,128)(2,1)} custom-call(s32[8]{0:T(128)S(1)} %bitcast.20, bf16[8,8,1152]{2,1,0:T(8,128)(2,1)S(1)} %all-to-all-done.2.got_in, bf16[15616,1152]{1,0:T(8,128)(2,1)} %get-tuple-element.52.full_in, bf16[1,8,48,1152]{3,2,1,0:T(8,128)(2,1)S(1)} %copy-done.1, f32[384,256]{1,0:T(8,128)S(1)} %get-tuple-element.53.side_in, ...), custom_call_target="tpu_custom_call" | custom-call | flops 500000000 | bytes 8000000 | tf_op jit(solution)/shard_map/back/pallas_call | solution.py:483
  71.3 3.6 %all-to-all-start.3 = ((bf16[8,64,1152]{2,1,0:T(8,128)(2,1)}), bf16[8,64,1152]{2,1,0:T(8,128)(2,1)S(1)}, u32[]{:S(2)}, u32[]{:S(2)}) async-start(bf16[8,64,1152]{2,1,0:T(8,128)(2,1)} %back.1), calls=%async_computation.3 | async-start | bytes 2359296 | tf_op jit(solution)/shard_map/all_to_all | solution.py:506
  76.0 3.3 %collective-permute-done.9.got_ref = bf16[32,1152]{1,0:T(8,128)(2,1)S(1)} collective-permute-done((bf16[32,1152]{1,0:T(8,128)(2,1)S(1)}, bf16[32,1152]{1,0:T(8,128)(2,1)S(1)}, u32[]{:S(2)}, u32[]{:S(2)}) %collective-permute-start.9) | collective-permute-done | bytes 73760 | tf_op jit(solution)/shard_map/ppermute | solution.py:27
  79.3 6.0 %collective-permute-start.10 = (bf16[8,1152]{1,0:T(8,128)(2,1)S(1)}, bf16[8,1152]{1,0:T(8,128)(2,1)S(1)}, u32[]{:S(2)}, u32[]{:S(2)}) collective-permute-start(bf16[8,1152]{1,0:T(8,128)(2,1)S(1)} %get-tuple-element.67), channel_id=1, source_target_pairs={{0,64},{8,72},{16,80},{24,88},{32,96},{40,104},{48,112},{56,120},{... | collective-permute-start | bytes 55304 | tf_op jit(solution)/shard_map/ppermute | solution.py:27
  85.3 1.5 %collective-permute-start.11 = (bf16[8,1152]{1,0:T(8,128)(2,1)S(1)}, bf16[8,1152]{1,0:T(8,128)(2,1)S(1)}, u32[]{:S(2)}, u32[]{:S(2)}) collective-permute-start(bf16[8,1152]{1,0:T(8,128)(2,1)S(1)} %get-tuple-element.68), channel_id=1, source_target_pairs={{0,32},{8,40},{16,48},{24,56},{32,0},{40,8},{48,16},{56,24},{64,96... | collective-permute-start | bytes 55304 | tf_op jit(solution)/shard_map/ppermute | solution.py:27
  87.6 2.4 %collective-permute-done.11.refs_6_ = bf16[8,1152]{1,0:T(8,128)(2,1)S(1)} collective-permute-done((bf16[8,1152]{1,0:T(8,128)(2,1)S(1)}, bf16[8,1152]{1,0:T(8,128)(2,1)S(1)}, u32[]{:S(2)}, u32[]{:S(2)}) %collective-permute-start.11) | collective-permute-done | bytes 18464 | tf_op jit(solution)/shard_map/ppermute | solution.py:27
  90.0 2.7 %collective-permute-done.12.refs_7_ = bf16[8,1152]{1,0:T(8,128)(2,1)S(1)} collective-permute-done((bf16[8,1152]{1,0:T(8,128)(2,1)S(1)}, bf16[8,1152]{1,0:T(8,128)(2,1)S(1)}, u32[]{:S(2)}, u32[]{:S(2)}) %collective-permute-start.12) | collective-permute-done | bytes 18464 | tf_op jit(solution)/shard_map/ppermute | solution.py:27
  93.6 1.7 %last.1 = (bf16[1,8,48,1152]{3,2,1,0:T(8,128)(2,1)}, bf16[1,144,1152]{2,1,0:T(8,128)(2,1)}, bf16[16,144]{1,0:T(8,128)(2,1)}, bf16[1,144]{1,0:T(2,128)(2,1)}, f32[1,1]{1,0:T(1,128)}, /*index=5*/bf16[8,1152]{1,0:T(8,128)(2,1)}) custom-call(bf16[8,64,1152]{2,1,0:T(8,128)(2,1)S(1)} %all-to-all-done.3.refs_0_, bf16[16,64,144]{2,1,0:T(8,128)(2,1)S(1)} %bitcast.16, ...), custom_call_target="tpu_custom_call" | custom-call | flops 400000000 | bytes 3000000 | tf_op jit(solution)/shard_map/last/pallas_call | solution.py:531
  (48 shorter events, 11.1 us)
Async XLA Ops:
  2.8 6.2 %copy-start.7 = (bf16[1,8,1152]{2,1,0:T(8,128)(2,1)S(1)}, bf16[1,8,1152]{2,1,0:T(8,128)(2,1)}, u32[]{:S(2)}) copy-start(bf16[1,8,1152]{2,1,0:T(8,128)(2,1)} %param.12) | copy-start | bytes 55300
  2.8 21.2 %copy-start.8 = (f32[1152]{0:T(1024)S(1)}, f32[1152]{0:T(1024)}, u32[]{:S(2)}) copy-start(f32[1152]{0:T(1024)} %param.13) | copy-start | bytes 13828
  2.8 21.2 %copy-start.1 = (bf16[1,8,48,1152]{3,2,1,0:T(8,128)(2,1)S(1)}, bf16[1,8,48,1152]{3,2,1,0:T(8,128)(2,1)}, u32[]{:S(2)}) copy-start(bf16[1,8,48,1152]{3,2,1,0:T(8,128)(2,1)} %x_in.1) | copy-start | bytes 2654212
  2.8 21.2 %copy-start.4 = (bf16[1152,16]{0,1:T(8,128)(2,1)S(1)}, bf16[1152,16]{0,1:T(8,128)(2,1)}, u32[]{:S(2)}) copy-start(bf16[1152,16]{0,1:T(8,128)(2,1)} %param.14) | copy-start | bytes 110596
  2.8 21.2 %copy-start.5 = (s32[1,8]{1,0:T(1,128)S(1)}, s32[1,8]{1,0:T(1,128)}, u32[]{:S(2)}) copy-start(s32[1,8]{1,0:T(1,128)} %param.11) | copy-start | bytes 100
  2.8 21.2 %copy-start.6 = (s32[1,8]{1,0:T(1,128)S(1)}, s32[1,8]{1,0:T(1,128)}, u32[]{:S(2)}) copy-start(s32[1,8]{1,0:T(1,128)} %param.10) | copy-start | bytes 100
  2.8 26.4 %all-to-all-start = ((bf16[8,72,1152]{2,1,0:T(8,128)(2,1)}), bf16[8,72,1152]{2,1,0:T(8,128)(2,1)S(1)}, u32[]{:S(2)}, u32[]{:S(2)}) async-start(bf16[8,72,1152]{2,1,0:T(8,128)(2,1)} %broadcast_in_dim.12), calls=%async_computation | async-start | bytes 2654208 | tf_op jit(solution)/shard_map/all_to_all | solution.py:396
  9.1 8.9 %collective-permute-start = (bf16[8,1152]{1,0:T(8,128)(2,1)S(1)}, bf16[8,1152]{1,0:T(8,128)(2,1)S(1)}, u32[]{:S(2)}, u32[]{:S(2)}) collective-permute-start(bf16[8,1152]{1,0:T(8,128)(2,1)S(1)} %get-tuple-element.41), channel_id=1, source_target_pairs={{0,64},{8,72},{16,80},{24,88},{32,96},{40,104},{48,112},{56,120},{... | collective-permute-start | bytes 55304 | tf_op jit(solution)/shard_map/ppermute | solution.py:27
  18.1 4.9 %collective-permute-start.1 = (bf16[16,1152]{1,0:T(8,128)(2,1)S(1)}, bf16[16,1152]{1,0:T(8,128)(2,1)S(1)}, u32[]{:S(2)}, u32[]{:S(2)}) collective-permute-start(bf16[16,1152]{1,0:T(8,128)(2,1)S(1)} %pad_maximum_fusion.3), channel_id=1, source_target_pairs={{0,32},{8,40},{16,48},{24,56},{32,0},{40,8},{48,16},{56,24},{64,96... | collective-permute-start | bytes 110600 | tf_op jit(solution)/shard_map/ppermute | solution.py:27
  22.9 4.4 %collective-permute-start.2 = (bf16[32,1152]{1,0:T(8,128)(2,1)S(1)}, bf16[32,1152]{1,0:T(8,128)(2,1)S(1)}, u32[]{:S(2)}, u32[]{:S(2)}) collective-permute-start(bf16[32,1152]{1,0:T(8,128)(2,1)S(1)} %pad_maximum_fusion.2), channel_id=1, source_target_pairs={{0,16},{8,24},{16,0},{24,8},{32,48},{40,56},{48,32},{56,40},{64,80... | collective-permute-start | bytes 221192 | tf_op jit(solution)/shard_map/ppermute | solution.py:27
  29.2 3.1 %collective-permute-start.3 = (bf16[8,72,1152]{2,1,0:T(8,128)(2,1)S(1)}, bf16[8,72,1152]{2,1,0:T(8,128)(2,1)S(1)}, u32[]{:S(2)}, u32[]{:S(2)}) collective-permute-start(bf16[8,72,1152]{2,1,0:T(8,128)(2,1)S(1)} %all-to-all-done.mine_ref), channel_id=1, source_target_pairs={{0,8},{8,0},{16,24},{24,16},{32,40},{40,32},{48,56},{56,48},{64,72... | collective-permute-start | bytes 3981320 | tf_op jit(solution)/shard_map/ppermute | solution.py:27
  29.2 12.9 %collective-permute-start.4 = (bf16[64,1152]{1,0:T(8,128)(2,1)}, bf16[64,1152]{1,0:T(8,128)(2,1)}, u32[]{:S(2)}, u32[]{:S(2)}) collective-permute-start(bf16[64,1152]{1,0:T(8,128)(2,1)} %pad_maximum_fusion.1), channel_id=1, source_target_pairs={{0,128},{8,136},{16,144},{24,152},{32,160},{40,168},{48,176},{56,1... | collective-permute-start | bytes 442376 | tf_op jit(solution)/shard_map/ppermute | solution.py:27
  30.7 11.5 %collective-permute-start.5 = (bf16[64,1152]{1,0:T(8,128)(2,1)}, bf16[64,1152]{1,0:T(8,128)(2,1)}, u32[]{:S(2)}, u32[]{:S(2)}) collective-permute-start(bf16[64,1152]{1,0:T(8,128)(2,1)} %pad_maximum_fusion.1), channel_id=1, source_target_pairs={{0,8},{8,0},{16,24},{24,16},{32,40},{40,32},{48,56},{56,48},{64,72... | collective-permute-start | bytes 442376 | tf_op jit(solution)/shard_map/ppermute | solution.py:27
  30.9 11.3 %collective-permute-start.6 = (bf16[64,1152]{1,0:T(8,128)(2,1)}, bf16[64,1152]{1,0:T(8,128)(2,1)}, u32[]{:S(2)}, u32[]{:S(2)}) collective-permute-start(bf16[64,1152]{1,0:T(8,128)(2,1)} %pad_maximum_fusion.1), channel_id=1, source_target_pairs={{0,136},{8,128},{16,152},{24,144},{32,168},{40,160},{48,184},{56,1... | collective-permute-start | bytes 442376 | tf_op jit(solution)/shard_map/ppermute | solution.py:27
  34.9 16.9 %all-to-all-start.1 = ((bf16[8,24,1152]{2,1,0:T(8,128)(2,1)}), bf16[8,24,1152]{2,1,0:T(8,128)(2,1)S(1)}, u32[]{:S(2)}, u32[]{:S(2)}) async-start(bf16[8,24,1152]{2,1,0:T(8,128)(2,1)} %get-tuple-element.45), calls=%async_computation.1 | async-start | bytes 884736 | tf_op jit(solution)/shard_map/all_to_all | solution.py:447
  54.0 3.4 %collective-permute-start.7 = (bf16[128,1152]{1,0:T(8,128)(2,1)}, bf16[128,1152]{1,0:T(8,128)(2,1)S(1)}, u32[]{:S(2)}, u32[]{:S(2)}) collective-permute-start(bf16[128,1152]{1,0:T(8,128)(2,1)} %get-tuple-element.56), channel_id=1, source_target_pairs={{0,8},{8,0},{16,24},{24,16},{32,40},{40,32},{48,56},{56,48},{64,72... | collective-permute-start | bytes 884744 | tf_op jit(solution)/shard_map/ppermute | solution.py:27
  54.0 11.9 %all-to-all-start.2 = ((bf16[8,8,1152]{2,1,0:T(8,128)(2,1)}), bf16[8,8,1152]{2,1,0:T(8,128)(2,1)S(1)}, u32[]{:S(2)}, u32[]{:S(2)}) async-start(bf16[8,8,1152]{2,1,0:T(8,128)(2,1)} %get-tuple-element.51), calls=%async_computation.2 | async-start | bytes 294912 | tf_op jit(solution)/shard_map/all_to_all | solution.py:463
  58.8 12.4 %collective-permute-start.8 = (bf16[64,1152]{1,0:T(8,128)(2,1)}, bf16[64,1152]{1,0:T(8,128)(2,1)S(1)}, u32[]{:S(2)}, u32[]{:S(2)}) collective-permute-start(bf16[64,1152]{1,0:T(8,128)(2,1)} %get-tuple-element.58), channel_id=1, source_target_pairs={{0,128},{8,136},{16,144},{24,152},{32,160},{40,168},{48,176},{56,1... | collective-permute-start | bytes 442376 | tf_op jit(solution)/shard_map/ppermute | solution.py:27
  65.9 5.4 %copy-start.3 = (f32[64,1152]{1,0:T(8,128)S(1)}, f32[64,1152]{1,0:T(8,128)}, u32[]{:S(2)}) copy-start(f32[64,1152]{1,0:T(8,128)} %copy-done.2) | copy-start | bytes 884740
  71.3 22.3 %all-to-all-start.3 = ((bf16[8,64,1152]{2,1,0:T(8,128)(2,1)}), bf16[8,64,1152]{2,1,0:T(8,128)(2,1)S(1)}, u32[]{:S(2)}, u32[]{:S(2)}) async-start(bf16[8,64,1152]{2,1,0:T(8,128)(2,1)} %back.1), calls=%async_computation.3 | async-start | bytes 2359296 | tf_op jit(solution)/shard_map/all_to_all | solution.py:506
  74.9 4.4 %collective-permute-start.9 = (bf16[32,1152]{1,0:T(8,128)(2,1)S(1)}, bf16[32,1152]{1,0:T(8,128)(2,1)S(1)}, u32[]{:S(2)}, u32[]{:S(2)}) collective-permute-start(bf16[32,1152]{1,0:T(8,128)(2,1)S(1)} %get-tuple-element.63), channel_id=1, source_target_pairs={{0,16},{8,24},{16,0},{24,8},{32,48},{40,56},{48,32},{56,40},{64,80... | collective-permute-start | bytes 221192 | tf_op jit(solution)/shard_map/ppermute | solution.py:27
  79.3 8.2 %collective-permute-start.10 = (bf16[8,1152]{1,0:T(8,128)(2,1)S(1)}, bf16[8,1152]{1,0:T(8,128)(2,1)S(1)}, u32[]{:S(2)}, u32[]{:S(2)}) collective-permute-start(bf16[8,1152]{1,0:T(8,128)(2,1)S(1)} %get-tuple-element.67), channel_id=1, source_target_pairs={{0,64},{8,72},{16,80},{24,88},{32,96},{40,104},{48,112},{56,120},{... | collective-permute-start | bytes 55304 | tf_op jit(solution)/shard_map/ppermute | solution.py:27
  85.3 4.7 %collective-permute-start.11 = (bf16[8,1152]{1,0:T(8,128)(2,1)S(1)}, bf16[8,1152]{1,0:T(8,128)(2,1)S(1)}, u32[]{:S(2)}, u32[]{:S(2)}) collective-permute-start(bf16[8,1152]{1,0:T(8,128)(2,1)S(1)} %get-tuple-element.68), channel_id=1, source_target_pairs={{0,32},{8,40},{16,48},{24,56},{32,0},{40,8},{48,16},{56,24},{64,96... | collective-permute-start | bytes 55304 | tf_op jit(solution)/shard_map/ppermute | solution.py:27
  86.8 5.9 %collective-permute-start.12 = (bf16[8,1152]{1,0:T(8,128)(2,1)S(1)}, bf16[8,1152]{1,0:T(8,128)(2,1)S(1)}, u32[]{:S(2)}, u32[]{:S(2)}) collective-permute-start(bf16[8,1152]{1,0:T(8,128)(2,1)S(1)} %get-tuple-element.69), channel_id=1, source_target_pairs={{0,96},{8,104},{16,112},{24,120},{32,64},{40,72},{48,80},{56,88},{... | collective-permute-start | bytes 55304 | tf_op jit(solution)/shard_map/ppermute | solution.py:27
  (2 other events, 1.7 us)

commit v7 on v5

--- a/solution.py
+++ b/solution.py
@@ -12,7 +12,7 @@
 BF16 = jnp.bfloat16
 
 VMEM_LIMIT = 16 * 1024 * 1024
-VMEM_LARGE = 60_000_000
+VMEM_BACK = 40_000_000
 VMEM_IMAGE = 28_000_000
 KEPT_ROWS = 96
 STASH_ROWS = 15_616
@@ -172,13 +172,12 @@
     text_ref[...] = unit.astype(BF16)
 
 
-def pair_body(place, scalars, got_ref, text_ref, d_image_ref, coefficient_ref, image_ref, loss_ref):
+def pair_body(place, scalars, got_ref, text_ref, d_image_ref, loss_ref, keep_ref, *send_refs):
     loaders, got_rows, width = got_ref.shape
     slots = d_image_ref.shape[1]
     images = jnp.concatenate(
         [got_ref[s].astype(F32)[got_rows - slots :] for s in range(loaders)], axis=0
     ).astype(BF16)
-    image_ref[...] = images
     texts = text_ref[...]
     count = images.shape[0]
     text_count = texts.shape[0]
@@ -194,23 +193,23 @@
     losses = jnp.maximum(signed, 0.0) + jnp.log1p(decay)
     sigmoid = jnp.where(logits >= 0.0, 1.0, decay) / (1.0 + decay)
     coefficient = (scale * (sigmoid - matched)).astype(BF16)
-    coefficient_ref[...] = coefficient
     d_image = jnp.dot(coefficient, texts, preferred_element_type=F32)
     d_image_ref[...] = d_image.reshape(d_image_ref.shape).astype(BF16)
+    d_text = tn_dot(coefficient, images)
+    part = keep_ref.shape[0]
+    keep_ref[...] = d_text[:part]
+    for k, send_ref in enumerate(send_refs):
+        send_ref[...] = d_text[(k + 1) * part : (k + 2) * part].astype(BF16)
     per_image = jnp.sum(losses, axis=-1, keepdims=True)
     per_owner = jnp.sum(per_image.reshape(loaders, slots, 1), axis=0)
     loss_ref[...] = jnp.broadcast_to(per_owner, loss_ref.shape)
 
 
-def text_body(coefficient_ref, image_ref, keep_ref, send_ref):
-    d_text = tn_dot(coefficient_ref[...], image_ref[...])
-    half = keep_ref.shape[0]
-    keep_ref[...] = d_text[:half]
-    send_ref[...] = d_text[half:].astype(BF16)
-
-
-def fold_body(total_ref, got_ref, keep_ref, send_ref):
-    total = total_ref[...] + got_ref[...].astype(F32)
+def fold_body(total_ref, *refs):
+    *got_refs, keep_ref, send_ref = refs
+    total = total_ref[...]
+    for got_ref in got_refs:
+        total = total + got_ref[...].astype(F32)
     half = keep_ref.shape[0]
     keep_ref[...] = total[:half]
     send_ref[...] = total[half:].astype(BF16)
@@ -234,8 +233,8 @@
 
 
 def back_body(
-    owners_in, got_in, full_in, x_in, side_in, loss_in, out_ref,
-    owners, got_ref, full, x_ref, side_ref, loss_ref, normed_ref, scaled_ref, right, result, sems,
+    owners_in, got_ref, full_in, x_in, side_in, loss_in, out_ref,
+    owners, full, x_ref, side_ref, loss_ref, normed_ref, scaled_ref, right, result, sems,
 ):
     slots, rows, width = x_ref.shape
     lanes = side_ref.shape[1] // 2
@@ -246,7 +245,6 @@
     rows_of = [pl.ds(width, KEPT_ROWS)] + [pl.ds(c * chunk, chunk) for c in range(3)]
     pairs = [
         (full_in.at[rows_of[0], :], full.at[rows_of[0], :]),
-        (got_in, got_ref),
         (owners_in, owners),
         (side_in, side_ref),
         (x_in.at[0], x_ref),
@@ -259,7 +257,6 @@
     for copy in copies:
         copy.start()
     copies[0].wait()
-    copies[1].wait()
     d_image = jnp.sum(got_ref[...].astype(F32), axis=0)
     kept = full[width:, :].astype(F32)
 
@@ -272,9 +269,8 @@
     d_context = d_context.astype(BF16).astype(F32)
     right[lanes:, :] = jnp.concatenate([kept[80 : 80 + heads]] * slots, axis=0).astype(BF16)
     spread = (d_context[:, None, :] * head_mask(heads, width)[None]).reshape(lanes, width).astype(BF16)
-    copies[2].wait()
-    copies[3].wait()
-    copies[4].wait()
+    for copy in copies[1:4]:
+        copy.wait()
     for r in range(slots):
         at = slice(r * rows, (r + 1) * rows)
         x = x_ref[source_of(owners, r, slots)].astype(F32)
@@ -282,7 +278,7 @@
         normed_ref[at, :] = normed
         scaled_ref[at, :] = (normed * gain).astype(BF16)
     for c in range(3):
-        copies[5 + c].wait()
+        copies[4 + c].wait()
         at = slice(c * chunk, (c + 1) * chunk)
         right[0:lanes, at] = nt_dot(spread, full[at, :]).astype(BF16)
     scaled = scaled_ref[...]
@@ -318,7 +314,7 @@
         sent.append(copy)
     probe_total = jnp.sum(tn_dot(d_scores, scaled).reshape(slots, heads, width), axis=0)
     gain_sum = jnp.sum(gain_total, axis=0, keepdims=True)
-    copies[8].wait()
+    copies[7].wait()
     high, middle, low = terms(loss_ref[...])
     pad = jnp.zeros((8, 256 - cut), F32)
     for p in range(slots):
@@ -451,16 +447,16 @@
     full, flanks = lax.optimization_barrier((full, flanks))
     got = lax.all_to_all(sent, "fsdp", 0, 0, tiled=True)
     texts = jnp.concatenate([texts] + flanks, axis=0)
-    count = peers * slots
     text_count = ranks * slots
-    d_image_part, coefficient, images, loss_sums = call(
+    parts_of = len(bits) + 1
+    d_image_part, loss_sums, keep, *sends = call(
         pair_body,
         [
             (shape((peers, slots, width), BF16), vspec()),
-            (shape((count, text_count), BF16), vspec()),
-            (shape((count, width), BF16), vspec()),
             (shape((slots, 128), F32), vspec()),
-        ],
+            (shape((text_count // parts_of, width), F32), vspec()),
+        ]
+        + [(shape((text_count // parts_of, width), BF16), vspec())] * len(bits),
         [sspec(), sspec(), vspec(), vspec()],
         80_000_000,
         2_000_000,
@@ -474,30 +470,25 @@
             (shape((rows_out, width), BF16), vspec()),
         ]
 
-    def fold(keep, send, bit):
-        if bit >= ranks:
-            return keep, send
-        return call(
-            fold_body, halves(keep.shape[0] // 2), [vspec(), vspec()], 40_000_000, 1_000_000, name="fold"
-        )(keep, swapped(send, bit))
-
-    keep, send = call(
-        text_body, halves(text_count // 2), [vspec(), vspec()], 0, 0, name="text"
-    )(coefficient, images)
+    send = sends[0]
     if ranks > 2:
-        keep, send = fold(keep, send, CORE_BIT)
-    if ranks > 2:
-        keep, send = fold(keep, send, SIDE_BIT)
+        keep, send = call(
+            fold_body,
+            halves(keep.shape[0] // 2),
+            [vspec()] * (1 + len(bits)),
+            40_000_000,
+            1_000_000,
+            name="fold",
+        )(keep, *[swapped(block, bit) for block, bit in zip(sends, bits)])
 
     outgoing = call(
         back_body,
         [(shape((peers, rows + 16, width), BF16), hspec())],
-        [hspec()] * 6,
+        [hspec(), vspec()] + [hspec()] * 4,
         500_000_000,
         8_000_000,
         [
             pltpu.SMEM((slots,), jnp.int32),
-            pltpu.VMEM((peers, slots, width), BF16),
             pltpu.VMEM((width + KEPT_ROWS, width), BF16),
             pltpu.VMEM((slots, rows, width), BF16),
             pltpu.VMEM((slots * rows, 2 * lanes), F32),
@@ -509,7 +500,7 @@
             dma((12,)),
         ],
         name="back",
-        limit=40_000_000,
+        limit=VMEM_BACK,
     )(owners[0], d_image_got, full, patches, side, loss_sums)[0]
     outgoing, keep, send = lax.optimization_barrier((outgoing, keep, send))
     arrived = lax.all_to_all(outgoing, "fsdp", 0, 0, tiled=True)
@@ -562,6 +553,7 @@
         0,
         name="finish",
     )(d_caption, caption_unit, caption_inv, *blocks)[0]
+
     return (loss_part, row_grad, text_grad[None], value_grad, probe_t.T[None], gain_grad)
 
 

time: 96.6 us -> 95.1 us (0.984)
  waiting for transfers between devices: 32.5 us -> 30.7 us
  Pallas kernels: 15.4 us -> 14.3 us
  starting transfers between devices: 41.2 us -> 42.2 us
    all_to_all x1, waiting for transfers between devices: 6.21 us -> 4.6 us  [local(): arrived = lax.all_to_all(outgoing, 'fsdp', 0, 0, tiled=True)]
    ppermute x13 -> x14, starting transfers between devices: 22.7 us -> 23.7 us  [swapped(): lax.ppermute(block, 'dp', [(i, i ^ bit) for i in range(lax.axis_size('dp'...]
    pallas_call x4 -> x2, Pallas kernels: 2.93 us -> 1.99 us  [the longest x1 1.92 us: local(): call(pair_body, [(shape((peers, slots, width), BF16), vspec()), (shape((s...]
    ppermute x13 -> x14, waiting for transfers between devices: 9.24 us -> 9.25 us  [swapped(): lax.ppermute(block, 'dp', [(i, i ^ bit) for i in range(lax.axis_size('dp'...]
  transfers between devices with their start and end apart: 17 -> 18, of which waited for: 9 -> 9; matrix products, arithmetic and copies ran while one was open for 2% -> 2% of each run, Pallas kernels for 13% -> 12%
where the time goes in v7:
time: 95.1 us; the launch traced here: 94.1 us
  starting transfers between devices  42.2 us (44%)
  waiting for transfers between devices  30.7 us (32%)
  Pallas kernels  14.3 us (15%)
  local copies, waits for them, and re-layouts  3.58 us (4%)
  between operations  2.15 us (2%)
  other arithmetic  1.2 us (1%)
    ppermute x14, starting transfers between devices, swapped(): lax.ppermute(block, 'dp', [(i, i ^ bit) for i in range(lax.axis_size('dp'...  23.7 us
    ppermute x14, waiting for transfers between devices, swapped(): lax.ppermute(block, 'dp', [(i, i ^ bit) for i in range(lax.axis_size('dp'...  9.25 us
    all_to_all x1, waiting for transfers between devices, local(): got = lax.all_to_all(sent, 'fsdp', 0, 0, tiled=True)  8.52 us
    all_to_all x1, waiting for transfers between devices, local(): d_image_got = lax.all_to_all(d_image_part, 'fsdp', 0, 0, tiled=True)  6.34 us
    all_to_all x1, starting transfers between devices, local(): lax.all_to_all(jnp.broadcast_to(part[None], (peers, SEND_ROWS, width)), '...  6.18 us
    all_to_all x1, starting transfers between devices, local(): got = lax.all_to_all(sent, 'fsdp', 0, 0, tiled=True)  5.37 us
    pallas_call x1, Pallas kernels, local(): call(back_body, [(shape((peers, rows + 16, width), BF16), hspec())], [hsp...  5.12 us
    all_to_all x1, waiting for transfers between devices, local(): arrived = lax.all_to_all(outgoing, 'fsdp', 0, 0, tiled=True)  4.6 us
  transfers between devices with their start and end apart: 18, of which 9 were waited for; matrix products, arithmetic and copies ran while one was open for 2% of the time, Pallas kernels for 12%

profile of v7, /device:TPU:2, one launch (start us, length us, event | category | flops | bytes accessed | tf_op | source)
XLA Modules:
  0.0 94.1 jit_solution(2798899395559007280)
XLA Ops:
  1.6 1.2 %broadcast_in_dim.12 = bf16[8,72,1152]{2,1,0:T(8,128)(2,1)} broadcast(bf16[72,1152]{1,0:T(8,128)(2,1)S(1)} %constant_dynamic-slice_fusion), dimensions={1,2} | broadcast | bytes 1492992 | tf_op jit(solution)/shard_map/broadcast_in_dim | solution.py:398
  2.8 6.2 %all-to-all-start = ((bf16[8,72,1152]{2,1,0:T(8,128)(2,1)}), bf16[8,72,1152]{2,1,0:T(8,128)(2,1)S(1)}, u32[]{:S(2)}, u32[]{:S(2)}) async-start(bf16[8,72,1152]{2,1,0:T(8,128)(2,1)} %broadcast_in_dim.12), calls=%async_computation | async-start | bytes 2654208 | tf_op jit(solution)/shard_map/all_to_all | solution.py:397
  9.1 7.2 %collective-permute-start = (bf16[8,1152]{1,0:T(8,128)(2,1)S(1)}, bf16[8,1152]{1,0:T(8,128)(2,1)S(1)}, u32[]{:S(2)}, u32[]{:S(2)}) collective-permute-start(bf16[8,1152]{1,0:T(8,128)(2,1)S(1)} %get-tuple-element.44), channel_id=1, source_target_pairs={{0,64},{8,72},{16,80},{24,88},{32,96},{40,104},{48,112},{56,120},{... | collective-permute-start | bytes 55304 | tf_op jit(solution)/shard_map/ppermute | solution.py:27
  16.3 1.7 %collective-permute-done = bf16[8,1152]{1,0:T(8,128)(2,1)S(1)} collective-permute-done((bf16[8,1152]{1,0:T(8,128)(2,1)S(1)}, bf16[8,1152]{1,0:T(8,128)(2,1)S(1)}, u32[]{:S(2)}, u32[]{:S(2)}) %collective-permute-start) | collective-permute-done | bytes 18464 | tf_op jit(solution)/shard_map/ppermute | solution.py:27
  18.1 2.0 %collective-permute-start.1 = (bf16[16,1152]{1,0:T(8,128)(2,1)S(1)}, bf16[16,1152]{1,0:T(8,128)(2,1)S(1)}, u32[]{:S(2)}, u32[]{:S(2)}) collective-permute-start(bf16[16,1152]{1,0:T(8,128)(2,1)S(1)} %pad_maximum_fusion.3), channel_id=1, source_target_pairs={{0,32},{8,40},{16,48},{24,56},{32,0},{40,8},{48,16},{56,24},{64,96... | collective-permute-start | bytes 110600 | tf_op jit(solution)/shard_map/ppermute | solution.py:27
  20.1 2.8 %collective-permute-done.1 = bf16[16,1152]{1,0:T(8,128)(2,1)S(1)} collective-permute-done((bf16[16,1152]{1,0:T(8,128)(2,1)S(1)}, bf16[16,1152]{1,0:T(8,128)(2,1)S(1)}, u32[]{:S(2)}, u32[]{:S(2)}) %collective-permute-start.1) | collective-permute-done | bytes 36896 | tf_op jit(solution)/shard_map/ppermute | solution.py:27
  24.0 2.1 %pool.1 = (f32[384,256]{1,0:T(8,128)S(1)}, bf16[128,1152]{1,0:T(8,128)(2,1)S(1)}) custom-call(s32[8]{0:T(128)S(1)} %bitcast.19, s32[8]{0:T(128)S(1)} %bitcast.21, bf16[8,48,1152]{2,1,0:T(8,128)(2,1)S(1)} %bitcast.15, f32[1,1152]{1,0:T(1,128)S(1)} %reshape.26.gain_ref, bf16[16,1152]{1,0:T(8,128)(2,1)S(1)} %bitcast.17), custom_call_target="tpu_custom_call" | custom-call | flops 40000000 | bytes 4000000 | tf_op jit(solution)/shard_map/pool/pallas_call | solution.py:402
  27.3 1.9 %all-to-all-done.mine_ref = bf16[8,72,1152]{2,1,0:T(8,128)(2,1)S(1)} async-done(((bf16[8,72,1152]{2,1,0:T(8,128)(2,1)}), bf16[8,72,1152]{2,1,0:T(8,128)(2,1)S(1)}, u32[]{:S(2)}, u32[]{:S(2)}) %all-to-all-start) | async-done | bytes 1327136 | tf_op jit(solution)/shard_map/all_to_all | solution.py:397
  29.3 1.4 %collective-permute-start.4 = (bf16[64,1152]{1,0:T(8,128)(2,1)S(1)}, bf16[64,1152]{1,0:T(8,128)(2,1)}, u32[]{:S(2)}, u32[]{:S(2)}) collective-permute-start(bf16[64,1152]{1,0:T(8,128)(2,1)S(1)} %pad_maximum_fusion.1), channel_id=1, source_target_pairs={{0,128},{8,136},{16,144},{24,152},{32,160},{40,168},{48,176},{56,1... | collective-permute-start | bytes 442376 | tf_op jit(solution)/shard_map/ppermute | solution.py:27
  32.3 2.6 %image.1 = (bf16[15616,1152]{1,0:T(8,128)(2,1)}, bf16[8,24,1152]{2,1,0:T(8,128)(2,1)}) custom-call(bf16[8,72,1152]{2,1,0:T(8,128)(2,1)S(1)} %all-to-all-done.mine_ref, bf16[8,72,1152]{2,1,0:T(8,128)(2,1)S(1)} %collective-permute-done.3.other_ref, bf16[128,1152]{1,0:T(8,128)(2,1)S(1)} %get-tuple-element.47.a_ref, f32[1,1152]{1,0:T(1,128)S(1)} %reshape.26.gain_ref, ...), custom_call_target="tpu_custom_call" | custom-call | flops 400000000 | bytes 6000000 | tf_op jit(solution)/shard_map/image/pallas_call | solution.py:434
  34.9 5.4 %all-to-all-start.1 = ((bf16[8,24,1152]{2,1,0:T(8,128)(2,1)}), bf16[8,24,1152]{2,1,0:T(8,128)(2,1)S(1)}, u32[]{:S(2)}, u32[]{:S(2)}) async-start(bf16[8,24,1152]{2,1,0:T(8,128)(2,1)} %get-tuple-element.48), calls=%async_computation.1 | async-start | bytes 884736 | tf_op jit(solution)/shard_map/all_to_all | solution.py:448
  42.7 8.5 %all-to-all-done.1.got_ref = bf16[8,24,1152]{2,1,0:T(8,128)(2,1)S(1)} async-done(((bf16[8,24,1152]{2,1,0:T(8,128)(2,1)}), bf16[8,24,1152]{2,1,0:T(8,128)(2,1)S(1)}, u32[]{:S(2)}, u32[]{:S(2)}) %all-to-all-start.1) | async-done | bytes 442400 | tf_op jit(solution)/shard_map/all_to_all | solution.py:448
  51.3 1.9 %pair.1 = (bf16[8,8,1152]{2,1,0:T(8,128)(2,1)}, f32[8,128]{1,0:T(8,128)S(1)}, f32[64,1152]{1,0:T(8,128)S(1)}, bf16[64,1152]{1,0:T(8,128)(2,1)S(1)}, bf16[64,1152...) custom-call(s32[1]{0:T(128)} %bitcast.1.place, f32[2]{0:T(128)S(1)} %pad_maximum_fusion.4.scalars, ...), custom_call_target="tpu_custom_call" | custom-call | flops 80000000 | bytes 2000000 | tf_op jit(solution)/shard_map/pair/pallas_call | solution.py:452
  53.8 3.4 %all-to-all-start.2 = ((bf16[8,8,1152]{2,1,0:T(8,128)(2,1)}), bf16[8,8,1152]{2,1,0:T(8,128)(2,1)S(1)}, u32[]{:S(2)}, u32[]{:S(2)}) async-start(bf16[8,8,1152]{2,1,0:T(8,128)(2,1)} %get-tuple-element.54), calls=%async_computation.2 | async-start | bytes 294912 | tf_op jit(solution)/shard_map/all_to_all | solution.py:465
  57.2 1.5 %collective-permute-start.7 = (bf16[64,1152]{1,0:T(8,128)(2,1)}, bf16[64,1152]{1,0:T(8,128)(2,1)S(1)}, u32[]{:S(2)}, u32[]{:S(2)}) collective-permute-start(bf16[64,1152]{1,0:T(8,128)(2,1)} %copy-done.5), channel_id=1, source_target_pairs={{0,128},{8,136},{16,144},{24,152},{32,160},{40,168},{48,176},{56,1... | collective-permute-start | bytes 442376 | tf_op jit(solution)/shard_map/ppermute | solution.py:27
  59.4 6.3 %all-to-all-done.2.got_ref = bf16[8,8,1152]{2,1,0:T(8,128)(2,1)S(1)} async-done(((bf16[8,8,1152]{2,1,0:T(8,128)(2,1)}), bf16[8,8,1152]{2,1,0:T(8,128)(2,1)S(1)}, u32[]{:S(2)}, u32[]{:S(2)}) %all-to-all-start.2) | async-done | bytes 147488 | tf_op jit(solution)/shard_map/all_to_all | solution.py:465
  65.8 5.1 %back.1 = bf16[8,64,1152]{2,1,0:T(8,128)(2,1)} custom-call(s32[8]{0:T(128)S(1)} %bitcast.20, bf16[8,8,1152]{2,1,0:T(8,128)(2,1)S(1)} %all-to-all-done.2.got_ref, bf16[15616,1152]{1,0:T(8,128)(2,1)} %get-tuple-element.55.full_in, bf16[1,8,48,1152]{3,2,1,0:T(8,128)(2,1)S(1)} %copy-done.1, f32[384,256]{1,0:T(8,128)S(1)} %get-tuple-element.56.side_in, ...), custom_call_target="tpu_custom_call" | custom-call | flops 500000000 | bytes 8000000 | tf_op jit(solution)/shard_map/back/pallas_call | solution.py:484
  71.0 3.6 %all-to-all-start.3 = ((bf16[8,64,1152]{2,1,0:T(8,128)(2,1)}), bf16[8,64,1152]{2,1,0:T(8,128)(2,1)S(1)}, u32[]{:S(2)}, u32[]{:S(2)}) async-start(bf16[8,64,1152]{2,1,0:T(8,128)(2,1)} %back.1), calls=%async_computation.3 | async-start | bytes 2359296 | tf_op jit(solution)/shard_map/all_to_all | solution.py:506
  74.6 1.3 %collective-permute-start.10 = (bf16[32,1152]{1,0:T(8,128)(2,1)S(1)}, bf16[32,1152]{1,0:T(8,128)(2,1)S(1)}, u32[]{:S(2)}, u32[]{:S(2)}) collective-permute-start(bf16[32,1152]{1,0:T(8,128)(2,1)S(1)} %get-tuple-element.67), channel_id=1, source_target_pairs={{0,16},{8,24},{16,0},{24,8},{32,48},{40,56},{48,32},{56,40},{64,80... | collective-permute-start | bytes 221192 | tf_op jit(solution)/shard_map/ppermute | solution.py:27
  76.6 2.6 %collective-permute-done.10.got_ref = bf16[32,1152]{1,0:T(8,128)(2,1)S(1)} collective-permute-done((bf16[32,1152]{1,0:T(8,128)(2,1)S(1)}, bf16[32,1152]{1,0:T(8,128)(2,1)S(1)}, u32[]{:S(2)}, u32[]{:S(2)}) %collective-permute-start.10) | collective-permute-done | bytes 73760 | tf_op jit(solution)/shard_map/ppermute | solution.py:27
  79.2 6.0 %collective-permute-start.11 = (bf16[8,1152]{1,0:T(8,128)(2,1)S(1)}, bf16[8,1152]{1,0:T(8,128)(2,1)S(1)}, u32[]{:S(2)}, u32[]{:S(2)}) collective-permute-start(bf16[8,1152]{1,0:T(8,128)(2,1)S(1)} %get-tuple-element.68), channel_id=1, source_target_pairs={{0,64},{8,72},{16,80},{24,88},{32,96},{40,104},{48,112},{56,120},{... | collective-permute-start | bytes 55304 | tf_op jit(solution)/shard_map/ppermute | solution.py:27
  85.3 1.8 %collective-permute-start.12 = (bf16[8,1152]{1,0:T(8,128)(2,1)S(1)}, bf16[8,1152]{1,0:T(8,128)(2,1)S(1)}, u32[]{:S(2)}, u32[]{:S(2)}) collective-permute-start(bf16[8,1152]{1,0:T(8,128)(2,1)S(1)} %get-tuple-element.69), channel_id=1, source_target_pairs={{0,32},{8,40},{16,48},{24,56},{32,0},{40,8},{48,16},{56,24},{64,96... | collective-permute-start | bytes 55304 | tf_op jit(solution)/shard_map/ppermute | solution.py:27
  87.1 4.6 %all-to-all-done.3.refs_0_ = bf16[8,64,1152]{2,1,0:T(8,128)(2,1)S(1)} async-done(((bf16[8,64,1152]{2,1,0:T(8,128)(2,1)}), bf16[8,64,1152]{2,1,0:T(8,128)(2,1)S(1)}, u32[]{:S(2)}, u32[]{:S(2)}) %all-to-all-start.3) | async-done | bytes 1179680 | tf_op jit(solution)/shard_map/all_to_all | solution.py:506
  91.7 1.7 %last.1 = (bf16[1,8,48,1152]{3,2,1,0:T(8,128)(2,1)}, bf16[1,144,1152]{2,1,0:T(8,128)(2,1)}, bf16[16,144]{1,0:T(8,128)(2,1)}, bf16[1,144]{1,0:T(2,128)(2,1)}, f32[1,1]{1,0:T(1,128)}) custom-call(bf16[8,64,1152]{2,1,0:T(8,128)(2,1)S(1)} %all-to-all-done.3.refs_0_, bf16[16,64,144]{2,1,0:T(8,128)(2,1)S(1)} %bitcast.16), custom_call_target="tpu_custom_call" | custom-call | flops 400000000 | bytes 3000000 | tf_op jit(solution)/shard_map/last/pallas_call | solution.py:531
  (48 shorter events, 9.0 us)
Async XLA Ops:
  2.8 6.2 %copy-start.6 = (bf16[1,8,1152]{2,1,0:T(8,128)(2,1)S(1)}, bf16[1,8,1152]{2,1,0:T(8,128)(2,1)}, u32[]{:S(2)}) copy-start(bf16[1,8,1152]{2,1,0:T(8,128)(2,1)} %param.12) | copy-start | bytes 55300
  2.8 21.2 %copy-start.7 = (f32[1152]{0:T(1024)S(1)}, f32[1152]{0:T(1024)}, u32[]{:S(2)}) copy-start(f32[1152]{0:T(1024)} %param.13) | copy-start | bytes 13828
  2.8 21.2 %copy-start.1 = (bf16[1,8,48,1152]{3,2,1,0:T(8,128)(2,1)S(1)}, bf16[1,8,48,1152]{3,2,1,0:T(8,128)(2,1)}, u32[]{:S(2)}) copy-start(bf16[1,8,48,1152]{3,2,1,0:T(8,128)(2,1)} %x_in.1) | copy-start | bytes 2654212
  2.8 21.2 %copy-start.2 = (bf16[1152,16]{0,1:T(8,128)(2,1)S(1)}, bf16[1152,16]{0,1:T(8,128)(2,1)}, u32[]{:S(2)}) copy-start(bf16[1152,16]{0,1:T(8,128)(2,1)} %param.14) | copy-start | bytes 110596
  2.8 21.2 %copy-start.3 = (s32[1,8]{1,0:T(1,128)S(1)}, s32[1,8]{1,0:T(1,128)}, u32[]{:S(2)}) copy-start(s32[1,8]{1,0:T(1,128)} %param.11) | copy-start | bytes 100
  2.8 21.2 %copy-start.4 = (s32[1,8]{1,0:T(1,128)S(1)}, s32[1,8]{1,0:T(1,128)}, u32[]{:S(2)}) copy-start(s32[1,8]{1,0:T(1,128)} %param.10) | copy-start | bytes 100
  2.8 26.4 %all-to-all-start = ((bf16[8,72,1152]{2,1,0:T(8,128)(2,1)}), bf16[8,72,1152]{2,1,0:T(8,128)(2,1)S(1)}, u32[]{:S(2)}, u32[]{:S(2)}) async-start(bf16[8,72,1152]{2,1,0:T(8,128)(2,1)} %broadcast_in_dim.12), calls=%async_computation | async-start | bytes 2654208 | tf_op jit(solution)/shard_map/all_to_all | solution.py:397
  9.1 8.9 %collective-permute-start = (bf16[8,1152]{1,0:T(8,128)(2,1)S(1)}, bf16[8,1152]{1,0:T(8,128)(2,1)S(1)}, u32[]{:S(2)}, u32[]{:S(2)}) collective-permute-start(bf16[8,1152]{1,0:T(8,128)(2,1)S(1)} %get-tuple-element.44), channel_id=1, source_target_pairs={{0,64},{8,72},{16,80},{24,88},{32,96},{40,104},{48,112},{56,120},{... | collective-permute-start | bytes 55304 | tf_op jit(solution)/shard_map/ppermute | solution.py:27
  18.1 4.9 %collective-permute-start.1 = (bf16[16,1152]{1,0:T(8,128)(2,1)S(1)}, bf16[16,1152]{1,0:T(8,128)(2,1)S(1)}, u32[]{:S(2)}, u32[]{:S(2)}) collective-permute-start(bf16[16,1152]{1,0:T(8,128)(2,1)S(1)} %pad_maximum_fusion.3), channel_id=1, source_target_pairs={{0,32},{8,40},{16,48},{24,56},{32,0},{40,8},{48,16},{56,24},{64,96... | collective-permute-start | bytes 110600 | tf_op jit(solution)/shard_map/ppermute | solution.py:27
  22.9 4.4 %collective-permute-start.2 = (bf16[32,1152]{1,0:T(8,128)(2,1)S(1)}, bf16[32,1152]{1,0:T(8,128)(2,1)S(1)}, u32[]{:S(2)}, u32[]{:S(2)}) collective-permute-start(bf16[32,1152]{1,0:T(8,128)(2,1)S(1)} %pad_maximum_fusion.2), channel_id=1, source_target_pairs={{0,16},{8,24},{16,0},{24,8},{32,48},{40,56},{48,32},{56,40},{64,80... | collective-permute-start | bytes 221192 | tf_op jit(solution)/shard_map/ppermute | solution.py:27
  29.2 3.1 %collective-permute-start.3 = (bf16[8,72,1152]{2,1,0:T(8,128)(2,1)S(1)}, bf16[8,72,1152]{2,1,0:T(8,128)(2,1)S(1)}, u32[]{:S(2)}, u32[]{:S(2)}) collective-permute-start(bf16[8,72,1152]{2,1,0:T(8,128)(2,1)S(1)} %all-to-all-done.mine_ref), channel_id=1, source_target_pairs={{0,8},{8,0},{16,24},{24,16},{32,40},{40,32},{48,56},{56,48},{64,72... | collective-permute-start | bytes 3981320 | tf_op jit(solution)/shard_map/ppermute | solution.py:27
  29.3 12.4 %collective-permute-start.4 = (bf16[64,1152]{1,0:T(8,128)(2,1)S(1)}, bf16[64,1152]{1,0:T(8,128)(2,1)}, u32[]{:S(2)}, u32[]{:S(2)}) collective-permute-start(bf16[64,1152]{1,0:T(8,128)(2,1)S(1)} %pad_maximum_fusion.1), channel_id=1, source_target_pairs={{0,128},{8,136},{16,144},{24,152},{32,160},{40,168},{48,176},{56,1... | collective-permute-start | bytes 442376 | tf_op jit(solution)/shard_map/ppermute | solution.py:27
  30.7 10.9 %collective-permute-start.5 = (bf16[64,1152]{1,0:T(8,128)(2,1)S(1)}, bf16[64,1152]{1,0:T(8,128)(2,1)}, u32[]{:S(2)}, u32[]{:S(2)}) collective-permute-start(bf16[64,1152]{1,0:T(8,128)(2,1)S(1)} %pad_maximum_fusion.1), channel_id=1, source_target_pairs={{0,8},{8,0},{16,24},{24,16},{32,40},{40,32},{48,56},{56,48},{64,72... | collective-permute-start | bytes 442376 | tf_op jit(solution)/shard_map/ppermute | solution.py:27
  30.9 10.7 %collective-permute-start.6 = (bf16[64,1152]{1,0:T(8,128)(2,1)S(1)}, bf16[64,1152]{1,0:T(8,128)(2,1)}, u32[]{:S(2)}, u32[]{:S(2)}) collective-permute-start(bf16[64,1152]{1,0:T(8,128)(2,1)S(1)} %pad_maximum_fusion.1), channel_id=1, source_target_pairs={{0,136},{8,128},{16,152},{24,144},{32,168},{40,160},{48,184},{56,1... | collective-permute-start | bytes 442376 | tf_op jit(solution)/shard_map/ppermute | solution.py:27
  34.9 16.4 %all-to-all-start.1 = ((bf16[8,24,1152]{2,1,0:T(8,128)(2,1)}), bf16[8,24,1152]{2,1,0:T(8,128)(2,1)S(1)}, u32[]{:S(2)}, u32[]{:S(2)}) async-start(bf16[8,24,1152]{2,1,0:T(8,128)(2,1)} %get-tuple-element.48), calls=%async_computation.1 | async-start | bytes 884736 | tf_op jit(solution)/shard_map/all_to_all | solution.py:448
  53.8 12.0 %all-to-all-start.2 = ((bf16[8,8,1152]{2,1,0:T(8,128)(2,1)}), bf16[8,8,1152]{2,1,0:T(8,128)(2,1)S(1)}, u32[]{:S(2)}, u32[]{:S(2)}) async-start(bf16[8,8,1152]{2,1,0:T(8,128)(2,1)} %get-tuple-element.54), calls=%async_computation.2 | async-start | bytes 294912 | tf_op jit(solution)/shard_map/all_to_all | solution.py:465
  57.2 13.7 %collective-permute-start.7 = (bf16[64,1152]{1,0:T(8,128)(2,1)}, bf16[64,1152]{1,0:T(8,128)(2,1)S(1)}, u32[]{:S(2)}, u32[]{:S(2)}) collective-permute-start(bf16[64,1152]{1,0:T(8,128)(2,1)} %copy-done.5), channel_id=1, source_target_pairs={{0,128},{8,136},{16,144},{24,152},{32,160},{40,168},{48,176},{56,1... | collective-permute-start | bytes 442376 | tf_op jit(solution)/shard_map/ppermute | solution.py:27
  58.7 12.2 %collective-permute-start.8 = (bf16[64,1152]{1,0:T(8,128)(2,1)S(1)}, bf16[64,1152]{1,0:T(8,128)(2,1)S(1)}, u32[]{:S(2)}, u32[]{:S(2)}) collective-permute-start(bf16[64,1152]{1,0:T(8,128)(2,1)S(1)} %get-tuple-element.60), channel_id=1, source_target_pairs={{0,8},{8,0},{16,24},{24,16},{32,40},{40,32},{48,56},{56,48},{64,72... | collective-permute-start | bytes 442376 | tf_op jit(solution)/shard_map/ppermute | solution.py:27
  58.7 12.2 %collective-permute-start.9 = (bf16[64,1152]{1,0:T(8,128)(2,1)S(1)}, bf16[64,1152]{1,0:T(8,128)(2,1)S(1)}, u32[]{:S(2)}, u32[]{:S(2)}) collective-permute-start(bf16[64,1152]{1,0:T(8,128)(2,1)S(1)} %get-tuple-element.61), channel_id=1, source_target_pairs={{0,136},{8,128},{16,152},{24,144},{32,168},{40,160},{48,184},{56,1... | collective-permute-start | bytes 442376 | tf_op jit(solution)/shard_map/ppermute | solution.py:27
  71.0 20.7 %all-to-all-start.3 = ((bf16[8,64,1152]{2,1,0:T(8,128)(2,1)}), bf16[8,64,1152]{2,1,0:T(8,128)(2,1)S(1)}, u32[]{:S(2)}, u32[]{:S(2)}) async-start(bf16[8,64,1152]{2,1,0:T(8,128)(2,1)} %back.1), calls=%async_computation.3 | async-start | bytes 2359296 | tf_op jit(solution)/shard_map/all_to_all | solution.py:506
  74.6 4.6 %collective-permute-start.10 = (bf16[32,1152]{1,0:T(8,128)(2,1)S(1)}, bf16[32,1152]{1,0:T(8,128)(2,1)S(1)}, u32[]{:S(2)}, u32[]{:S(2)}) collective-permute-start(bf16[32,1152]{1,0:T(8,128)(2,1)S(1)} %get-tuple-element.67), channel_id=1, source_target_pairs={{0,16},{8,24},{16,0},{24,8},{32,48},{40,56},{48,32},{56,40},{64,80... | collective-permute-start | bytes 221192 | tf_op jit(solution)/shard_map/ppermute | solution.py:27
  79.2 14.1 %collective-permute-start.11 = (bf16[8,1152]{1,0:T(8,128)(2,1)S(1)}, bf16[8,1152]{1,0:T(8,128)(2,1)S(1)}, u32[]{:S(2)}, u32[]{:S(2)}) collective-permute-start(bf16[8,1152]{1,0:T(8,128)(2,1)S(1)} %get-tuple-element.68), channel_id=1, source_target_pairs={{0,64},{8,72},{16,80},{24,88},{32,96},{40,104},{48,112},{56,120},{... | collective-permute-start | bytes 55304 | tf_op jit(solution)/shard_map/ppermute | solution.py:27
  85.3 8.1 %collective-permute-start.12 = (bf16[8,1152]{1,0:T(8,128)(2,1)S(1)}, bf16[8,1152]{1,0:T(8,128)(2,1)S(1)}, u32[]{:S(2)}, u32[]{:S(2)}) collective-permute-start(bf16[8,1152]{1,0:T(8,128)(2,1)S(1)} %get-tuple-element.69), channel_id=1, source_target_pairs={{0,32},{8,40},{16,48},{24,56},{32,0},{40,8},{48,16},{56,24},{64,96... | collective-permute-start | bytes 55304 | tf_op jit(solution)/shard_map/ppermute | solution.py:27
  87.1 6.3 %collective-permute-start.13 = (bf16[8,1152]{1,0:T(8,128)(2,1)S(1)}, bf16[8,1152]{1,0:T(8,128)(2,1)S(1)}, u32[]{:S(2)}, u32[]{:S(2)}) collective-permute-start(bf16[8,1152]{1,0:T(8,128)(2,1)S(1)} %get-tuple-element.70), channel_id=1, source_target_pairs={{0,96},{8,104},{16,112},{24,120},{32,64},{40,72},{48,80},{56,88},{... | collective-permute-start | bytes 55304 | tf_op jit(solution)/shard_map/ppermute | solution.py:27
  (2 other events, 1.6 us)

commit v8 on v7

--- a/solution.py
+++ b/solution.py
@@ -172,7 +172,7 @@
     text_ref[...] = unit.astype(BF16)
 
 
-def pair_body(place, scalars, got_ref, text_ref, d_image_ref, loss_ref, keep_ref, *send_refs):
+def pair_body(scalars, got_ref, text_ref, d_image_ref, loss_ref, keep_ref, *send_refs):
     loaders, got_rows, width = got_ref.shape
     slots = d_image_ref.shape[1]
     images = jnp.concatenate(
@@ -181,12 +181,12 @@
     texts = text_ref[...]
     count = images.shape[0]
     text_count = texts.shape[0]
-    scale = scalars[0]
-    logits = scale * nt_dot(images, texts) + scalars[1]
+    scale = scalars[0:1, 0:1]
+    logits = scale * nt_dot(images, texts) + scalars[1:2, 0:1]
     row = lax.broadcasted_iota(jnp.int32, (count, text_count), 0)
     column = lax.broadcasted_iota(jnp.int32, (count, text_count), 1)
     loader, owner = row // slots, row % slots
-    matched = (owner == place[0]) & (column == loader)
+    matched = (owner == lax.axis_index("fsdp")) & (column == loader)
     matched = matched.astype(F32)
     decay = jnp.exp(-jnp.abs(logits))
     signed = (1.0 - 2.0 * matched) * logits
@@ -385,8 +385,7 @@
     ranks = lax.axis_size("dp")
     cut = width // peers
     core = lax.axis_index("dp") % 2
-    place = lax.axis_index("fsdp").astype(jnp.int32).reshape(1)
-    scalars = jnp.concatenate([logit_scale, logit_bias])
+    scalars = jnp.broadcast_to(jnp.stack([logit_scale, logit_bias]), (2, 128))
     gain = norm_gain.reshape(1, width)
     probe = key_probe.T
     shape = jax.ShapeDtypeStruct
@@ -457,11 +456,11 @@
             (shape((text_count // parts_of, width), F32), vspec()),
         ]
         + [(shape((text_count // parts_of, width), BF16), vspec())] * len(bits),
-        [sspec(), sspec(), vspec(), vspec()],
+        [vspec(), vspec(), vspec()],
         80_000_000,
         2_000_000,
         name="pair",
-    )(place, scalars, got, texts)
+    )(scalars, got, texts)
     d_image_got = lax.all_to_all(d_image_part, "fsdp", 0, 0, tiled=True)
 
     def halves(rows_out):

time: 95.1 us -> 94.6 us (level)
  no operation moved by 1% of the time
where the time goes in v8:
time: 94.6 us; the launch traced here: 93.7 us
  starting transfers between devices  42.2 us (45%)
  waiting for transfers between devices  30.6 us (32%)
  Pallas kernels  13.8 us (15%)
  local copies, waits for them, and re-layouts  3.65 us (4%)
  between operations  2.15 us (2%)
  other arithmetic  1.2 us (1%)
    ppermute x14, starting transfers between devices, swapped(): lax.ppermute(block, 'dp', [(i, i ^ bit) for i in range(lax.axis_size('dp'...  23.7 us
    ppermute x14, waiting for transfers between devices, swapped(): lax.ppermute(block, 'dp', [(i, i ^ bit) for i in range(lax.axis_size('dp'...  9.24 us
    all_to_all x1, waiting for transfers between devices, local(): got = lax.all_to_all(sent, 'fsdp', 0, 0, tiled=True)  8.52 us
    all_to_all x1, waiting for transfers between devices, local(): d_image_got = lax.all_to_all(d_image_part, 'fsdp', 0, 0, tiled=True)  6.34 us
    all_to_all x1, starting transfers between devices, local(): lax.all_to_all(jnp.broadcast_to(part[None], (peers, SEND_ROWS, width)), '...  6.18 us
    all_to_all x1, starting transfers between devices, local(): got = lax.all_to_all(sent, 'fsdp', 0, 0, tiled=True)  5.37 us
    pallas_call x1, Pallas kernels, local(): call(back_body, [(shape((peers, rows + 16, width), BF16), hspec())], [hsp...  5.11 us
    all_to_all x1, waiting for transfers between devices, local(): arrived = lax.all_to_all(outgoing, 'fsdp', 0, 0, tiled=True)  4.61 us
  transfers between devices with their start and end apart: 18, of which 9 were waited for; matrix products, arithmetic and copies ran while one was open for 2% of the time, Pallas kernels for 12%

profile of v8, /device:TPU:2, one launch (start us, length us, event | category | flops | bytes accessed | tf_op | source)
XLA Modules:
  0.0 93.7 jit_solution(219267178097686711)
XLA Ops:
  1.6 1.2 %broadcast_in_dim.21 = bf16[8,72,1152]{2,1,0:T(8,128)(2,1)} broadcast(bf16[72,1152]{1,0:T(8,128)(2,1)S(1)} %constant_dynamic-slice_fusion), dimensions={1,2} | broadcast | bytes 1492992 | tf_op jit(solution)/shard_map/broadcast_in_dim | solution.py:397
  2.8 6.2 %all-to-all-start = ((bf16[8,72,1152]{2,1,0:T(8,128)(2,1)}), bf16[8,72,1152]{2,1,0:T(8,128)(2,1)S(1)}, u32[]{:S(2)}, u32[]{:S(2)}) async-start(bf16[8,72,1152]{2,1,0:T(8,128)(2,1)} %broadcast_in_dim.21), calls=%async_computation | async-start | bytes 2654208 | tf_op jit(solution)/shard_map/all_to_all | solution.py:396
  9.1 7.2 %collective-permute-start = (bf16[8,1152]{1,0:T(8,128)(2,1)S(1)}, bf16[8,1152]{1,0:T(8,128)(2,1)S(1)}, u32[]{:S(2)}, u32[]{:S(2)}) collective-permute-start(bf16[8,1152]{1,0:T(8,128)(2,1)S(1)} %get-tuple-element.44), channel_id=1, source_target_pairs={{0,64},{8,72},{16,80},{24,88},{32,96},{40,104},{48,112},{56,120},{... | collective-permute-start | bytes 55304 | tf_op jit(solution)/shard_map/ppermute | solution.py:27
  16.3 1.7 %collective-permute-done = bf16[8,1152]{1,0:T(8,128)(2,1)S(1)} collective-permute-done((bf16[8,1152]{1,0:T(8,128)(2,1)S(1)}, bf16[8,1152]{1,0:T(8,128)(2,1)S(1)}, u32[]{:S(2)}, u32[]{:S(2)}) %collective-permute-start) | collective-permute-done | bytes 18464 | tf_op jit(solution)/shard_map/ppermute | solution.py:27
  18.1 2.0 %collective-permute-start.1 = (bf16[16,1152]{1,0:T(8,128)(2,1)S(1)}, bf16[16,1152]{1,0:T(8,128)(2,1)S(1)}, u32[]{:S(2)}, u32[]{:S(2)}) collective-permute-start(bf16[16,1152]{1,0:T(8,128)(2,1)S(1)} %pad_maximum_fusion.3), channel_id=1, source_target_pairs={{0,32},{8,40},{16,48},{24,56},{32,0},{40,8},{48,16},{56,24},{64,96... | collective-permute-start | bytes 110600 | tf_op jit(solution)/shard_map/ppermute | solution.py:27
  20.1 2.8 %collective-permute-done.1 = bf16[16,1152]{1,0:T(8,128)(2,1)S(1)} collective-permute-done((bf16[16,1152]{1,0:T(8,128)(2,1)S(1)}, bf16[16,1152]{1,0:T(8,128)(2,1)S(1)}, u32[]{:S(2)}, u32[]{:S(2)}) %collective-permute-start.1) | collective-permute-done | bytes 36896 | tf_op jit(solution)/shard_map/ppermute | solution.py:27
  24.0 2.1 %pool.1 = (f32[384,256]{1,0:T(8,128)S(1)}, bf16[128,1152]{1,0:T(8,128)(2,1)S(1)}) custom-call(s32[8]{0:T(128)S(1)} %bitcast.24, s32[8]{0:T(128)S(1)} %bitcast.26, bf16[8,48,1152]{2,1,0:T(8,128)(2,1)S(1)} %bitcast.20, f32[1,1152]{1,0:T(1,128)S(1)} %reshape.22.gain_ref, bf16[16,1152]{1,0:T(8,128)(2,1)S(1)} %bitcast.22), custom_call_target="tpu_custom_call" | custom-call | flops 40000000 | bytes 4000000 | tf_op jit(solution)/shard_map/pool/pallas_call | solution.py:401
  27.3 1.9 %all-to-all-done.mine_ref = bf16[8,72,1152]{2,1,0:T(8,128)(2,1)S(1)} async-done(((bf16[8,72,1152]{2,1,0:T(8,128)(2,1)}), bf16[8,72,1152]{2,1,0:T(8,128)(2,1)S(1)}, u32[]{:S(2)}, u32[]{:S(2)}) %all-to-all-start) | async-done | bytes 1327136 | tf_op jit(solution)/shard_map/all_to_all | solution.py:396
  29.3 1.4 %collective-permute-start.4 = (bf16[64,1152]{1,0:T(8,128)(2,1)S(1)}, bf16[64,1152]{1,0:T(8,128)(2,1)}, u32[]{:S(2)}, u32[]{:S(2)}) collective-permute-start(bf16[64,1152]{1,0:T(8,128)(2,1)S(1)} %pad_maximum_fusion.1), channel_id=1, source_target_pairs={{0,128},{8,136},{16,144},{24,152},{32,160},{40,168},{48,176},{56,1... | collective-permute-start | bytes 442376 | tf_op jit(solution)/shard_map/ppermute | solution.py:27
  32.3 2.6 %image.1 = (bf16[15616,1152]{1,0:T(8,128)(2,1)}, bf16[8,24,1152]{2,1,0:T(8,128)(2,1)}) custom-call(bf16[8,72,1152]{2,1,0:T(8,128)(2,1)S(1)} %all-to-all-done.mine_ref, bf16[8,72,1152]{2,1,0:T(8,128)(2,1)S(1)} %collective-permute-done.3.other_ref, bf16[128,1152]{1,0:T(8,128)(2,1)S(1)} %get-tuple-element.47.a_ref, f32[1,1152]{1,0:T(1,128)S(1)} %reshape.22.gain_ref, ...), custom_call_target="tpu_custom_call" | custom-call | flops 400000000 | bytes 6000000 | tf_op jit(solution)/shard_map/image/pallas_call | solution.py:433
  34.9 5.4 %all-to-all-start.1 = ((bf16[8,24,1152]{2,1,0:T(8,128)(2,1)}), bf16[8,24,1152]{2,1,0:T(8,128)(2,1)S(1)}, u32[]{:S(2)}, u32[]{:S(2)}) async-start(bf16[8,24,1152]{2,1,0:T(8,128)(2,1)} %get-tuple-element.48), calls=%async_computation.1 | async-start | bytes 884736 | tf_op jit(solution)/shard_map/all_to_all | solution.py:447
  42.7 8.5 %all-to-all-done.1.got_ref = bf16[8,24,1152]{2,1,0:T(8,128)(2,1)S(1)} async-done(((bf16[8,24,1152]{2,1,0:T(8,128)(2,1)}), bf16[8,24,1152]{2,1,0:T(8,128)(2,1)S(1)}, u32[]{:S(2)}, u32[]{:S(2)}) %all-to-all-start.1) | async-done | bytes 442400 | tf_op jit(solution)/shard_map/all_to_all | solution.py:447
  51.3 1.4 %pair.1 = (bf16[8,8,1152]{2,1,0:T(8,128)(2,1)}, f32[8,128]{1,0:T(8,128)S(1)}, f32[64,1152]{1,0:T(8,128)S(1)}, bf16[64,1152]{1,0:T(8,128)(2,1)S(1)}, bf16[64,1152...) custom-call(f32[2,128]{1,0:T(2,128)S(1)} %broadcast_in_dim.20.scalars, bf16[8,24,1152]{2,1,0:T(8,128)(2,1)S(1)} %all-to-all-done.1.got_ref, ...), custom_call_target="tpu_custom_call" | custom-call | flops 80000000 | bytes 2000000 | tf_op jit(solution)/shard_map/pair/pallas_call | solution.py:451
  53.4 3.4 %all-to-all-start.2 = ((bf16[8,8,1152]{2,1,0:T(8,128)(2,1)}), bf16[8,8,1152]{2,1,0:T(8,128)(2,1)S(1)}, u32[]{:S(2)}, u32[]{:S(2)}) async-start(bf16[8,8,1152]{2,1,0:T(8,128)(2,1)} %get-tuple-element.54), calls=%async_computation.2 | async-start | bytes 294912 | tf_op jit(solution)/shard_map/all_to_all | solution.py:464
  56.8 1.5 %collective-permute-start.7 = (bf16[64,1152]{1,0:T(8,128)(2,1)}, bf16[64,1152]{1,0:T(8,128)(2,1)S(1)}, u32[]{:S(2)}, u32[]{:S(2)}) collective-permute-start(bf16[64,1152]{1,0:T(8,128)(2,1)} %copy-done.5), channel_id=1, source_target_pairs={{0,128},{8,136},{16,144},{24,152},{32,160},{40,168},{48,176},{56,1... | collective-permute-start | bytes 442376 | tf_op jit(solution)/shard_map/ppermute | solution.py:27
  59.0 6.3 %all-to-all-done.2.got_ref = bf16[8,8,1152]{2,1,0:T(8,128)(2,1)S(1)} async-done(((bf16[8,8,1152]{2,1,0:T(8,128)(2,1)}), bf16[8,8,1152]{2,1,0:T(8,128)(2,1)S(1)}, u32[]{:S(2)}, u32[]{:S(2)}) %all-to-all-start.2) | async-done | bytes 147488 | tf_op jit(solution)/shard_map/all_to_all | solution.py:464
  65.3 5.1 %back.1 = bf16[8,64,1152]{2,1,0:T(8,128)(2,1)} custom-call(s32[8]{0:T(128)S(1)} %bitcast.25, bf16[8,8,1152]{2,1,0:T(8,128)(2,1)S(1)} %all-to-all-done.2.got_ref, bf16[15616,1152]{1,0:T(8,128)(2,1)} %get-tuple-element.55.full_in, bf16[1,8,48,1152]{3,2,1,0:T(8,128)(2,1)S(1)} %copy-done.1, f32[384,256]{1,0:T(8,128)S(1)} %get-tuple-element.56.side_in, ...), custom_call_target="tpu_custom_call" | custom-call | flops 500000000 | bytes 8000000 | tf_op jit(solution)/shard_map/back/pallas_call | solution.py:483
  70.6 3.6 %all-to-all-start.3 = ((bf16[8,64,1152]{2,1,0:T(8,128)(2,1)}), bf16[8,64,1152]{2,1,0:T(8,128)(2,1)S(1)}, u32[]{:S(2)}, u32[]{:S(2)}) async-start(bf16[8,64,1152]{2,1,0:T(8,128)(2,1)} %back.1), calls=%async_computation.3 | async-start | bytes 2359296 | tf_op jit(solution)/shard_map/all_to_all | solution.py:505
  74.1 1.3 %collective-permute-start.10 = (bf16[32,1152]{1,0:T(8,128)(2,1)S(1)}, bf16[32,1152]{1,0:T(8,128)(2,1)S(1)}, u32[]{:S(2)}, u32[]{:S(2)}) collective-permute-start(bf16[32,1152]{1,0:T(8,128)(2,1)S(1)} %get-tuple-element.67), channel_id=1, source_target_pairs={{0,16},{8,24},{16,0},{24,8},{32,48},{40,56},{48,32},{56,40},{64,80... | collective-permute-start | bytes 221192 | tf_op jit(solution)/shard_map/ppermute | solution.py:27
  76.2 2.6 %collective-permute-done.10.got_ref = bf16[32,1152]{1,0:T(8,128)(2,1)S(1)} collective-permute-done((bf16[32,1152]{1,0:T(8,128)(2,1)S(1)}, bf16[32,1152]{1,0:T(8,128)(2,1)S(1)}, u32[]{:S(2)}, u32[]{:S(2)}) %collective-permute-start.10) | collective-permute-done | bytes 73760 | tf_op jit(solution)/shard_map/ppermute | solution.py:27
  78.8 6.0 %collective-permute-start.11 = (bf16[8,1152]{1,0:T(8,128)(2,1)S(1)}, bf16[8,1152]{1,0:T(8,128)(2,1)S(1)}, u32[]{:S(2)}, u32[]{:S(2)}) collective-permute-start(bf16[8,1152]{1,0:T(8,128)(2,1)S(1)} %get-tuple-element.68), channel_id=1, source_target_pairs={{0,64},{8,72},{16,80},{24,88},{32,96},{40,104},{48,112},{56,120},{... | collective-permute-start | bytes 55304 | tf_op jit(solution)/shard_map/ppermute | solution.py:27
  84.8 1.8 %collective-permute-start.12 = (bf16[8,1152]{1,0:T(8,128)(2,1)S(1)}, bf16[8,1152]{1,0:T(8,128)(2,1)S(1)}, u32[]{:S(2)}, u32[]{:S(2)}) collective-permute-start(bf16[8,1152]{1,0:T(8,128)(2,1)S(1)} %get-tuple-element.69), channel_id=1, source_target_pairs={{0,32},{8,40},{16,48},{24,56},{32,0},{40,8},{48,16},{56,24},{64,96... | collective-permute-start | bytes 55304 | tf_op jit(solution)/shard_map/ppermute | solution.py:27
  86.6 4.6 %all-to-all-done.3.refs_0_ = bf16[8,64,1152]{2,1,0:T(8,128)(2,1)S(1)} async-done(((bf16[8,64,1152]{2,1,0:T(8,128)(2,1)}), bf16[8,64,1152]{2,1,0:T(8,128)(2,1)S(1)}, u32[]{:S(2)}, u32[]{:S(2)}) %all-to-all-start.3) | async-done | bytes 1179680 | tf_op jit(solution)/shard_map/all_to_all | solution.py:505
  91.2 1.7 %last.1 = (bf16[1,8,48,1152]{3,2,1,0:T(8,128)(2,1)}, bf16[1,144,1152]{2,1,0:T(8,128)(2,1)}, bf16[16,144]{1,0:T(8,128)(2,1)}, bf16[1,144]{1,0:T(2,128)(2,1)}, f32[1,1]{1,0:T(1,128)}) custom-call(bf16[8,64,1152]{2,1,0:T(8,128)(2,1)S(1)} %all-to-all-done.3.refs_0_, bf16[16,64,144]{2,1,0:T(8,128)(2,1)S(1)} %bitcast.21), custom_call_target="tpu_custom_call" | custom-call | flops 400000000 | bytes 3000000 | tf_op jit(solution)/shard_map/last/pallas_call | solution.py:530
  (49 shorter events, 9.1 us)
Async XLA Ops:
  2.8 6.2 %copy-start.6 = (bf16[1,8,1152]{2,1,0:T(8,128)(2,1)S(1)}, bf16[1,8,1152]{2,1,0:T(8,128)(2,1)}, u32[]{:S(2)}) copy-start(bf16[1,8,1152]{2,1,0:T(8,128)(2,1)} %param.12) | copy-start | bytes 55300
  2.8 21.2 %copy-start.7 = (f32[1152]{0:T(1024)S(1)}, f32[1152]{0:T(1024)}, u32[]{:S(2)}) copy-start(f32[1152]{0:T(1024)} %param.13) | copy-start | bytes 13828
  2.8 21.2 %copy-start.1 = (bf16[1,8,48,1152]{3,2,1,0:T(8,128)(2,1)S(1)}, bf16[1,8,48,1152]{3,2,1,0:T(8,128)(2,1)}, u32[]{:S(2)}) copy-start(bf16[1,8,48,1152]{3,2,1,0:T(8,128)(2,1)} %x_in.1) | copy-start | bytes 2654212
  2.8 21.2 %copy-start.2 = (bf16[1152,16]{0,1:T(8,128)(2,1)S(1)}, bf16[1152,16]{0,1:T(8,128)(2,1)}, u32[]{:S(2)}) copy-start(bf16[1152,16]{0,1:T(8,128)(2,1)} %param.14) | copy-start | bytes 110596
  2.8 21.2 %copy-start.3 = (s32[1,8]{1,0:T(1,128)S(1)}, s32[1,8]{1,0:T(1,128)}, u32[]{:S(2)}) copy-start(s32[1,8]{1,0:T(1,128)} %param.11) | copy-start | bytes 100
  2.8 21.2 %copy-start.4 = (s32[1,8]{1,0:T(1,128)S(1)}, s32[1,8]{1,0:T(1,128)}, u32[]{:S(2)}) copy-start(s32[1,8]{1,0:T(1,128)} %param.10) | copy-start | bytes 100
  2.8 26.4 %all-to-all-start = ((bf16[8,72,1152]{2,1,0:T(8,128)(2,1)}), bf16[8,72,1152]{2,1,0:T(8,128)(2,1)S(1)}, u32[]{:S(2)}, u32[]{:S(2)}) async-start(bf16[8,72,1152]{2,1,0:T(8,128)(2,1)} %broadcast_in_dim.21), calls=%async_computation | async-start | bytes 2654208 | tf_op jit(solution)/shard_map/all_to_all | solution.py:396
  9.1 8.9 %collective-permute-start = (bf16[8,1152]{1,0:T(8,128)(2,1)S(1)}, bf16[8,1152]{1,0:T(8,128)(2,1)S(1)}, u32[]{:S(2)}, u32[]{:S(2)}) collective-permute-start(bf16[8,1152]{1,0:T(8,128)(2,1)S(1)} %get-tuple-element.44), channel_id=1, source_target_pairs={{0,64},{8,72},{16,80},{24,88},{32,96},{40,104},{48,112},{56,120},{... | collective-permute-start | bytes 55304 | tf_op jit(solution)/shard_map/ppermute | solution.py:27
  18.1 4.9 %collective-permute-start.1 = (bf16[16,1152]{1,0:T(8,128)(2,1)S(1)}, bf16[16,1152]{1,0:T(8,128)(2,1)S(1)}, u32[]{:S(2)}, u32[]{:S(2)}) collective-permute-start(bf16[16,1152]{1,0:T(8,128)(2,1)S(1)} %pad_maximum_fusion.3), channel_id=1, source_target_pairs={{0,32},{8,40},{16,48},{24,56},{32,0},{40,8},{48,16},{56,24},{64,96... | collective-permute-start | bytes 110600 | tf_op jit(solution)/shard_map/ppermute | solution.py:27
  22.9 4.4 %collective-permute-start.2 = (bf16[32,1152]{1,0:T(8,128)(2,1)S(1)}, bf16[32,1152]{1,0:T(8,128)(2,1)S(1)}, u32[]{:S(2)}, u32[]{:S(2)}) collective-permute-start(bf16[32,1152]{1,0:T(8,128)(2,1)S(1)} %pad_maximum_fusion.2), channel_id=1, source_target_pairs={{0,16},{8,24},{16,0},{24,8},{32,48},{40,56},{48,32},{56,40},{64,80... | collective-permute-start | bytes 221192 | tf_op jit(solution)/shard_map/ppermute | solution.py:27
  29.2 3.1 %collective-permute-start.3 = (bf16[8,72,1152]{2,1,0:T(8,128)(2,1)S(1)}, bf16[8,72,1152]{2,1,0:T(8,128)(2,1)S(1)}, u32[]{:S(2)}, u32[]{:S(2)}) collective-permute-start(bf16[8,72,1152]{2,1,0:T(8,128)(2,1)S(1)} %all-to-all-done.mine_ref), channel_id=1, source_target_pairs={{0,8},{8,0},{16,24},{24,16},{32,40},{40,32},{48,56},{56,48},{64,72... | collective-permute-start | bytes 3981320 | tf_op jit(solution)/shard_map/ppermute | solution.py:27
  29.3 12.4 %collective-permute-start.4 = (bf16[64,1152]{1,0:T(8,128)(2,1)S(1)}, bf16[64,1152]{1,0:T(8,128)(2,1)}, u32[]{:S(2)}, u32[]{:S(2)}) collective-permute-start(bf16[64,1152]{1,0:T(8,128)(2,1)S(1)} %pad_maximum_fusion.1), channel_id=1, source_target_pairs={{0,128},{8,136},{16,144},{24,152},{32,160},{40,168},{48,176},{56,1... | collective-permute-start | bytes 442376 | tf_op jit(solution)/shard_map/ppermute | solution.py:27
  30.7 10.9 %collective-permute-start.5 = (bf16[64,1152]{1,0:T(8,128)(2,1)S(1)}, bf16[64,1152]{1,0:T(8,128)(2,1)}, u32[]{:S(2)}, u32[]{:S(2)}) collective-permute-start(bf16[64,1152]{1,0:T(8,128)(2,1)S(1)} %pad_maximum_fusion.1), channel_id=1, source_target_pairs={{0,8},{8,0},{16,24},{24,16},{32,40},{40,32},{48,56},{56,48},{64,72... | collective-permute-start | bytes 442376 | tf_op jit(solution)/shard_map/ppermute | solution.py:27
  30.9 10.7 %collective-permute-start.6 = (bf16[64,1152]{1,0:T(8,128)(2,1)S(1)}, bf16[64,1152]{1,0:T(8,128)(2,1)}, u32[]{:S(2)}, u32[]{:S(2)}) collective-permute-start(bf16[64,1152]{1,0:T(8,128)(2,1)S(1)} %pad_maximum_fusion.1), channel_id=1, source_target_pairs={{0,136},{8,128},{16,152},{24,144},{32,168},{40,160},{48,184},{56,1... | collective-permute-start | bytes 442376 | tf_op jit(solution)/shard_map/ppermute | solution.py:27
  34.9 16.4 %all-to-all-start.1 = ((bf16[8,24,1152]{2,1,0:T(8,128)(2,1)}), bf16[8,24,1152]{2,1,0:T(8,128)(2,1)S(1)}, u32[]{:S(2)}, u32[]{:S(2)}) async-start(bf16[8,24,1152]{2,1,0:T(8,128)(2,1)} %get-tuple-element.48), calls=%async_computation.1 | async-start | bytes 884736 | tf_op jit(solution)/shard_map/all_to_all | solution.py:447
  53.4 12.0 %all-to-all-start.2 = ((bf16[8,8,1152]{2,1,0:T(8,128)(2,1)}), bf16[8,8,1152]{2,1,0:T(8,128)(2,1)S(1)}, u32[]{:S(2)}, u32[]{:S(2)}) async-start(bf16[8,8,1152]{2,1,0:T(8,128)(2,1)} %get-tuple-element.54), calls=%async_computation.2 | async-start | bytes 294912 | tf_op jit(solution)/shard_map/all_to_all | solution.py:464
  56.8 13.7 %collective-permute-start.7 = (bf16[64,1152]{1,0:T(8,128)(2,1)}, bf16[64,1152]{1,0:T(8,128)(2,1)S(1)}, u32[]{:S(2)}, u32[]{:S(2)}) collective-permute-start(bf16[64,1152]{1,0:T(8,128)(2,1)} %copy-done.5), channel_id=1, source_target_pairs={{0,128},{8,136},{16,144},{24,152},{32,160},{40,168},{48,176},{56,1... | collective-permute-start | bytes 442376 | tf_op jit(solution)/shard_map/ppermute | solution.py:27
  58.3 12.2 %collective-permute-start.8 = (bf16[64,1152]{1,0:T(8,128)(2,1)S(1)}, bf16[64,1152]{1,0:T(8,128)(2,1)S(1)}, u32[]{:S(2)}, u32[]{:S(2)}) collective-permute-start(bf16[64,1152]{1,0:T(8,128)(2,1)S(1)} %get-tuple-element.60), channel_id=1, source_target_pairs={{0,8},{8,0},{16,24},{24,16},{32,40},{40,32},{48,56},{56,48},{64,72... | collective-permute-start | bytes 442376 | tf_op jit(solution)/shard_map/ppermute | solution.py:27
  58.3 12.2 %collective-permute-start.9 = (bf16[64,1152]{1,0:T(8,128)(2,1)S(1)}, bf16[64,1152]{1,0:T(8,128)(2,1)S(1)}, u32[]{:S(2)}, u32[]{:S(2)}) collective-permute-start(bf16[64,1152]{1,0:T(8,128)(2,1)S(1)} %get-tuple-element.61), channel_id=1, source_target_pairs={{0,136},{8,128},{16,152},{24,144},{32,168},{40,160},{48,184},{56,1... | collective-permute-start | bytes 442376 | tf_op jit(solution)/shard_map/ppermute | solution.py:27
  70.6 20.7 %all-to-all-start.3 = ((bf16[8,64,1152]{2,1,0:T(8,128)(2,1)}), bf16[8,64,1152]{2,1,0:T(8,128)(2,1)S(1)}, u32[]{:S(2)}, u32[]{:S(2)}) async-start(bf16[8,64,1152]{2,1,0:T(8,128)(2,1)} %back.1), calls=%async_computation.3 | async-start | bytes 2359296 | tf_op jit(solution)/shard_map/all_to_all | solution.py:505
  74.1 4.6 %collective-permute-start.10 = (bf16[32,1152]{1,0:T(8,128)(2,1)S(1)}, bf16[32,1152]{1,0:T(8,128)(2,1)S(1)}, u32[]{:S(2)}, u32[]{:S(2)}) collective-permute-start(bf16[32,1152]{1,0:T(8,128)(2,1)S(1)} %get-tuple-element.67), channel_id=1, source_target_pairs={{0,16},{8,24},{16,0},{24,8},{32,48},{40,56},{48,32},{56,40},{64,80... | collective-permute-start | bytes 221192 | tf_op jit(solution)/shard_map/ppermute | solution.py:27
  78.8 14.1 %collective-permute-start.11 = (bf16[8,1152]{1,0:T(8,128)(2,1)S(1)}, bf16[8,1152]{1,0:T(8,128)(2,1)S(1)}, u32[]{:S(2)}, u32[]{:S(2)}) collective-permute-start(bf16[8,1152]{1,0:T(8,128)(2,1)S(1)} %get-tuple-element.68), channel_id=1, source_target_pairs={{0,64},{8,72},{16,80},{24,88},{32,96},{40,104},{48,112},{56,120},{... | collective-permute-start | bytes 55304 | tf_op jit(solution)/shard_map/ppermute | solution.py:27
  84.8 8.1 %collective-permute-start.12 = (bf16[8,1152]{1,0:T(8,128)(2,1)S(1)}, bf16[8,1152]{1,0:T(8,128)(2,1)S(1)}, u32[]{:S(2)}, u32[]{:S(2)}) collective-permute-start(bf16[8,1152]{1,0:T(8,128)(2,1)S(1)} %get-tuple-element.69), channel_id=1, source_target_pairs={{0,32},{8,40},{16,48},{24,56},{32,0},{40,8},{48,16},{56,24},{64,96... | collective-permute-start | bytes 55304 | tf_op jit(solution)/shard_map/ppermute | solution.py:27
  86.6 6.3 %collective-permute-start.13 = (bf16[8,1152]{1,0:T(8,128)(2,1)S(1)}, bf16[8,1152]{1,0:T(8,128)(2,1)S(1)}, u32[]{:S(2)}, u32[]{:S(2)}) collective-permute-start(bf16[8,1152]{1,0:T(8,128)(2,1)S(1)} %get-tuple-element.70), channel_id=1, source_target_pairs={{0,96},{8,104},{16,112},{24,120},{32,64},{40,72},{48,80},{56,88},{... | collective-permute-start | bytes 55304 | tf_op jit(solution)/shard_map/ppermute | solution.py:27
  (2 other events, 1.6 us)
